TPU v7x, 128 devices: a whole 4x4x4 slice. The times are simulated.
128 devices in a mesh: view: 4 (over y_hi, core), row: 32 (over x, z, y_lo).
Axes of the slice: x: 4, y: 4 (y_hi: 2, y_lo: 2; y = y_hi * 2 + y_lo), z: 4, core: 2. Of those that a mesh axis runs over, the one named last changes fastest.
Arguments:
- tokens: bfloat16 [32, 4, 128, 1024], P('row', 'view'), may hold values from -6 to 6
- patches: bfloat16 [32, 4, 256, 768], P('row', 'view'), may hold values from -6 to 6
- patch_counts: int32 [8, 4], replicated, may hold values from 256 to 1024, as said below
- camera_ids: int32 [8], replicated, may hold values from 0 to 15
- modulation: float32 [16, 6144], replicated, may hold values from -1.5 to 1.5
- query_weight: bfloat16 [1024, 1024], replicated, may hold values from -0.1875 to 0.1875
- key_weight: bfloat16 [1024, 1024], replicated, may hold values from -0.1875 to 0.1875
- value_weight: bfloat16 [1024, 1024], replicated, may hold values from -0.1875 to 0.1875
- output_weight: bfloat16 [1024, 1024], replicated, may hold values from -0.75 to 0.75
- cross_query: bfloat16 [1024, 1024], replicated, may hold values from -0.1875 to 0.1875
- cross_key: bfloat16 [768, 1024], replicated, may hold values from -0.21875 to 0.21875
- cross_value: bfloat16 [768, 1024], replicated, may hold values from -0.21875 to 0.21875
- cross_output: bfloat16 [1024, 1024], replicated, may hold values from -0.5 to 0.5
- expand_weight: bfloat16 [1024, 4096], replicated, may hold values from -0.1875 to 0.1875
- reduce_weight: bfloat16 [4096, 1024], replicated, may hold values from -0.09375 to 0.09375
- cotangent: bfloat16 [32, 4, 128, 1024], P('row', 'view'), may hold values from -6 to 6
Outputs:
- layer_out: float32 [32, 4, 128, 1024], P('row', 'view')
- tokens_grad: float32 [32, 4, 128, 1024], P('row', 'view')
- patches_grad: float32 [32, 4, 256, 768], P('row', 'view')
- modulation_grad: float32 [16, 6144], P('view', 'row')
- query_grad: float32 [1024, 1024], P('view', 'row')
- key_grad: float32 [1024, 1024], P('view', 'row')
- value_grad: float32 [1024, 1024], P('view', 'row')
- output_grad: float32 [1024, 1024], P('view', 'row')
- cross_query_grad: float32 [1024, 1024], P('view', 'row')
- cross_key_grad: float32 [768, 1024], P('view', 'row')
- cross_value_grad: float32 [768, 1024], P('view', 'row')
- cross_output_grad: float32 [1024, 1024], P('view', 'row')
- expand_grad: float32 [1024, 4096], P('view', 'row')
- reduce_grad: float32 [4096, 1024], P('view', 'row')
Inputs may be any that keep to these rules, and one draw needn't show every extreme that they name: `patch_counts`: each entry is 256 or 1024; every item has a view of each kind.
All inputs are finite; a program needn't handle non-finite values.
Results may differ from a plain program's by a relative error of at most 0.02.
Values may be sent and summed in bfloat16 or wider, within the bound.
No kernel may reach another device: no remote copies, remote signals or barrier semaphores. Data moves between devices by JAX's collectives and lax.ppermute only.
A program may use at most 320 MiB of HBM per device.

v0:
```python
from functools import partial

import jax
import jax.numpy as jnp
from jax import lax
from jax.sharding import PartitionSpec as P

HEADS = 16
GROUP = 4


epsilon = 1e-05
block_heads = 4
hugely_negative = -1e30


def shortened(shard):
    return jax.tree.map(lambda a: a.astype(jnp.bfloat16) if a.dtype == jnp.float32 else a, shard)


def partner_2(block, axis, stride):
    count = lax.axis_size(axis)
    route = []
    for low in range(count):
        high = low | 1 << stride
        if high != low and high < count:
            route += [(low, high), (high, low)]
    return lax.ppermute(block, axis, route)


def joined(value, axis, join):
    pieces = jax.tree.map(lambda part: lax.all_gather(part, axis), value)
    head = jax.tree.map(lambda part: part[0], pieces)
    tail = jax.tree.map(lambda part: part[1:], pieces)
    so_far, _ = lax.scan(lambda so_far, slab: (join(so_far, slab), None), head, tail)
    return so_far


def modulated(values_in, gain, shift):
    centred = values_in - jnp.mean(values_in, -1, keepdims=True)
    spread = jnp.mean(centred * centred, -1, keepdims=True)
    return centred * lax.rsqrt(spread + epsilon) * (1.0 + gain) + shift


def product(left, right):
    return jnp.dot(left, right, preferred_element_type=jnp.float32)


def over_rows(left, right):
    return lax.dot_general(
        left, right, (((0,), (0,)), ((), ())), preferred_element_type=jnp.float32
    )


def against(left, right):
    return lax.dot_general(
        left, right, (((1,), (1,)), ((), ())), preferred_element_type=jnp.float32
    )


def head_slice(matrix, group_index):
    group_width = matrix.shape[1] // (HEADS // block_heads)
    piece = lax.dynamic_slice_in_dim(matrix, group_index * group_width, group_width, 1)
    return piece.reshape(matrix.shape[0], block_heads, group_width // block_heads)


def join_heads(stacked):
    return jnp.transpose(stacked, (1, 0, 2)).reshape(stacked.shape[1], -1)


def pair_gather(parts):
    row_index = lax.axis_index("row")
    for bit_index in range(GROUP.bit_length() - 1):
        partner = jax.tree.map(
            lambda part, own: part.astype(own.dtype),
            partner_2(shortened(parts), "row", bit_index),
            parts,
        )
        upper_half = row_index >> bit_index & 1 == 1
        parts = tuple(
            (
                jnp.where(
                    upper_half,
                    jnp.concatenate([peer_part, own_part], 0),
                    jnp.concatenate([own_part, peer_part], 0),
                )
                for own_part, peer_part in zip(parts, partner)
            )
        )
    return parts


def halve_cross(parts):
    row_index = lax.axis_index("row")
    for bit_index in reversed(range(GROUP.bit_length() - 1)):
        half_rows = parts[0].shape[0] // 2
        upper_half = row_index >> bit_index & 1 == 1
        kept = tuple(
            (
                jnp.where(upper_half, whole_part[half_rows:], whole_part[:half_rows])
                for whole_part in parts
            )
        )
        given = tuple(
            (
                jnp.where(upper_half, whole_part[:half_rows], whole_part[half_rows:])
                for whole_part in parts
            )
        )
        received = partner_2(given, "row", bit_index)
        parts = tuple((kept_part + got_part for kept_part, got_part in zip(kept, received)))
    return parts


def halve_self(parts):
    row_index = lax.axis_index("row")
    for bit_index in reversed(range(GROUP.bit_length() - 1)):
        half_rows = parts[0].shape[0] // 2
        upper_half = row_index >> bit_index & 1 == 1
        kept = tuple(
            (
                jnp.where(upper_half, whole_part[half_rows:], whole_part[:half_rows])
                for whole_part in parts
            )
        )
        given = tuple(
            (
                jnp.where(upper_half, whole_part[:half_rows], whole_part[half_rows:])
                for whole_part in parts
            )
        )
        received = partner_2(given, "row", bit_index)
        parts = tuple((kept_part + got_part for kept_part, got_part in zip(kept, received)))
    return parts


def self_forward(queries, keys, values, scale):
    rows = queries.shape[0]

    def one_group(group_index):
        query_part = head_slice(queries, group_index)
        key_part = head_slice(keys, group_index)
        value_part = head_slice(values, group_index)
        scores = (
            jnp.einsum("qhd,khd->hqk", query_part, key_part, preferred_element_type=jnp.float32)
            * scale
        )
        peak_value = jnp.max(scores, -1, keepdims=True)
        powered = jnp.exp(scores - peak_value)
        row_total = jnp.sum(powered, -1, keepdims=True)
        probs = (powered / row_total).astype(jnp.bfloat16)
        mixed = jnp.einsum("hqk,khd->qhd", probs, value_part, preferred_element_type=jnp.float32)
        return (mixed.reshape(rows, -1), peak_value[..., 0], row_total[..., 0])

    stacked, peaks, totals = lax.map(one_group, jnp.arange(HEADS // block_heads))
    return (join_heads(stacked), peaks, totals)


def self_backward(queries, keys, values, out_grad, peaks, totals, scale):
    rows = queries.shape[0]
    key_rows = keys.shape[0]

    def one_group(group_args):
        group_index, peak_value, row_total = group_args
        query_part = head_slice(queries, group_index)
        key_part = head_slice(keys, group_index)
        value_part = head_slice(values, group_index)
        grad_part = head_slice(out_grad, group_index)
        scores = (
            jnp.einsum("qhd,khd->hqk", query_part, key_part, preferred_element_type=jnp.float32)
            * scale
        )
        probs = jnp.exp(scores - peak_value[..., None]) / row_total[..., None]
        prob_grad = jnp.einsum(
            "qhd,khd->hqk", grad_part, value_part, preferred_element_type=jnp.float32
        )
        row_dot = jnp.sum(probs * prob_grad, -1, keepdims=True)
        score_grad = (probs * (prob_grad - row_dot) * scale).astype(jnp.bfloat16)
        query_grad = jnp.einsum(
            "hqk,khd->qhd", score_grad, key_part, preferred_element_type=jnp.float32
        )
        key_grad = jnp.einsum(
            "hqk,qhd->khd", score_grad, query_part, preferred_element_type=jnp.float32
        )
        value_grad = jnp.einsum(
            "hqk,qhd->khd",
            probs.astype(jnp.bfloat16),
            grad_part,
            preferred_element_type=jnp.float32,
        )
        return (
            query_grad.reshape(rows, -1),
            key_grad.reshape(key_rows, -1),
            value_grad.reshape(key_rows, -1),
        )

    query_stack, key_stack, value_stack = lax.map(
        one_group, (jnp.arange(HEADS // block_heads), peaks, totals)
    )
    return (join_heads(query_stack), join_heads(key_stack), join_heads(value_stack))


def cross_partial(queries_all, keys, values, valid, scale):
    rows = queries_all.shape[0]

    def one_group(group_index):
        query_part = head_slice(queries_all, group_index)
        key_part = head_slice(keys, group_index)
        value_part = head_slice(values, group_index)
        raw_scores = jnp.einsum(
            "qhd,khd->hqk", query_part, key_part, preferred_element_type=jnp.float32
        )
        scores = jnp.where(valid, raw_scores * scale, hugely_negative)
        peak_value = jnp.max(scores, -1, keepdims=True)
        powered = jnp.exp(scores - peak_value)
        row_total = jnp.sum(powered, -1)
        numer = jnp.einsum(
            "hqk,khd->qhd",
            powered.astype(jnp.bfloat16),
            value_part,
            preferred_element_type=jnp.float32,
        )
        return (peak_value[..., 0], row_total, numer.reshape(rows, -1))

    peaks, totals, numers = lax.map(one_group, jnp.arange(HEADS // block_heads))
    return (peaks.reshape(-1, rows), totals.reshape(-1, rows), join_heads(numers))


def combine_parts(earlier, later):
    peak_first, total_first, numer_first = earlier
    peak_second, total_second, numer_second = later
    peak_joint = jnp.maximum(peak_first, peak_second)
    weight_first = jnp.exp(peak_first - peak_joint)
    weight_second = jnp.exp(peak_second - peak_joint)
    heads_count, rows = peak_first.shape

    def scaled(numer, weight):
        return (numer.reshape(rows, heads_count, -1) * weight.T[:, :, None]).reshape(rows, -1)

    return (
        peak_joint,
        total_first * weight_first + total_second * weight_second,
        scaled(numer_first, weight_first) + scaled(numer_second, weight_second),
    )


def cross_backward(
    queries_all, keys, values, valid, grad_all, merged_out, merged_peak, merged_total, scale
):
    rows = queries_all.shape[0]
    key_rows = keys.shape[0]
    heads_count = merged_peak.shape[0]
    groups = HEADS // block_heads
    delta = jnp.sum(
        (grad_all.astype(jnp.float32) * merged_out).reshape(rows, heads_count, -1), -1
    ).T

    def one_group(group_args):
        group_index, peak_all, total_all, delta_part = group_args
        query_part = head_slice(queries_all, group_index)
        key_part = head_slice(keys, group_index)
        value_part = head_slice(values, group_index)
        grad_part = head_slice(grad_all, group_index)
        raw_scores = jnp.einsum(
            "qhd,khd->hqk", query_part, key_part, preferred_element_type=jnp.float32
        )
        scores = jnp.where(valid, raw_scores * scale, hugely_negative)
        local_peak = jnp.max(scores, -1, keepdims=True)
        powered = jnp.exp(scores - local_peak).astype(jnp.bfloat16)
        probs = jnp.exp(scores - peak_all[..., None]) / total_all[..., None]
        prob_grad = jnp.einsum(
            "qhd,khd->hqk", grad_part, value_part, preferred_element_type=jnp.float32
        )
        score_grad = (probs * (prob_grad - delta_part[..., None]) * scale).astype(jnp.bfloat16)
        query_grad = jnp.einsum(
            "hqk,khd->qhd", score_grad, key_part, preferred_element_type=jnp.float32
        )
        key_grad = jnp.einsum(
            "hqk,qhd->khd", score_grad, query_part, preferred_element_type=jnp.float32
        )
        share = jnp.exp(local_peak[..., 0] - peak_all) / total_all
        scaled_grad = grad_part.astype(jnp.float32) * share.T[:, :, None]
        scaled_upper = scaled_grad.astype(jnp.bfloat16)
        scaled_lower = (scaled_grad - scaled_upper.astype(jnp.float32)).astype(jnp.bfloat16)
        value_grad = jnp.einsum(
            "hqk,qhd->khd", powered, scaled_upper, preferred_element_type=jnp.float32
        ) + jnp.einsum("hqk,qhd->khd", powered, scaled_lower, preferred_element_type=jnp.float32)
        return (
            query_grad.reshape(rows, -1),
            key_grad.reshape(key_rows, -1),
            value_grad.reshape(key_rows, -1),
        )

    query_stack, key_stack, value_stack = lax.map(
        one_group,
        (
            jnp.arange(groups),
            merged_peak.reshape(groups, block_heads, rows),
            merged_total.reshape(groups, block_heads, rows),
            delta.reshape(groups, block_heads, rows),
        ),
    )
    return (join_heads(query_stack), join_heads(key_stack), join_heads(value_stack))


def on_device(
    tokens,
    patches,
    patch_counts,
    camera_ids,
    modulation,
    query_weight,
    key_weight,
    value_weight,
    output_weight,
    cross_query,
    cross_key,
    cross_value,
    cross_output,
    expand_weight,
    reduce_weight,
    cotangent,
):
    width = tokens.shape[3]
    rows = tokens.shape[2]
    scale = (width // HEADS) ** (-0.5)
    view_index = lax.axis_index("view")
    row_index = lax.axis_index("row")
    item_index = row_index // GROUP
    item_match = jnp.arange(patch_counts.shape[0]) == item_index
    view_match = jnp.arange(patch_counts.shape[1]) == view_index
    count_here = jnp.sum(jnp.where(item_match[:, None] & view_match[None, :], patch_counts, 0))
    camera_here = jnp.sum(jnp.where(item_match, camera_ids, 0))
    camera_onehot = (jnp.arange(modulation.shape[0]) == camera_here).astype(jnp.float32)
    gains = jnp.sum(camera_onehot[:, None] * modulation, 0).reshape(6, width)
    inputs = tokens[0, 0].astype(jnp.float32)
    own_patches = patches[0, 0]
    attn_in = modulated(inputs, gains[0], gains[1]).astype(jnp.bfloat16)
    queries = product(attn_in, query_weight).astype(jnp.bfloat16)
    keys = product(attn_in, key_weight).astype(jnp.bfloat16)
    values = product(attn_in, value_weight).astype(jnp.bfloat16)
    row_keys, row_values = (
        lax.all_gather(keys, "view", axis=0, tiled=True),
        lax.all_gather(values, "view", axis=0, tiled=True),
    )
    cross_keys_own = product(own_patches, cross_key).astype(jnp.bfloat16)
    cross_values_own = product(own_patches, cross_value).astype(jnp.bfloat16)
    group_keys, group_values, cross_keys, cross_values = pair_gather(
        (row_keys, row_values, cross_keys_own, cross_values_own)
    )
    self_out, self_peaks, self_totals = self_forward(queries, group_keys, group_values, scale)
    self_mixed = self_out.astype(jnp.bfloat16)
    first_sum = inputs + product(self_mixed, output_weight)
    cross_in = modulated(first_sum, gains[2], gains[3]).astype(jnp.bfloat16)
    cross_queries = product(cross_in, cross_query).astype(jnp.bfloat16)
    queries_all = lax.all_gather(cross_queries, "view", axis=0, tiled=True)
    valid = jnp.arange(cross_keys.shape[0]) < count_here
    partial_peak, partial_total, partial_numer = cross_partial(
        queries_all, cross_keys, cross_values, valid, scale
    )
    merged_peak, merged_total, merged_numer = joined(
        (partial_peak, partial_total, partial_numer), "view", combine_parts
    )
    all_rows = merged_numer.shape[0]
    merged_out = (merged_numer.reshape(all_rows, HEADS, -1) / merged_total.T[:, :, None]).reshape(
        all_rows, width
    )
    cross_mixed = lax.dynamic_slice_in_dim(merged_out, view_index * rows, rows, 0).astype(
        jnp.bfloat16
    )
    second_sum = first_sum + product(cross_mixed, cross_output)
    mlp_in = modulated(second_sum, gains[4], gains[5]).astype(jnp.bfloat16)
    expanded = product(mlp_in, expand_weight)
    hidden = jax.nn.gelu(expanded, approximate=True).astype(jnp.bfloat16)
    layer_out = second_sum + product(hidden, reduce_weight)
    grad_out = cotangent[0, 0]
    hidden_grad = against(grad_out, reduce_weight).astype(jnp.bfloat16)
    gelu_pull = jax.vjp(partial(jax.nn.gelu, approximate=True), expanded)[1]
    expanded_grad = gelu_pull(hidden_grad.astype(jnp.float32))[0].astype(jnp.bfloat16)
    mlp_in_grad = against(expanded_grad, expand_weight)
    third_pull = jax.vjp(modulated, second_sum, gains[4], gains[5])[1]
    second_back, gain_five, shift_five = third_pull(mlp_in_grad)
    second_grad = grad_out.astype(jnp.float32) + second_back
    branch_two = second_grad.astype(jnp.bfloat16)
    mixed_grad = against(branch_two, cross_output).astype(jnp.bfloat16)
    grad_all = lax.all_gather(mixed_grad, "view", axis=0, tiled=True)
    query_part_grad, cross_key_part, cross_value_part = cross_backward(
        queries_all,
        cross_keys,
        cross_values,
        valid,
        grad_all,
        merged_out,
        merged_peak,
        merged_total,
        scale,
    )
    own_query_grad = lax.psum_scatter(
        query_part_grad, "view", scatter_dimension=0, tiled=True
    ).astype(jnp.bfloat16)
    key_rows_grad, value_rows_grad = halve_cross((cross_key_part, cross_value_part))
    patch_key_grad = key_rows_grad.astype(jnp.bfloat16)
    patch_value_grad = value_rows_grad.astype(jnp.bfloat16)
    patches_grad = against(patch_key_grad, cross_key) + against(patch_value_grad, cross_value)
    cross_in_grad = against(own_query_grad, cross_query)
    second_pull = jax.vjp(modulated, first_sum, gains[2], gains[3])[1]
    first_back, gain_three, shift_three = second_pull(cross_in_grad)
    first_grad = second_grad + first_back
    branch_one = first_grad.astype(jnp.bfloat16)
    self_grad = against(branch_one, output_weight).astype(jnp.bfloat16)
    query_self_grad, key_full, value_full = self_backward(
        queries, group_keys, group_values, self_grad, self_peaks, self_totals, scale
    )
    key_rows, value_rows = halve_self((key_full, value_full))
    key_own, value_own = (
        lax.psum_scatter(key_rows, "view", scatter_dimension=0, tiled=True),
        lax.psum_scatter(value_rows, "view", scatter_dimension=0, tiled=True),
    )
    query_round = query_self_grad.astype(jnp.bfloat16)
    key_round = key_own.astype(jnp.bfloat16)
    value_round = value_own.astype(jnp.bfloat16)
    attn_in_grad = (
        against(query_round, query_weight)
        + against(key_round, key_weight)
        + against(value_round, value_weight)
    )
    first_pull = jax.vjp(modulated, inputs, gains[0], gains[1])[1]
    input_back, gain_one, shift_one = first_pull(attn_in_grad)
    tokens_grad = first_grad + input_back
    camera_grad = jnp.concatenate(
        [gain_one, shift_one, gain_three, shift_three, gain_five, shift_five]
    )
    modulation_term = camera_onehot[:, None] * camera_grad[None, :]
    partly = (
        lax.psum_scatter(modulation_term, "view", scatter_dimension=0, tiled=True),
        lax.psum_scatter(over_rows(attn_in, query_round), "view", scatter_dimension=0, tiled=True),
        lax.psum_scatter(over_rows(attn_in, key_round), "view", scatter_dimension=0, tiled=True),
        lax.psum_scatter(over_rows(attn_in, value_round), "view", scatter_dimension=0, tiled=True),
        lax.psum_scatter(
            over_rows(self_mixed, branch_one), "view", scatter_dimension=0, tiled=True
        ),
        lax.psum_scatter(
            over_rows(cross_in, own_query_grad), "view", scatter_dimension=0, tiled=True
        ),
        lax.psum_scatter(
            over_rows(own_patches, patch_key_grad), "view", scatter_dimension=0, tiled=True
        ),
        lax.psum_scatter(
            over_rows(own_patches, patch_value_grad), "view", scatter_dimension=0, tiled=True
        ),
        lax.psum_scatter(
            over_rows(cross_mixed, branch_two), "view", scatter_dimension=0, tiled=True
        ),
        lax.psum_scatter(over_rows(mlp_in, expanded_grad), "view", scatter_dimension=0, tiled=True),
        lax.psum_scatter(over_rows(hidden, grad_out), "view", scatter_dimension=0, tiled=True),
    )
    summed = (
        lax.psum_scatter(partly[0], "row", scatter_dimension=1, tiled=True),
        lax.psum_scatter(partly[1], "row", scatter_dimension=1, tiled=True),
        lax.psum_scatter(partly[2], "row", scatter_dimension=1, tiled=True),
        lax.psum_scatter(partly[3], "row", scatter_dimension=1, tiled=True),
        lax.psum_scatter(partly[4], "row", scatter_dimension=1, tiled=True),
        lax.psum_scatter(partly[5], "row", scatter_dimension=1, tiled=True),
        lax.psum_scatter(partly[6], "row", scatter_dimension=1, tiled=True),
        lax.psum_scatter(partly[7], "row", scatter_dimension=1, tiled=True),
        lax.psum_scatter(partly[8], "row", scatter_dimension=1, tiled=True),
        lax.psum_scatter(partly[9], "row", scatter_dimension=1, tiled=True),
        lax.psum_scatter(partly[10], "row", scatter_dimension=1, tiled=True),
    )
    return (
        layer_out[None, None],
        tokens_grad[None, None],
        patches_grad[None, None],
        summed[0],
        summed[1],
        summed[2],
        summed[3],
        summed[4],
        summed[5],
        summed[6],
        summed[7],
        summed[8],
        summed[9],
        summed[10],
    )


def solution(mesh):
    in_specs = (
        P("row", "view", None, None),
        P("row", "view", None, None),
        P(),
        P(),
        P(),
        P(),
        P(),
        P(),
        P(),
        P(),
        P(),
        P(),
        P(),
        P(),
        P(),
        P("row", "view", None, None),
    )
    out_specs = (
        P("row", "view", None, None),
        P("row", "view", None, None),
        P("row", "view", None, None),
        P("view", "row"),
        P("view", "row"),
        P("view", "row"),
        P("view", "row"),
        P("view", "row"),
        P("view", "row"),
        P("view", "row"),
        P("view", "row"),
        P("view", "row"),
        P("view", "row"),
        P("view", "row"),
    )
    return jax.shard_map(
        on_device, mesh=mesh, in_specs=in_specs, out_specs=out_specs, check_vma=False
    )
```

profile of v0, /device:TPU:25, one launch (start us, length us, event | category | flops | bytes accessed | tf_op | source)
XLA Modules:
  0.0 3566.8 jit_solution(17243311798624619473)
XLA Ops:
  19.8 18.9 all-gather.8.cloned.1.call-done
  38.7 28.2 all-gather.6.cloned.1.call-done
  75.2 16.5 collective-permute-done
  103.7 16.6 collective-permute-done.3
  132.2 33.0 collective-permute-done.1
  177.5 29.2 while.72
  220.3 17.2 collective-permute-done.5
  246.2 13.8 collective-permute-done.7
  272.8 44.8 %while.75 = (s32[]{:T(128)}, f32[4,4,512]{2,1,0:T(4,128)S(1)}, f32[4,4,512]{2,1,0:T(4,128)S(1)}, f32[4,512,256]{1,2,0:T(8,128)}, s32[4]{0:T(128)S(1)}, /*index=5...) while((s32[]{:T(128)}, f32[4,4,512]{2,1,0:T(4,128)S(1)}, ...), condition=%wide.region_14.15_spmd.clone, body=%wide.region_11.14_spmd.clone.sunk | while | flops 559936512 | bytes 30740696 | solution.py:225
  320.6 9.7 all_gather.25
  337.5 48.0 %all-gather.12.cloned.1.call-done = f32[4,512,1024]{2,1,0:T(8,128)} async-done(((f32[1,512,1024]{2,1,0:T(8,128)}), f32[4,512,1024]{2,1,0:T(8,128)}) %all-gather.12.cloned.1.call-update) | async-done | bytes 8388624 | tf_op jit(solution)/shard_map/all_gather | solution.py:32
  398.1 30.9 while.73
  460.2 20.0 all-gather.14.cloned.1.call-done
  490.3 78.3 %while.76 = (s32[]{:T(128)}, f32[4,512,256]{1,2,0:T(8,128)}, f32[4,1024,256]{1,2,0:T(8,128)}, f32[4,1024,256]{1,2,0:T(8,128)}, s32[4]{0:T(128)S(1)}, /*index=5*/...) while((s32[]{:T(128)}, f32[4,512,256]{1,2,0:T(8,128)}, ...), condition=%wide.region_24.25_spmd.clone, body=%wide.region_22.24_spmd.clone.sunk | while | flops 1651903488 | bytes 62788868 | solution.py:294
  569.2 37.0 %reduce-scatter.45.cloned.1.call-done = f32[128,1024]{0,1:T(8,128)} async-done(((f32[512,1024]{0,1:T(8,128)}), f32[128,1024]{0,1:T(8,128)}) %reduce-scatter.45.cloned.1.call-update) | async-done | bytes 524304 | tf_op jit(solution)/shard_map/reduce_scatter | solution.py:398
  610.4 133.6 %while.74 = (s32[]{:T(128)}, bf16[4,128,256]{1,2,0:T(8,128)(2,1)S(1)}, f32[4,2048,256]{1,2,0:T(8,128)}, f32[4,2048,256]{1,2,0:T(8,128)}, s32[4]{0:T(128)S(1)}, /...) while((s32[]{:T(128)}, ...), condition=%wide.region_30.31_spmd, body=%wide.region_28.30_spmd.sunk | while | flops 685773824 | bytes 60895768 | solution.py:197
  630.2 8.4 fusion.250
  743.9 8.9 slice_select_fusion.2
  764.8 8.8 slice_select_fusion
  779.2 70.7 %collective-permute-done.8 = f32[1024,1024]{1,0:T(8,128)} collective-permute-done((f32[1024,1024]{1,0:T(8,128)}, f32[1024,1024]{1,0:T(8,128)}, u32[]{:S(2)}, u32[]{:S(2)}) %collective-permute-start.8) | collective-permute-done | bytes 4194336 | tf_op jit(solution)/shard_map/ppermute | solution.py:28
  855.0 44.5 %collective-permute-done.9 = f32[512,1024]{1,0:T(8,128)S(1)} collective-permute-done((f32[512,1024]{1,0:T(8,128)S(1)}, f32[512,1024]{1,0:T(8,128)S(1)}, u32[]{:S(2)}, u32[]{:S(2)}) %collective-permute-start.9) | collective-permute-done | bytes 2097184 | tf_op jit(solution)/shard_map/ppermute | solution.py:28
  907.0 32.8 collective-permute-done.10
  944.8 45.6 %collective-permute-done.11 = f32[512,1024]{1,0:T(8,128)S(1)} collective-permute-done((f32[512,1024]{1,0:T(8,128)S(1)}, f32[512,1024]{1,0:T(8,128)S(1)}, u32[]{:S(2)}, u32[]{:S(2)}) %collective-permute-start.11) | collective-permute-done | bytes 2097184 | tf_op jit(solution)/shard_map/ppermute | solution.py:28
  997.7 34.4 reduce-scatter.49.cloned.1.call-done
  1045.7 45.2 %collective-permute-done.14 = f32[512,1024]{0,1:T(8,128)S(1)} collective-permute-done((f32[512,1024]{0,1:T(8,128)S(1)}, f32[512,1024]{0,1:T(8,128)S(1)}, u32[]{:S(2)}, u32[]{:S(2)}) %collective-permute-start.14) | collective-permute-done | bytes 2097184 | tf_op jit(solution)/shard_map/ppermute | solution.py:28
  1091.7 30.3 collective-permute-done.15
  1133.3 39.4 %collective-permute-done.12 = f32[512,1024]{0,1:T(8,128)S(1)} collective-permute-done((f32[512,1024]{0,1:T(8,128)S(1)}, f32[512,1024]{0,1:T(8,128)S(1)}, u32[]{:S(2)}, u32[]{:S(2)}) %collective-permute-start.12) | collective-permute-done | bytes 2097184 | tf_op jit(solution)/shard_map/ppermute | solution.py:28
  1173.8 33.6 collective-permute-done.13
  1234.7 10.1 fusion.85
  1245.9 9.5 fusion.112
  1268.3 47.1 %reduce-scatter.59.cloned.1.call-done = f32[256,1024]{1,0:T(8,128)} async-done(((f32[1024,1024]{1,0:T(8,128)}), f32[256,1024]{1,0:T(8,128)}) %reduce-scatter.59.cloned.1.call-update) | async-done | bytes 1048592 | tf_op jit(solution)/shard_map/reduce_scatter | solution.py:442
  1318.3 50.5 %reduce-scatter.57.cloned.1.call-done = f32[256,1024]{1,0:T(8,128)} async-done(((f32[1024,1024]{1,0:T(8,128)}), f32[256,1024]{1,0:T(8,128)}) %reduce-scatter.57.cloned.1.call-update) | async-done | bytes 1048592 | tf_op jit(solution)/shard_map/reduce_scatter | solution.py:439
  1371.4 50.9 %reduce-scatter.51.cloned.1.call-done = f32[256,1024]{1,0:T(8,128)} async-done(((f32[1024,1024]{1,0:T(8,128)}), f32[256,1024]{1,0:T(8,128)}) %reduce-scatter.51.cloned.1.call-update) | async-done | bytes 1048592 | tf_op jit(solution)/shard_map/reduce_scatter | solution.py:436
  1424.9 50.8 %reduce-scatter.55.cloned.1.call-done = f32[256,1024]{1,0:T(8,128)} async-done(((f32[1024,1024]{1,0:T(8,128)}), f32[256,1024]{1,0:T(8,128)}) %reduce-scatter.55.cloned.1.call-update) | async-done | bytes 1048592 | tf_op jit(solution)/shard_map/reduce_scatter | solution.py:438
  1478.3 50.9 %reduce-scatter.53.cloned.1.call-done = f32[256,1024]{1,0:T(8,128)} async-done(((f32[1024,1024]{1,0:T(8,128)}), f32[256,1024]{1,0:T(8,128)}) %reduce-scatter.53.cloned.1.call-update) | async-done | bytes 1048592 | tf_op jit(solution)/shard_map/reduce_scatter | solution.py:437
  1531.9 132.3 %reduce-scatter.71.cloned.1.call-done = f32[1024,1024]{1,0:T(8,128)} async-done(((f32[4096,1024]{1,0:T(8,128)}), f32[1024,1024]{1,0:T(8,128)}) %reduce-scatter.71.cloned.1.call-update) | async-done | bytes 4194320 | tf_op jit(solution)/shard_map/reduce_scatter | solution.py:455
  1669.6 129.9 %reduce-scatter.67.cloned.1.call-done = f32[256,4096]{1,0:T(8,128)} async-done(((f32[1024,4096]{1,0:T(8,128)}), f32[256,4096]{1,0:T(8,128)}) %reduce-scatter.67.cloned.1.call-update) | async-done | bytes 4194320 | tf_op jit(solution)/shard_map/reduce_scatter | solution.py:454
  1810.2 131.8 %reduce-scatter.73.cloned.1.call-done = f32[192,4]{1,0:T(8,128)} async-done(((f32[6144,4]{1,0:T(8,128)}), f32[192,4]{1,0:T(8,128)}) %reduce-scatter.73.cloned.1.call-update) | async-done | bytes 3088
  1943.6 156.4 %reduce-scatter.89.cloned.1.call-done = f32[32,256]{1,0:T(8,128)} async-done(((f32[1024,256]{1,0:T(8,128)}), f32[32,256]{1,0:T(8,128)}) %reduce-scatter.89.cloned.1.call-update) | async-done | bytes 32784
  2100.0 160.6 %reduce-scatter.63.cloned.1.call-done = f32[192,32]{0,1:T(8,128)} async-done(((f32[192,1024]{0,1:T(8,128)}), f32[192,32]{0,1:T(8,128)}) %reduce-scatter.63.cloned.1.call-update) | async-done | bytes 24592 | tf_op jit(solution)/shard_map/reduce_scatter | solution.py:465
  2260.6 159.5 %reduce-scatter.61.cloned.1.call-done = f32[192,32]{0,1:T(8,128)} async-done(((f32[192,1024]{0,1:T(8,128)}), f32[192,32]{0,1:T(8,128)}) %reduce-scatter.61.cloned.1.call-update) | async-done | bytes 24592 | tf_op jit(solution)/shard_map/reduce_scatter | solution.py:464
  2420.1 160.8 %reduce-scatter.83.cloned.1.call-done = f32[32,256]{1,0:T(8,128)} async-done(((f32[1024,256]{1,0:T(8,128)}), f32[32,256]{1,0:T(8,128)}) %reduce-scatter.83.cloned.1.call-update) | async-done | bytes 32784
  2580.9 159.9 %reduce-scatter.81.cloned.1.call-done = f32[32,256]{1,0:T(8,128)} async-done(((f32[1024,256]{1,0:T(8,128)}), f32[32,256]{1,0:T(8,128)}) %reduce-scatter.81.cloned.1.call-update) | async-done | bytes 32784
  2740.7 161.0 %reduce-scatter.75.cloned.1.call-done = f32[32,256]{1,0:T(8,128)} async-done(((f32[1024,256]{1,0:T(8,128)}), f32[32,256]{1,0:T(8,128)}) %reduce-scatter.75.cloned.1.call-update) | async-done | bytes 32784
  2901.8 158.6 %reduce-scatter.79.cloned.1.call-done = f32[32,256]{1,0:T(8,128)} async-done(((f32[1024,256]{1,0:T(8,128)}), f32[32,256]{1,0:T(8,128)}) %reduce-scatter.79.cloned.1.call-update) | async-done | bytes 32784
  3060.3 159.7 %reduce-scatter.77.cloned.1.call-done = f32[32,256]{1,0:T(8,128)} async-done(((f32[1024,256]{1,0:T(8,128)}), f32[32,256]{1,0:T(8,128)}) %reduce-scatter.77.cloned.1.call-update) | async-done | bytes 32784
  3220.1 171.0 %reduce-scatter.91.cloned.1.call-done = f32[32,1024]{1,0:T(8,128)} async-done(((f32[1024,1024]{1,0:T(8,128)}), f32[32,1024]{1,0:T(8,128)}) %reduce-scatter.91.cloned.1.call-update) | async-done | bytes 131088
  3391.1 168.6 %reduce-scatter.69.cloned.1.call-done = f32[256,128]{1,0:T(8,128)} async-done(((f32[256,4096]{1,0:T(8,128)}), f32[256,128]{1,0:T(8,128)}) %reduce-scatter.69.cloned.1.call-update) | async-done | bytes 131088 | tf_op jit(solution)/shard_map/reduce_scatter | solution.py:467
  (675 shorter events, 597.2 us)
Async XLA Ops:
  7.2 31.5 all-gather.8.cloned.1.call-start
  16.8 50.0 %all-gather.6.cloned.1.call-start = ((), (), s32[]{:S(2)}) async-start(), calls=%async_computation.24 | async-start | bytes 1310720 | tf_op jit(solution)/shard_map/all_gather | solution.py:344
  19.7 249.1 %all-gather.10.cloned.1.call-start = ((), (), s32[]{:S(2)}) async-start(), calls=%async_computation.26 | async-start | bytes 1310720 | tf_op jit(solution)/shard_map/all_gather | solution.py:356
  38.7 30.4 collective-permute-start.2
  66.9 24.8 collective-permute-start
  73.8 46.4 %collective-permute-start.3 = (bf16[1024,1024]{1,0:T(8,128)(2,1)}, bf16[1024,1024]{1,0:T(8,128)(2,1)}, u32[]{:S(2)}, u32[]{:S(2)}) collective-permute-start(bf16[1024,1024]{1,0:T(8,128)(2,1)} %maximum_select_fusion.3), channel_id=1, source_target_pairs={{0,2},{2,0},{1,3},{3,1},{4,6},{6,4},{5,7},{7,5},{8,10},{10,8},{9,1... | collective-permute-start | bytes 6291464 | tf_op jit(solution)/shard_map/ppermute | solution.py:28
  95.6 69.6 %collective-permute-start.1 = (bf16[1024,1024]{1,0:T(8,128)(2,1)}, bf16[1024,1024]{1,0:T(8,128)(2,1)}, u32[]{:S(2)}, u32[]{:S(2)}) collective-permute-start(bf16[1024,1024]{1,0:T(8,128)(2,1)} %maximum_select_fusion.2), channel_id=1, source_target_pairs={{0,2},{2,0},{1,3},{3,1},{4,6},{6,4},{5,7},{7,5},{8,10},{10,8},{9,1... | collective-permute-start | bytes 6291464 | tf_op jit(solution)/shard_map/ppermute | solution.py:28
  98.2 117.6 %collective-permute-start.6 = (bf16[256,1024]{1,0:T(8,128)(2,1)}, bf16[256,1024]{1,0:T(8,128)(2,1)}, u32[]{:S(2)}, u32[]{:S(2)}) collective-permute-start(bf16[256,1024]{1,0:T(8,128)(2,1)} %convolution_convert_fusion.1), channel_id=1, source_target_pairs={{0,1},{1,0},{2,3},{3,2},{4,5},{5,4},{6,7},{7,6},{8,9},{9,8},{10,11... | collective-permute-start | bytes 1572872 | tf_op jit(solution)/shard_map/ppermute | solution.py:28
  99.9 111.6 %collective-permute-start.4 = (bf16[256,1024]{1,0:T(8,128)(2,1)}, bf16[256,1024]{1,0:T(8,128)(2,1)}, u32[]{:S(2)}, u32[]{:S(2)}) collective-permute-start(bf16[256,1024]{1,0:T(8,128)(2,1)} %convolution_convert_fusion.2), channel_id=1, source_target_pairs={{0,1},{1,0},{2,3},{3,2},{4,5},{5,4},{6,7},{7,6},{8,9},{9,8},{10,11... | collective-permute-start | bytes 1572872 | tf_op jit(solution)/shard_map/ppermute | solution.py:28
  209.5 229.8 %copy-start.2 = (f32[128,1024]{1,0:T(8,128)}, f32[128,1024]{1,0:T(8,128)S(1)}, u32[]{:S(2)}) copy-start(f32[128,1024]{1,0:T(8,128)S(1)} %get-tuple-element.657) | copy-start | bytes 1572868
  211.5 174.0 %all-gather.12.cloned.1.call-start = ((), (), s32[]{:S(2)}) async-start(), calls=%async_computation.27 | async-start | bytes 10485760 | tf_op jit(solution)/shard_map/all_gather | solution.py:32
  214.6 23.0 collective-permute-start.5
  218.9 41.1 %collective-permute-start.7 = (bf16[512,1024]{1,0:T(8,128)(2,1)}, bf16[512,1024]{1,0:T(8,128)(2,1)}, u32[]{:S(2)}, u32[]{:S(2)}) collective-permute-start(bf16[512,1024]{1,0:T(8,128)(2,1)} %maximum_select_fusion.7), channel_id=1, source_target_pairs={{0,2},{2,0},{1,3},{3,1},{4,6},{6,4},{5,7},{7,5},{8,10},{10,8},{9,1... | collective-permute-start | bytes 3145736 | tf_op jit(solution)/shard_map/ppermute | solution.py:28
  320.5 159.6 %all-gather.14.cloned.1.call-start = ((), (), s32[]{:S(2)}) async-start(), calls=%async_computation.28 | async-start | bytes 1310720 | tf_op jit(solution)/shard_map/all_gather | solution.py:386
  459.9 146.3 %reduce-scatter.45.cloned.1.call-start = ((), (), s32[]{:S(2)}) async-start(), calls=%async_computation.29 | async-start | bytes 2621440 | tf_op jit(solution)/shard_map/reduce_scatter | solution.py:398
  568.7 426.3 %reduce-scatter.47.cloned.1.call-start = ((), (), s32[]{:S(2)}) async-start(), calls=%async_computation.30 | async-start | bytes 2621440 | tf_op jit(solution)/shard_map/reduce_scatter | solution.py:416
  743.9 248.5 %copy-start.38 = (bf16[4,128,256]{1,2,0:T(8,128)(2,1)}, bf16[4,128,256]{1,2,0:T(8,128)(2,1)S(1)}, u32[]{:S(2)}) copy-start(bf16[4,128,256]{1,2,0:T(8,128)(2,1)S(1)} %get-tuple-element.284) | copy-start | bytes 786436
  758.2 91.8 %collective-permute-start.8 = (f32[1024,1024]{1,0:T(8,128)}, f32[1024,1024]{1,0:T(8,128)}, u32[]{:S(2)}, u32[]{:S(2)}) collective-permute-start(f32[1024,1024]{1,0:T(8,128)} %copy.120), channel_id=1, source_target_pairs={{0,2},{2,0},{1,3},{3,1},{4,6},{6,4},{5,7},{7,5},{8,10},{10,8},{9,1... | collective-permute-start | bytes 12582920 | tf_op jit(solution)/shard_map/ppermute | solution.py:28
  779.0 160.8 %collective-permute-start.10 = (f32[1024,1024]{1,0:T(8,128)}, f32[1024,1024]{1,0:T(8,128)}, u32[]{:S(2)}, u32[]{:S(2)}) collective-permute-start(f32[1024,1024]{1,0:T(8,128)} %copy.122), channel_id=1, source_target_pairs={{0,2},{2,0},{1,3},{3,1},{4,6},{6,4},{5,7},{7,5},{8,10},{10,8},{9,1... | collective-permute-start | bytes 12582920 | tf_op jit(solution)/shard_map/ppermute | solution.py:28
  854.8 44.8 %collective-permute-start.9 = (f32[512,1024]{1,0:T(8,128)S(1)}, f32[512,1024]{1,0:T(8,128)S(1)}, u32[]{:S(2)}, u32[]{:S(2)}) collective-permute-start(f32[512,1024]{1,0:T(8,128)S(1)} %slice_select_fusion.9), channel_id=1, source_target_pairs={{0,1},{1,0},{2,3},{3,2},{4,5},{5,4},{6,7},{7,6},{8,9},{9,8},{10,11... | collective-permute-start | bytes 6291464 | tf_op jit(solution)/shard_map/ppermute | solution.py:28
  901.6 130.5 %reduce-scatter.49.cloned.1.call-start = ((), (), s32[]{:S(2)}) async-start(), calls=%async_computation.31 | async-start | bytes 2621440 | tf_op jit(solution)/shard_map/reduce_scatter | solution.py:417
  944.7 45.7 %collective-permute-start.11 = (f32[512,1024]{1,0:T(8,128)S(1)}, f32[512,1024]{1,0:T(8,128)S(1)}, u32[]{:S(2)}, u32[]{:S(2)}) collective-permute-start(f32[512,1024]{1,0:T(8,128)S(1)} %slice_select_fusion.8), channel_id=1, source_target_pairs={{0,1},{1,0},{2,3},{3,2},{4,5},{5,4},{6,7},{7,6},{8,9},{9,8},{10,11... | collective-permute-start | bytes 6291464 | tf_op jit(solution)/shard_map/ppermute | solution.py:28
  992.4 264.8 %all-reduce.3.cloned.1.call-start = ((), (), s32[]{:S(2)}) async-start(), calls=%async_computation.53 | async-start | bytes 786432
  1037.5 223.0 %reduce-scatter.65.cloned.1.call-start = ((), (), s32[]{:S(2)}) async-start(), calls=%async_computation.39 | async-start | bytes 5242880 | tf_op jit(solution)/shard_map/reduce_scatter | solution.py:451
  1041.3 221.9 %reduce-scatter.87.cloned.1.call-start = ((), (), s32[]{:S(2)}) async-start(), calls=%async_computation.50 | async-start | bytes 3932160
  1044.4 46.6 %collective-permute-start.14 = (f32[512,1024]{0,1:T(8,128)S(1)}, f32[512,1024]{0,1:T(8,128)S(1)}, u32[]{:S(2)}, u32[]{:S(2)}) collective-permute-start(f32[512,1024]{0,1:T(8,128)S(1)} %bitcast.439), channel_id=1, source_target_pairs={{0,2},{2,0},{1,3},{3,1},{4,6},{6,4},{5,7},{7,5},{8,10},{10,8},{9,1... | collective-permute-start | bytes 6291464 | tf_op jit(solution)/shard_map/ppermute | solution.py:28
  1091.6 30.4 collective-permute-start.15
  1128.8 136.9 %reduce-scatter.85.cloned.1.call-start = ((), (), s32[]{:S(2)}) async-start(), calls=%async_computation.49 | async-start | bytes 3932160
  1132.0 40.8 %collective-permute-start.12 = (f32[512,1024]{0,1:T(8,128)S(1)}, f32[512,1024]{0,1:T(8,128)S(1)}, u32[]{:S(2)}, u32[]{:S(2)}) collective-permute-start(f32[512,1024]{0,1:T(8,128)S(1)} %bitcast.438), channel_id=1, source_target_pairs={{0,2},{2,0},{1,3},{3,1},{4,6},{6,4},{5,7},{7,5},{8,10},{10,8},{9,1... | collective-permute-start | bytes 6291464 | tf_op jit(solution)/shard_map/ppermute | solution.py:28
  1173.4 34.0 collective-permute-start.13
  1214.3 101.1 %reduce-scatter.59.cloned.1.call-start = ((), (), s32[]{:S(2)}) async-start(), calls=%async_computation.36 | async-start | bytes 5242880 | tf_op jit(solution)/shard_map/reduce_scatter | solution.py:442
  1218.3 150.5 %reduce-scatter.57.cloned.1.call-start = ((), (), s32[]{:S(2)}) async-start(), calls=%async_computation.35 | async-start | bytes 5242880 | tf_op jit(solution)/shard_map/reduce_scatter | solution.py:439
  1222.1 200.2 %reduce-scatter.51.cloned.1.call-start = ((), (), s32[]{:S(2)}) async-start(), calls=%async_computation.32 | async-start | bytes 5242880 | tf_op jit(solution)/shard_map/reduce_scatter | solution.py:436
  1225.8 249.9 %reduce-scatter.55.cloned.1.call-start = ((), (), s32[]{:S(2)}) async-start(), calls=%async_computation.34 | async-start | bytes 5242880 | tf_op jit(solution)/shard_map/reduce_scatter | solution.py:438
  1229.8 299.4 %reduce-scatter.53.cloned.1.call-start = ((), (), s32[]{:S(2)}) async-start(), calls=%async_computation.33 | async-start | bytes 5242880 | tf_op jit(solution)/shard_map/reduce_scatter | solution.py:437
  1233.8 430.4 %reduce-scatter.71.cloned.1.call-start = ((), (), s32[]{:S(2)}) async-start(), calls=%async_computation.42 | async-start | bytes 20971520 | tf_op jit(solution)/shard_map/reduce_scatter | solution.py:455
  1244.8 554.7 %reduce-scatter.67.cloned.1.call-start = ((), (), s32[]{:S(2)}) async-start(), calls=%async_computation.40 | async-start | bytes 20971520 | tf_op jit(solution)/shard_map/reduce_scatter | solution.py:454
  1255.3 686.7 %reduce-scatter.73.cloned.1.call-start = ((), (), s32[]{:S(2)}) async-start(), calls=%async_computation.43 | async-start | bytes 3244032
  1260.4 839.6 %reduce-scatter.89.cloned.1.call-start = ((), (), s32[]{:S(2)}) async-start(), calls=%async_computation.51 | async-start | bytes 1081344
  1263.2 997.4 %reduce-scatter.63.cloned.1.call-start = ((), (), s32[]{:S(2)}) async-start(), calls=%async_computation.38 | async-start | bytes 1081344 | tf_op jit(solution)/shard_map/reduce_scatter | solution.py:465
  1265.7 1154.4 %reduce-scatter.61.cloned.1.call-start = ((), (), s32[]{:S(2)}) async-start(), calls=%async_computation.37 | async-start | bytes 1081344 | tf_op jit(solution)/shard_map/reduce_scatter | solution.py:464
  1268.3 1312.6 %reduce-scatter.83.cloned.1.call-start = ((), (), s32[]{:S(2)}) async-start(), calls=%async_computation.48 | async-start | bytes 1081344
  1318.0 1422.8 %reduce-scatter.81.cloned.1.call-start = ((), (), s32[]{:S(2)}) async-start(), calls=%async_computation.47 | async-start | bytes 1081344
  1371.3 1530.4 %reduce-scatter.75.cloned.1.call-start = ((), (), s32[]{:S(2)}) async-start(), calls=%async_computation.44 | async-start | bytes 1081344
  1424.9 1635.5 %reduce-scatter.79.cloned.1.call-start = ((), (), s32[]{:S(2)}) async-start(), calls=%async_computation.46 | async-start | bytes 1081344
  1478.2 1741.8 %reduce-scatter.77.cloned.1.call-start = ((), (), s32[]{:S(2)}) async-start(), calls=%async_computation.45 | async-start | bytes 1081344
  1531.8 1859.3 %reduce-scatter.91.cloned.1.call-start = ((), (), s32[]{:S(2)}) async-start(), calls=%async_computation.52 | async-start | bytes 4325376
  1669.6 1890.1 %reduce-scatter.69.cloned.1.call-start = ((), (), s32[]{:S(2)}) async-start(), calls=%async_computation.41 | async-start | bytes 4325376 | tf_op jit(solution)/shard_map/reduce_scatter | solution.py:467
  (108 other events, 2323.1 us)
Sparse Core Ops, SparseCore 0:
  17.0 21.6 all-gather.7
  40.9 25.9 all-gather.5
  211.6 21.9 all-gather.9
  320.7 64.7 all-gather.11
  460.0 20.1 all-gather.13
  568.8 37.3 reduce-scatter.44
  901.7 40.5 reduce-scatter.46
  992.5 39.5 reduce-scatter.48
  1037.6 41.2 all-reduce.2
  1081.4 60.8 reduce-scatter.64
  1145.1 50.4 reduce-scatter.86
  1214.4 47.2 reduce-scatter.84
  1264.5 50.8 reduce-scatter.58
  1317.9 50.8 reduce-scatter.56
  1371.4 50.8 reduce-scatter.50
  1424.8 50.8 reduce-scatter.54
  1478.4 50.8 reduce-scatter.52
  1531.8 132.4 reduce-scatter.70
  1667.1 132.4 reduce-scatter.66
  1801.8 140.2 reduce-scatter.72
  1945.1 154.8 reduce-scatter.88
  2102.9 157.5 reduce-scatter.62
  2263.6 156.3 reduce-scatter.60
  2422.8 157.9 reduce-scatter.82
  2583.9 156.8 reduce-scatter.80
  2743.5 158.1 reduce-scatter.74
  2904.7 155.6 reduce-scatter.78
  3063.3 156.7 reduce-scatter.76
  3223.2 167.8 reduce-scatter.90
  3394.0 165.5 reduce-scatter.68
where the time goes:
time: 3600 us; the launch traced here: 3570 us
  waiting for transfers between devices  2890 us (80%)
  matrix products  257 us (7%)
  local copies, waits for them, and re-layouts  239 us (7%)
  other arithmetic  123 us (3%)
    unnamed x41, waiting for transfers between devices  1260 us
    ppermute x16, waiting for transfers between devices, partner_2(): return lax.ppermute(block, axis, route)  442 us
    reduce_scatter x1, waiting for transfers between devices, on_device(): lax.psum_scatter(partly[9], 'row', scatter_dimension=1, tiled=True)  169 us
    reduce_scatter x1, waiting for transfers between devices, on_device(): lax.psum_scatter(partly[7], 'row', scatter_dimension=1, tiled=True)  161 us
    reduce_scatter x1, waiting for transfers between devices, on_device(): lax.psum_scatter(partly[6], 'row', scatter_dimension=1, tiled=True)  159 us
    reduce_scatter x1, waiting for transfers between devices, on_device(): lax.psum_scatter(over_rows(hidden, grad_out), 'view', scatter_dimension=0...  132 us
    reduce_scatter x1, waiting for transfers between devices, on_device(): lax.psum_scatter(over_rows(mlp_in, expanded_grad), 'view', scatter_dimens...  130 us
  transfers between devices with their start and end apart: 46, of which 38 were waited for; matrix products, arithmetic and copies ran while one was open for 7% of the time, Pallas kernels for 0%

commit v1 on v0

v1 whole, which is shorter than its diff:
```python
from functools import partial
from itertools import product as every

import jax
import jax.numpy as jnp
from jax import lax
from jax.experimental import pallas as pl
from jax.experimental.pallas import tpu as pltpu
from jax.sharding import Mesh
from jax.sharding import PartitionSpec as P

HEADS = 16
HEAD = 64
TOK = 128
SLOTS = 256
BLOCKS = 16
LIVE_MAX = 13
EPS = 1e-05
LOG2E = 1.4426950408889634
FAR = -1e30

AXES = ("yh", "c", "x", "zh", "zl", "yl")
SIZES = (2, 2, 4, 2, 2, 2)
VIEW = ("yh", "c")
ROW = ("x", "zh", "zl", "yl")
ITEM = ("yh", "c", "zl", "yl")
ITEMS = ("x", "zh")
VMEM_BYTES = 56 * 1024 * 1024

bf16 = jnp.bfloat16
f32 = jnp.float32


def mm(left, right, lc=1, rc=0):
    return lax.dot_general(left, right, (((lc,), (rc,)), ((), ())), preferred_element_type=f32)


def swap(block, axes):
    return lax.all_to_all(block, axes, 0, 0, tiled=True)


def three_parts(row):
    high = row.astype(bf16)
    rest = row - high.astype(f32)
    middle = rest.astype(bf16)
    low = (rest - middle.astype(f32)).astype(bf16)
    return high, middle, low


def softmax_block(q, kt, v, o_ref, keep_ref, at, scale):
    s = mm(q, kt)
    m = jnp.max(s, 1, keepdims=True)
    p = jnp.exp2((s - m) * (scale * LOG2E))
    total = jnp.sum(p, 1, keepdims=True)
    o = mm(p.astype(bf16), v)[:, :HEAD] / total
    lse = m + jnp.log2(total) * (1.0 / (scale * LOG2E))
    packed = jnp.concatenate([o, jnp.broadcast_to(lse, o.shape)], 1).T
    for part in range(packed.shape[1] // TOK):
        piece = packed[:, part * TOK : (part + 1) * TOK]
        o_ref[at + part] = piece[:HEAD].astype(bf16)
        keep_ref[at + part] = piece[: HEAD + 8]


def backward_block(qts, dots, keeps, kt, k, vt, dk_acc, dv_acc, scale):
    q_rows, do_rows = [], []
    for qt, dot, keep in zip(qts, dots, keeps):
        lse = keep[HEAD : HEAD + 1]
        delta = jnp.sum(dot.astype(f32) * keep[:HEAD], 0, keepdims=True) * scale
        one = jnp.ones_like(lse)
        zero = jnp.zeros((HEAD - 4, TOK), f32)
        parts = [part.astype(f32) for part in three_parts(-lse)]
        q_rows.append(jnp.concatenate([qt.astype(f32), one] + parts + [zero], 0))
        parts = [part.astype(f32) for part in three_parts(-delta)]
        do_rows.append(jnp.concatenate([dot.astype(f32) * scale] + parts + [0.0 * one, zero], 0))
    q = jnp.concatenate([rows.T for rows in q_rows], 0).astype(bf16)
    do = jnp.concatenate([rows.T for rows in do_rows], 0).astype(bf16)
    p = jnp.exp2(mm(q, kt) * (scale * LOG2E))
    ds = (p * mm(do, vt)).astype(bf16)
    dq = mm(ds, k)
    dk_acc[...] += mm(jnp.concatenate(qts, 1), ds)
    dv_acc[...] += mm(jnp.concatenate(dots, 1), p.astype(bf16))
    return dq[:, :HEAD]


def store_blocks(ref, at, rows, value):
    turned = value.T
    for part in range(turned.shape[1] // TOK):
        ref[at + part, rows, :] = turned[:, part * TOK : (part + 1) * TOK].astype(ref.dtype)


def self_forward_kernel(qkv_ref, o_ref, keep_ref, kt, v, *, scale, step):
    for j in range(BLOCKS):
        cols = slice(j * TOK, (j + 1) * TOK)
        kt[:, cols] = qkv_ref[j, HEAD : 2 * HEAD, :]
        v[cols, :] = qkv_ref[j, 2 * HEAD :, :].T

    def one(i, carry):
        at = i * step
        q = jnp.concatenate([qkv_ref[at + n, :HEAD, :].T for n in range(step)], 0)
        softmax_block(q, kt[...], v[...], o_ref, keep_ref, at, scale)
        return carry

    lax.fori_loop(0, BLOCKS // step, one, 0)


def self_backward_kernel(qkv_ref, do_ref, keep_ref, out_ref, kt, k, vt, dk_acc, dv_acc, *, scale, step):
    ones = jnp.ones((HEAD, BLOCKS * TOK), bf16)
    row = lax.broadcasted_iota(jnp.int32, ones.shape, 0)
    kt[HEAD:, :] = jnp.where((row >= 1) & (row < 4), ones, 0)
    vt[HEAD:, :] = jnp.where(row < 3, ones, 0)
    for j in range(BLOCKS):
        cols = slice(j * TOK, (j + 1) * TOK)
        kt[:HEAD, cols] = qkv_ref[j, HEAD : 2 * HEAD, :]
        k[cols, :] = qkv_ref[j, HEAD : 2 * HEAD, :].T
        vt[:HEAD, cols] = qkv_ref[j, 2 * HEAD :, :]
    dk_acc[...] = jnp.zeros_like(dk_acc)
    dv_acc[...] = jnp.zeros_like(dv_acc)

    def one(i, carry):
        at = i * step
        qts = [qkv_ref[at + n, :HEAD, :] for n in range(step)]
        dots = [do_ref[at + n] for n in range(step)]
        keeps = [keep_ref[at + n] for n in range(step)]
        dq = backward_block(qts, dots, keeps, kt[...], k[...], vt[...], dk_acc, dv_acc, scale)
        store_blocks(out_ref, at, slice(0, HEAD), dq)
        return carry

    lax.fori_loop(0, BLOCKS // step, one, 0)
    for j in range(BLOCKS):
        cols = slice(j * TOK, (j + 1) * TOK)
        out_ref[j, HEAD : 2 * HEAD, :] = dk_acc[:, cols].astype(bf16)
        out_ref[j, 2 * HEAD :, :] = dv_acc[:, cols].astype(bf16)


def slot_block(kv_ref, index):
    return kv_ref[:, pl.ds(pl.multiple_of(index * SLOTS, SLOTS), SLOTS)]


def cross_forward_kernel(order_ref, live_ref, q_ref, kv_ref, o_ref, keep_ref, kt, v, *, scale, step):
    kt[HEAD:, :] = jnp.zeros((HEAD, LIVE_MAX * SLOTS), bf16)
    for t in range(LIVE_MAX):
        cols = slice(t * SLOTS, (t + 1) * SLOTS)
        block = slot_block(kv_ref, order_ref[t])
        kt[:HEAD, cols] = block[:HEAD]
        bias = jnp.where(t < live_ref[0], 0.0, FAR)
        row = lax.broadcasted_iota(jnp.int32, (16, SLOTS), 0)
        kt[HEAD : HEAD + 16, cols] = jnp.where(row == 0, bias, 0.0).astype(bf16)
        v[cols, :] = block[HEAD:].T
    one_row = jnp.where(lax.broadcasted_iota(jnp.int32, (HEAD, TOK), 0) == 0, 1.0, 0.0)

    def one(i, carry):
        at = i * step
        q = jnp.concatenate(
            [jnp.concatenate([q_ref[at + n].astype(f32), one_row], 0).T for n in range(step)], 0
        ).astype(bf16)
        softmax_block(q, kt[...], v[...], o_ref, keep_ref, at, scale)
        return carry

    lax.fori_loop(0, BLOCKS // step, one, 0)


def cross_backward_kernel(
    order_ref, live_ref, q_ref, do_ref, keep_ref, kv_ref, dq_ref, dkv_ref, kt, k, vt, dk_acc, dv_acc, *, scale, step
):
    shape = (HEAD, LIVE_MAX * SLOTS)
    row = lax.broadcasted_iota(jnp.int32, shape, 0)
    kt[HEAD:, :] = jnp.where((row >= 1) & (row < 4), 1.0, 0.0).astype(bf16)
    vt[HEAD:, :] = jnp.where(row < 3, 1.0, 0.0).astype(bf16)
    for t in range(LIVE_MAX):
        cols = slice(t * SLOTS, (t + 1) * SLOTS)
        block = slot_block(kv_ref, order_ref[t])
        kt[:HEAD, cols] = block[:HEAD]
        bias = jnp.where(t < live_ref[0], 0.0, FAR)
        row = lax.broadcasted_iota(jnp.int32, (16, SLOTS), 0)
        ones = jnp.where((row >= 1) & (row < 4), 1.0, 0.0)
        kt[HEAD : HEAD + 16, cols] = jnp.where(row == 0, bias, ones).astype(bf16)
        k[cols, :] = block[:HEAD].T
        vt[:HEAD, cols] = block[HEAD:]
    dk_acc[...] = jnp.zeros_like(dk_acc)
    dv_acc[...] = jnp.zeros_like(dv_acc)

    def one(i, carry):
        at = i * step
        qts = [q_ref[at + n] for n in range(step)]
        dots = [do_ref[at + n] for n in range(step)]
        keeps = [keep_ref[at + n] for n in range(step)]
        dq = backward_block(qts, dots, keeps, kt[...], k[...], vt[...], dk_acc, dv_acc, scale)
        store_blocks(dq_ref, at, slice(0, HEAD), dq)
        return carry

    lax.fori_loop(0, BLOCKS // step, one, 0)
    for t in range(LIVE_MAX):
        cols = slice(t * SLOTS, (t + 1) * SLOTS)
        dkv_ref[order_ref[t], :HEAD, :] = dk_acc[:, cols].astype(bf16)
        dkv_ref[order_ref[t], HEAD:, :] = dv_acc[:, cols].astype(bf16)
    for t in range(LIVE_MAX, BLOCKS):
        dkv_ref[order_ref[t]] = jnp.zeros((2 * HEAD, SLOTS), bf16)


def params():
    return pltpu.CompilerParams(vmem_limit_bytes=VMEM_BYTES)


def vmem(count):
    return [pl.BlockSpec(memory_space=pltpu.VMEM)] * count


def smem(count):
    return [pl.BlockSpec(memory_space=pltpu.SMEM)] * count


def cost(keys, products):
    flops = 2 * BLOCKS * TOK * keys * HEAD * products
    return pl.CostEstimate(flops=4 * flops, bytes_accessed=4 << 20, transcendentals=BLOCKS * TOK * keys)


OUT_T = jax.ShapeDtypeStruct((BLOCKS, HEAD, TOK), bf16)
KEEP_T = jax.ShapeDtypeStruct((BLOCKS, HEAD + 8, TOK), f32)


def self_forward(qkv, scale):
    keys = BLOCKS * TOK
    return pl.pallas_call(
        partial(self_forward_kernel, scale=scale, step=2),
        out_shape=(OUT_T, KEEP_T),
        in_specs=vmem(1),
        out_specs=tuple(vmem(2)),
        scratch_shapes=[pltpu.VMEM((HEAD, keys), bf16), pltpu.VMEM((keys, HEAD), bf16)],
        compiler_params=params(),
        cost_estimate=cost(keys, 2),
        name="self_forward",
    )(qkv)


def self_backward(qkv, do, keep, scale):
    keys = BLOCKS * TOK
    return pl.pallas_call(
        partial(self_backward_kernel, scale=scale, step=2),
        out_shape=jax.ShapeDtypeStruct((BLOCKS, 3 * HEAD, TOK), bf16),
        in_specs=vmem(3),
        out_specs=vmem(1)[0],
        scratch_shapes=[
            pltpu.VMEM((2 * HEAD, keys), bf16),
            pltpu.VMEM((keys, HEAD), bf16),
            pltpu.VMEM((2 * HEAD, keys), bf16),
            pltpu.VMEM((HEAD, keys), f32),
            pltpu.VMEM((HEAD, keys), f32),
        ],
        compiler_params=params(),
        cost_estimate=cost(keys, 5),
        name="self_backward",
    )(qkv, do, keep)


def cross_forward(order, live, q, kv, scale):
    keys = LIVE_MAX * SLOTS
    return pl.pallas_call(
        partial(cross_forward_kernel, scale=scale, step=2),
        out_shape=(OUT_T, KEEP_T),
        in_specs=smem(2) + vmem(2),
        out_specs=tuple(vmem(2)),
        scratch_shapes=[pltpu.VMEM((2 * HEAD, keys), bf16), pltpu.VMEM((keys, HEAD), bf16)],
        compiler_params=params(),
        cost_estimate=cost(keys, 2),
        name="cross_forward",
    )(order, live, q, kv)


def cross_backward(order, live, q, do, keep, kv, scale):
    keys = LIVE_MAX * SLOTS
    return pl.pallas_call(
        partial(cross_backward_kernel, scale=scale, step=2),
        out_shape=(OUT_T, jax.ShapeDtypeStruct((BLOCKS, 2 * HEAD, SLOTS), bf16)),
        in_specs=smem(2) + vmem(4),
        out_specs=tuple(vmem(2)),
        scratch_shapes=[
            pltpu.VMEM((2 * HEAD, keys), bf16),
            pltpu.VMEM((keys, HEAD), bf16),
            pltpu.VMEM((2 * HEAD, keys), bf16),
            pltpu.VMEM((HEAD, keys), f32),
            pltpu.VMEM((HEAD, keys), f32),
        ],
        compiler_params=params(),
        cost_estimate=cost(keys, 5),
        name="cross_backward",
    )(order, live, q, do, keep, kv)


def normed(v):
    centred = v - jnp.mean(v, -1, keepdims=True)
    spread = jnp.mean(centred * centred, -1, keepdims=True)
    r = lax.rsqrt(spread + EPS)
    return centred * r, r


def norm_backward(da, xh, r, gain):
    d = da * (1.0 + gain)
    along = jnp.mean(d * xh, -1, keepdims=True)
    back = r * (d - jnp.mean(d, -1, keepdims=True) - xh * along)
    return back, jnp.sum(da * xh, 0), jnp.sum(da, 0)


def over_item(turned, gathered):
    return lax.dot_general(turned, gathered, (((0, 2), (0, 1)), ((), ())), preferred_element_type=f32)


def column_pieces(grad_t):
    columns, rows = grad_t.shape
    pieces = grad_t.astype(bf16).reshape(2, columns // 2, 4, rows // 4).transpose(0, 2, 1, 3)
    pieces = pieces.reshape(8, columns // 2, rows // 4)
    return jnp.pad(pieces, ((0, 0), (0, 0), (0, 256 - rows // 4)))


def home_route():
    size = dict(zip(AXES, SIZES))
    place = lambda at: sum(at[a] * s for a, s in zip(AXES, (64, 32, 8, 4, 2, 1)))
    route = []
    for spot in every(*[range(size[a]) for a in AXES]):
        at = dict(zip(AXES, spot))
        p = at["x"] * 2 + at["zh"]
        to = dict(x=at["yh"] * 2 + at["c"], zh=at["zl"], zl=at["yl"], yl=p >> 2, yh=p >> 1 & 1, c=p & 1)
        route.append((place(at), place(to)))
    return route


def on_device(
    tokens, patches, patch_counts, camera_ids, modulation, query_weight, key_weight, value_weight, output_weight,
    cross_query, cross_key, cross_value, cross_output, expand_weight, reduce_weight, cotangent,
):
    width = tokens.shape[3]
    scale = HEAD**-0.5
    item = lax.axis_index(ITEMS)
    head = lax.axis_index(ITEM)
    view = lax.axis_index(VIEW)
    camera = lax.dynamic_index_in_dim(camera_ids, item, 0, keepdims=False)
    gains = lax.dynamic_index_in_dim(modulation, camera, 0, keepdims=False).reshape(6, width)
    counts = lax.dynamic_index_in_dim(patch_counts, item, 0, keepdims=False)

    x = tokens[0, 0].astype(f32)
    own_patches = patches[0, 0]
    grad_out = cotangent[0, 0]
    patches_all = lax.all_gather(own_patches, ITEM, axis=0, tiled=False)
    grad_out_all = lax.all_gather(grad_out, ITEM, axis=0, tiled=False)

    live = (jnp.arange(4)[None, :] * SLOTS < counts[:, None]).reshape(BLOCKS)
    n_live = jnp.sum(live.astype(jnp.int32))
    rank = jnp.where(live, jnp.cumsum(live) - 1, n_live + jnp.cumsum(~live) - 1)
    slot = jnp.arange(BLOCKS)
    order = jnp.sum(jnp.where(rank[None, :] == slot[:, None], slot[None, :], 0), 1).astype(jnp.int32)
    n_live = n_live.reshape(1)

    xh1, r1 = normed(x)
    a1 = (xh1 * (1.0 + gains[0]) + gains[1]).astype(bf16)

    def heads_of(weight, rows, rc=1, lc=0):
        return mm(weight, rows, lc, rc).astype(bf16).reshape(HEADS, HEAD, -1)

    qkv = swap(
        jnp.concatenate([heads_of(w, a1) for w in (query_weight, key_weight, value_weight)], 1), ITEM
    )
    o_t, keep_self = self_forward(qkv, scale)
    o1_t = swap(o_t, ITEM).reshape(width, TOK)
    first_sum = x + mm(o1_t, output_weight, 0, 0)
    xh2, r2 = normed(first_sum)
    a2 = (xh2 * (1.0 + gains[2]) + gains[3]).astype(bf16)
    qc = swap(heads_of(cross_query, a2), ITEM)

    own_columns = lambda w: lax.dynamic_slice_in_dim(w, head * HEAD, HEAD, 1)
    kv_weight = jnp.concatenate([own_columns(cross_key), own_columns(cross_value)], 1)
    kv = mm(kv_weight, patches_all.reshape(BLOCKS * SLOTS, -1), 0, 1).astype(bf16)
    oc_t, keep_cross = cross_forward(order, n_live, qc, kv, scale)
    oc1_t = swap(oc_t, ITEM).reshape(width, TOK)
    second_sum = first_sum + mm(oc1_t, cross_output, 0, 0)
    xh3, r3 = normed(second_sum)
    a3 = (xh3 * (1.0 + gains[4]) + gains[5]).astype(bf16)
    u_t = mm(expand_weight, a3, 0, 1)
    h32, gelu_pull = jax.vjp(partial(jax.nn.gelu, approximate=True), u_t)
    h_t = h32.astype(bf16)
    layer_out = second_sum + mm(h_t, reduce_weight, 0, 0)

    dh_t = mm(reduce_weight, grad_out, 1, 1).astype(bf16)
    du_t = gelu_pull(dh_t.astype(f32))[0].astype(bf16)
    da3 = mm(du_t, expand_weight, 0, 1)
    back3, dg3, db3 = norm_backward(da3, xh3, r3, gains[4])
    d_second = grad_out.astype(f32) + back3
    dy2 = d_second.astype(bf16)
    do_t = heads_of(cross_output, dy2, 1, 1)
    hidden = HEADS * HEAD // 4
    sent = jnp.concatenate([do_t, h_t.reshape(HEADS, hidden, TOK), du_t.reshape(HEADS, hidden, TOK)], 1)
    got = swap(sent, ITEM)
    do_c, h_all, du_all = got[:, :HEAD], got[:, HEAD : HEAD + hidden], got[:, HEAD + hidden :]
    acts = lax.all_gather(jnp.stack([a1, a2, a3, dy2]), ITEM, axis=0, tiled=False)
    a1_all, a2_all, a3_all, dy2_all = (acts[:, n] for n in range(4))

    dqc, dkv = cross_backward(order, n_live, qc, do_c, keep_cross, kv, scale)
    halves = dkv.reshape(BLOCKS, 2 * HEAD, 2, TOK).transpose(0, 2, 1, 3).reshape(BLOCKS, 4 * HEAD, TOK)
    got = swap(jnp.concatenate([dqc, halves], 1), ITEM)
    dqc_t = got[:, :HEAD].reshape(width, TOK)
    dkv_t = got[:, HEAD:].reshape(HEADS, 2, 2, HEAD, TOK).transpose(2, 0, 3, 1, 4).reshape(2, width, SLOTS)
    patches_grad = mm(dkv_t[0], cross_key, 0, 1) + mm(dkv_t[1], cross_value, 0, 1)
    da2 = mm(dqc_t, cross_query, 0, 1)
    back2, dg2, db2 = norm_backward(da2, xh2, r2, gains[2])
    d_first = d_second + back2
    dy1 = d_first.astype(bf16)
    dy1_all = lax.all_gather(dy1, ITEM, axis=0, tiled=False)
    do1 = swap(heads_of(output_weight, dy1, 1, 1), ITEM)
    dqkv = self_backward(qkv, do1, keep_self, scale)
    dqkv_t = swap(dqkv, ITEM)
    da1 = sum(
        mm(dqkv_t[:, n * HEAD : (n + 1) * HEAD].reshape(width, TOK), w, 0, 1)
        for n, w in enumerate((query_weight, key_weight, value_weight))
    )
    back1, dg1, db1 = norm_backward(da1, xh1, r1, gains[0])
    tokens_grad = d_first + back1

    qkv_grad = over_item(dqkv, a1_all)
    cq_grad = over_item(dqc, a2_all)
    ckv_grad = over_item(dkv, patches_all)
    e_grad = over_item(du_all, a3_all)
    turned = lambda gathered, block: lax.dot_general(
        gathered, block, (((0, 1), (0, 2)), ((), ())), preferred_element_type=f32
    )
    o_grad = turned(dy1_all, o_t)
    co_grad = turned(dy2_all, oc_t)
    r_grad = turned(grad_out_all, h_all)

    camera_grad = jnp.concatenate([dg1, db1, dg2, db2, dg3, db3]).reshape(8, 4, -1).transpose(1, 0, 2)
    camera_grad = swap(jnp.broadcast_to(camera_grad[None], (4,) + camera_grad.shape).reshape(16, 8, -1), ITEM)
    camera_grad = jnp.sum(camera_grad, 0)
    high = camera_grad.astype(bf16)
    low = (camera_grad - high.astype(f32)).astype(bf16)
    camera_rows = jnp.pad(jnp.stack([high, low], 1), ((0, 0), (0, 14), (0, 256 - camera_grad.shape[1])))

    pieces = [qkv_grad[n * HEAD : (n + 1) * HEAD] for n in range(3)]
    pieces += [cq_grad, ckv_grad[:HEAD], ckv_grad[HEAD:], e_grad]
    pieces = [column_pieces(piece) for piece in pieces]
    columns = sum(piece.shape[1] for piece in pieces)
    got = swap(jnp.concatenate(pieces + [camera_rows], 1), ITEMS).astype(f32)
    from_items = got[:, columns] + got[:, columns + 1]
    hits = camera_ids[None, :] == (view * 4 + jnp.arange(4))[:, None]
    modulation_grad = jnp.sum(jnp.where(hits[:, :, None], from_items[None], 0.0), 1)[:, :192]
    summed = lax.ppermute(jnp.sum(got[:, :columns], 0), AXES, home_route())

    row_grads = jnp.concatenate([o_grad, co_grad, r_grad], 1).astype(bf16).reshape(32, 32, -1)
    got = swap(row_grads, ROW).astype(f32)
    row_sums = jnp.sum(got.reshape((8, 4) + got.shape[1:]), 0)
    rows_of = lambda lo, hi: row_sums[:, :, lo:hi].transpose(0, 2, 1).reshape(4 * (hi - lo), 32)

    half = HEAD // 2
    column_outs = [summed[n * half : (n + 1) * half].T for n in range(6)]
    return (
        layer_out[None, None],
        tokens_grad[None, None],
        patches_grad[None, None],
        modulation_grad,
        column_outs[0],
        column_outs[1],
        column_outs[2],
        rows_of(0, HEAD),
        column_outs[3],
        column_outs[4][:192],
        column_outs[5][:192],
        rows_of(HEAD, 2 * HEAD),
        summed[6 * half :].T,
        rows_of(2 * HEAD, 2 * HEAD + hidden),
    )


def solution(mesh):
    fine = Mesh(mesh.devices.reshape(SIZES), AXES)
    split = P(ROW, VIEW, None, None)
    grads = P(VIEW, ROW)
    return jax.shard_map(
        on_device,
        mesh=fine,
        in_specs=(split, split) + (P(),) * 13 + (split,),
        out_specs=(split,) * 3 + (grads,) * 11,
        check_vma=False,
    )
```

time: 3600 us -> 513 us (0.14)
  waiting for transfers between devices: 2890 us -> 129 us
  matrix products: 257 us -> 77.7 us
  local copies, waits for them, and re-layouts: 239 us -> 67.3 us
  other arithmetic: 123 us -> 26.8 us
  Pallas kernels: 0 us -> 62.5 us
  starting transfers between devices: 13.4 us -> 64.9 us
  blocking collectives: 16.8 us -> 59.2 us
    unnamed x41 -> x4, waiting for transfers between devices: 1260 us -> 1.41 us
    reduce_scatter x14 -> x0, waiting for transfers between devices: 1070 us -> none  [the longest x1 169 us: on_device(): lax.psum_scatter(partly[9], 'row', scatter_dimension=1, tiled=True)]
    ppermute x16 -> x1, waiting for transfers between devices: 442 us -> 14.9 us  [on_device(): summed = lax.ppermute(jnp.sum(got[:, :columns], 0), AXES, home_route())]
    dot_general x90 -> x26, matrix products: 257 us -> 77.7 us  [the longest x19 50.6 us: mm(): lax.dot_general(left, right, (((lc,), (rc,)), ((), ())), preferred_elemen...]
    dynamic_slice x86 -> x3, local copies, waits for them, and re-layouts: 82.4 us -> 2.65 us  [the longest x1 1.24 us: on_device(): camera = lax.dynamic_index_in_dim(camera_ids, item, 0, keepdims=False)]
    pallas_call x0 -> x4, Pallas kernels: none -> 62.5 us  [the longest x1 20.6 us: cross_backward(): pl.pallas_call(partial(cross_backward_kernel, scale=scale, step=2), out_s...]
    all_to_all x0 -> x9, starting transfers between devices: none -> 61.2 us  [swap(): return lax.all_to_all(block, axes, 0, 0, tiled=True)]
    select_n x16 -> x1, other arithmetic: 60.4 us -> 0.01 us  [on_device(): rank = jnp.where(live, jnp.cumsum(live) - 1, n_live + jnp.cumsum(~live) - 1)]
  transfers between devices with their start and end apart: 46 -> 14, of which waited for: 38 -> 10; matrix products, arithmetic and copies ran while one was open for 7% -> 25% of each run, Pallas kernels for 0% -> 9%
where the time goes in v1:
time: 513 us; the launch traced here: 504 us
  waiting for transfers between devices  129 us (25%)
  matrix products  77.7 us (15%)
  local copies, waits for them, and re-layouts  67.3 us (13%)
  starting transfers between devices  64.9 us (13%)
  Pallas kernels  62.5 us (12%)
  blocking collectives  59.2 us (12%)
  other arithmetic  26.8 us (5%)
  between operations  17 us (3%)
    all_gather x1, waiting for transfers between devices, on_device(): lax.all_gather(jnp.stack([a1, a2, a3, dy2]), ITEM, axis=0, tiled=False)  70.9 us
    all_to_all x9, starting transfers between devices, swap(): return lax.all_to_all(block, axes, 0, 0, tiled=True)  61.2 us
    all_to_all x2, blocking collectives, swap(): return lax.all_to_all(block, axes, 0, 0, tiled=True)  59.2 us
    dot_general x19, matrix products, mm(): lax.dot_general(left, right, (((lc,), (rc,)), ((), ())), preferred_elemen...  50.6 us
    all_to_all x9, waiting for transfers between devices, swap(): return lax.all_to_all(block, axes, 0, 0, tiled=True)  41.7 us
    pallas_call x1, Pallas kernels, cross_backward(): pl.pallas_call(partial(cross_backward_kernel, scale=scale, step=2), out_s...  20.6 us
    pallas_call x1, Pallas kernels, cross_forward(): pl.pallas_call(partial(cross_forward_kernel, scale=scale, step=2), out_sh...  17 us
    dot_general x4, matrix products, over_item(): lax.dot_general(turned, gathered, (((0, 2), (0, 1)), ((), ())), preferred...  16.1 us
  transfers between devices with their start and end apart: 14, of which 10 were waited for; matrix products, arithmetic and copies ran while one was open for 25% of the time, Pallas kernels for 9%

profile of v1, /device:TPU:25, one launch (start us, length us, event | category | flops | bytes accessed | tf_op | source)
XLA Modules:
  0.0 504.5 jit_solution(4646358337094766219)
XLA Ops:
  21.3 6.4 %all-to-all-start = ((bf16[16,192,128]{2,1,0:T(8,128)(2,1)}), bf16[16,192,128]{2,1,0:T(8,128)(2,1)S(1)}, u32[]{:S(2)}, u32[]{:S(2)}) async-start(bf16[16,192,128]{2,1,0:T(8,128)(2,1)} %pad_maximum_fusion.3), calls=%async_computation | async-start | bytes 1572864 | tf_op jit(solution)/shard_map/all_to_all | solution.py:39
  28.8 12.4 %all-to-all-done.qkv_ref = bf16[16,192,128]{2,1,0:T(8,128)(2,1)S(1)} async-done(((bf16[16,192,128]{2,1,0:T(8,128)(2,1)}), bf16[16,192,128]{2,1,0:T(8,128)(2,1)S(1)}, u32[]{:S(2)}, u32[]{:S(2)}) %all-to-all-start) | async-done | bytes 786464 | tf_op jit(solution)/shard_map/all_to_all | solution.py:39
  42.1 11.3 %self_forward.1 = (bf16[16,64,128]{2,1,0:T(8,128)(2,1)}, f32[16,72,128]{2,1,0:T(8,128)}) custom-call(bf16[16,192,128]{2,1,0:T(8,128)(2,1)} %copy-done.18), custom_call_target="tpu_custom_call" | custom-call | flops 4294967296 | bytes 4194304 | tf_op jit(solution)/shard_map/self_forward/pallas_call | solution.py:223
  53.4 7.7 %all-to-all-start.1 = ((bf16[16,64,128]{2,1,0:T(8,128)(2,1)}), bf16[16,64,128]{2,1,0:T(8,128)(2,1)S(1)}, u32[]{:S(2)}, u32[]{:S(2)}) async-start(bf16[16,64,128]{2,1,0:T(8,128)(2,1)} %get-tuple-element.20), calls=%async_computation.1 | async-start | bytes 524288 | tf_op jit(solution)/shard_map/all_to_all | solution.py:39
  63.9 3.3 all-to-all-done.1
  67.2 2.3 fusion.99
  71.6 6.6 %all-to-all-start.2 = ((bf16[16,64,128]{2,1,0:T(8,128)(2,1)}), bf16[16,64,128]{2,1,0:T(8,128)(2,1)S(1)}, u32[]{:S(2)}, u32[]{:S(2)}) async-start(bf16[16,64,128]{2,1,0:T(8,128)(2,1)} %bitcast.15), calls=%async_computation.2 | async-start | bytes 524288 | tf_op jit(solution)/shard_map/all_to_all | solution.py:39
  78.2 6.1 %convolution_convert_fusion.1.kv_ref = bf16[128,4096]{1,0:T(8,128)(2,1)} fusion(bf16[4096,768]{1,0:T(8,128)(2,1)} %bitcast.311, bf16[768,64]{1,0:T(8,128)(2,1)S(1)} %get-tuple-element.167, bf16[768,64]{1,0:T(8,128)(2,1)S(1)} %get-tuple-element.168), kind=kOutput, calls=%fused_computation.5 | convolution fusion | flops 806223872 | bytes 7536640 | tf_op jit(solution)/shard_map/dot_general | solution.py:35
  85.1 17.0 %cross_forward.1 = (bf16[16,64,128]{2,1,0:T(8,128)(2,1)}, f32[16,72,128]{2,1,0:T(8,128)}) custom-call(s32[16]{0:T(128)} %select_reduce_fusion.1.order_ref, s32[1]{0:T(128)} %bitcast.11.live_ref, bf16[16,64,128]{2,1,0:T(8,128)(2,1)} %copy-done.25, bf16[128,4096]{1,0:T(8,128)(2,1)} %convolution_convert_fusion.1.kv_ref), custom_call_target="tpu_custom_call" | custom-call | flops 6979321856 | bytes 4194304 | tf_op jit(solution)/shard_map/cross_forward/pallas_call | solution.py:257
  102.0 5.7 %all-to-all-start.3 = ((bf16[16,64,128]{2,1,0:T(8,128)(2,1)}), bf16[16,64,128]{2,1,0:T(8,128)(2,1)S(1)}, u32[]{:S(2)}, u32[]{:S(2)}) async-start(bf16[16,64,128]{2,1,0:T(8,128)(2,1)} %get-tuple-element.21), calls=%async_computation.3 | async-start | bytes 524288 | tf_op jit(solution)/shard_map/all_to_all | solution.py:39
  108.7 4.4 all-to-all-done.3
  113.8 2.4 fusion.100
  116.5 6.5 %multiply_convert_fusion = (bf16[4096,128]{0,1:T(8,128)(2,1)}, f32[4096,128]{0,1:T(8,128)S(1)}) fusion(bf16[1024,4096]{1,0:T(8,128)(2,1)} %param.29, f32[128,1024]{1,0:T(8,128)S(1)} %get-tuple-element.161, f32[1024]{0:T(1024)S(1)} %bitcast.373, f32[1024]{0:T(1024)S(1)} %bitcast.363, f32[128]{0:T(128)S(1)} %add_rsqrt_fusion, f32[128]{0:T(128)S(1)} %broadcast_multiply_fusion.6), kind=kOutput, calls=%fused_computation.28 | convolution fusion | flops 1079115776 | bytes 12067840 | tf_op jit(solution)/shard_map/dot_general | solution.py:35
  123.0 3.6 fusion.16
  127.6 3.7 fusion.101
  131.2 2.3 copy.189
  133.5 2.6 multiply_reduce_fusion
  136.1 2.3 copy.188
  138.4 2.3 convert_bitcast_fusion.2
  146.6 37.1 %all_to_all.55 = bf16[16,576,128]{2,1,0:T(8,128)(2,1)S(1)} all-to-all(bf16[16,576,128]{2,1,0:T(8,128)(2,1)S(1)} %pad_maximum_fusion), channel_id=1, replica_groups=mesh['yh'=2,'c'=2,'x'=4,'zh'=2,'zl'=2,'yl'=2] {'yh','c','zl','yl'}, dimensions={0} | all-to-all | bytes 4718592 | tf_op jit(solution)/shard_map/all_to_all | solution.py:39
  185.8 20.6 %cross_backward.1 = (bf16[16,64,128]{2,1,0:T(8,128)(2,1)}, bf16[16,128,256]{2,1,0:T(8,128)(2,1)}) custom-call(s32[16]{0:T(128)} %select_reduce_fusion.1.order_ref, s32[1]{0:T(128)} %bitcast.11.live_ref, bf16[16,64,128]{2,1,0:T(8,128)(2,1)} %copy-done.25, bf16[16,64,128]{2,1,0:T(8,128)(2,1)} %slice.180.do_ref, f32[16,72,128]{2,1,0:T(8,128)} %get-tuple-element.22.keep_ref, ...), custom_call_target="tpu_custom_call" | custom-call | flops 17448304640 | bytes 4194304 | tf_op jit(solution)/shard_map/cross_backward/pallas_call | solution.py:271
  208.0 22.1 %all_to_all.56 = bf16[16,320,128]{2,1,0:T(8,128)(2,1)S(1)} all-to-all(bf16[16,320,128]{2,1,0:T(8,128)(2,1)S(1)} %pad_maximum_fusion.1), channel_id=1, replica_groups=mesh['yh'=2,'c'=2,'x'=4,'zh'=2,'zl'=2,'yl'=2] {'yh','c','zl','yl'}, dimensions={0} | all-to-all | bytes 2621440 | tf_op jit(solution)/shard_map/all_to_all | solution.py:39
  235.2 2.2 pad_maximum_fusion.2
  238.1 5.8 %fusion.34 = f32[1,1,128,1024]{3,2,1,0:T(8,128)} fusion(f32[128,1024]{1,0:T(8,128)S(1)} %get-tuple-element.161, bf16[4096,128]{0,1:T(8,128)(2,1)} %get-tuple-element.162, bf16[4096,1024]{1,0:T(8,128)(2,1)} %param.30), kind=kOutput, calls=%fused_computation.46 | convolution fusion | flops 1073872896 | bytes 10485760 | tf_op jit(solution)/shard_map/dot_general | solution.py:35
  243.8 3.8 fusion.31
  248.6 3.3 fusion.49
  253.7 6.6 %all-to-all-start.6 = ((bf16[16,64,128]{2,1,0:T(8,128)(2,1)}), bf16[16,64,128]{2,1,0:T(8,128)(2,1)}, u32[]{:S(2)}, u32[]{:S(2)}) async-start(bf16[16,64,128]{2,1,0:T(8,128)(2,1)} %bitcast.335), calls=%async_computation.6 | async-start | bytes 524288 | tf_op jit(solution)/shard_map/all_to_all | solution.py:39
  260.3 4.5 fusion.41
  266.8 13.6 %self_backward.1 = bf16[16,192,128]{2,1,0:T(8,128)(2,1)} custom-call(bf16[16,192,128]{2,1,0:T(8,128)(2,1)} %copy-done.18, bf16[16,64,128]{2,1,0:T(8,128)(2,1)} %all-to-all-done.6.do_ref, f32[16,72,128]{2,1,0:T(8,128)} %get-tuple-element.25.keep_ref), custom_call_target="tpu_custom_call" | custom-call | flops 10737418240 | bytes 4194304 | tf_op jit(solution)/shard_map/self_backward/pallas_call | solution.py:237
  280.4 7.3 %all-to-all-start.7 = ((bf16[16,192,128]{2,1,0:T(8,128)(2,1)}), bf16[16,192,128]{2,1,0:T(8,128)(2,1)}, u32[]{:S(2)}, u32[]{:S(2)}) async-start(bf16[16,192,128]{2,1,0:T(8,128)(2,1)} %self_backward.1), calls=%async_computation.7 | async-start | bytes 1572864 | tf_op jit(solution)/shard_map/all_to_all | solution.py:39
  299.1 2.4 fusion.103
  302.5 2.3 fusion.69
  305.6 7.0 %all-to-all-start.8 = ((f32[16,8,192]{2,1,0:T(8,128)}), f32[16,8,192]{2,1,0:T(8,128)S(1)}, u32[]{:S(2)}, u32[]{:S(2)}) async-start(f32[16,8,192]{2,1,0:T(8,128)} %bitcast.67), calls=%async_computation.8 | async-start | bytes 262144 | tf_op jit(solution)/shard_map/all_to_all | solution.py:39
  312.6 3.1 fusion.26
  317.6 3.1 fusion.52
  321.6 70.9 %all-gather.11.cloned.1.call-done = bf16[64,128,1024]{2,1,0:T(8,128)(2,1)} async-done(((bf16[4,128,1024]{2,1,0:T(8,128)(2,1)}), bf16[64,128,1024]{2,1,0:T(8,128)(2,1)}) %all-gather.11.cloned.1.call-update) | async-done | bytes 16777232 | tf_op jit(solution)/shard_map/all_gather | solution.py:392
  392.5 4.0 fusion.27
  396.5 3.0 fusion.51
  399.5 4.8 slice_bitcast_fusion
  404.3 6.9 %copy.206 = bf16[1024,16,128]{2,1,0:T(8,128)(2,1)} copy(bf16[1024,16,128]{0,2,1:T(8,128)(2,1)} %slice_bitcast_fusion) | data formatting | bytes 8388608 | tf_op jit(solution)/shard_map/dot_general | solution.py:420
  411.3 4.1 fusion.35
  415.5 4.6 fusion.21
  427.2 7.7 %all-to-all-start.10 = ((bf16[32,32,384]{2,1,0:T(8,128)(2,1)}), bf16[32,32,384]{2,1,0:T(8,128)(2,1)S(1)}, u32[]{:S(2)}, u32[]{:S(2)}) async-start(bf16[32,32,384]{2,1,0:T(8,128)(2,1)} %pad_maximum_fusion.4), calls=%async_computation.10 | async-start | bytes 1572864 | tf_op jit(solution)/shard_map/all_to_all | solution.py:39
  448.4 6.2 %all-to-all-start.9 = ((bf16[8,336,256]{2,1,0:T(8,128)(2,1)}), bf16[8,336,256]{2,1,0:T(8,128)(2,1)}, u32[]{:S(2)}, u32[]{:S(2)}) async-start(bf16[8,336,256]{2,1,0:T(8,128)(2,1)} %pad_dynamic-update-slice_fusion.2), calls=%async_computation.9 | async-start | bytes 2752512 | tf_op jit(solution)/shard_map/all_to_all | solution.py:39
  454.7 2.2 fusion.68
  459.3 16.0 %all-to-all-done.9 = bf16[8,336,256]{2,1,0:T(8,128)(2,1)} async-done(((bf16[8,336,256]{2,1,0:T(8,128)(2,1)}), bf16[8,336,256]{2,1,0:T(8,128)(2,1)}, u32[]{:S(2)}, u32[]{:S(2)}) %all-to-all-start.9) | async-done | bytes 1376288 | tf_op jit(solution)/shard_map/all_to_all | solution.py:39
  477.1 3.4 collective-permute-start
  481.2 14.9 %collective-permute-done = f32[320,256]{1,0:T(8,128)S(1)} collective-permute-done((f32[320,256]{1,0:T(8,128)S(1)}, f32[320,256]{1,0:T(8,128)S(1)}, u32[]{:S(2)}, u32[]{:S(2)}) %collective-permute-start) | collective-permute-done | bytes 327712 | tf_op jit(solution)/shard_map/ppermute | solution.py:442
  (239 shorter events, 85.1 us)
Async XLA Ops:
  7.2 10.2 %copy-start = (bf16[1024,1024]{1,0:T(8,128)(2,1)S(1)}, bf16[1024,1024]{1,0:T(8,128)(2,1)}, u32[]{:S(2)}) copy-start(bf16[1024,1024]{1,0:T(8,128)(2,1)} %param.23) | copy-start | bytes 6291460
  7.2 10.2 %copy-start.1 = (bf16[1,1,128,1024]{3,2,1,0:T(8,128)(2,1)S(1)}, bf16[1,1,128,1024]{3,2,1,0:T(8,128)(2,1)}, u32[]{:S(2)}) copy-start(bf16[1,1,128,1024]{3,2,1,0:T(8,128)(2,1)} %param.16) | copy-start | bytes 786436
  7.2 71.0 %all-gather.9.cloned.1.call-start = ((), (), s32[]{:S(2)}) async-start(), calls=%async_computation.11 | async-start | bytes 6684672 | tf_op jit(solution)/shard_map/all_gather | solution.py:342
  12.7 5.4 %copy-start.26 = (f32[1,1024]{1,0:T(1,128)}, f32[1,1024]{1,0:T(1,128)S(1)}, u32[]{:S(2)}) copy-start(f32[1,1024]{1,0:T(1,128)S(1)} %get-tuple-element.143) | copy-start | bytes 12292
  13.8 4.3 copy-start.32
  14.9 3.1 copy-start.39
  20.2 7.5 %copy-start.43 = (s32[8,4]{0,1:T(4,128)S(1)}, s32[8,4]{0,1:T(4,128)}, u32[]{:S(2)}) copy-start(s32[8,4]{0,1:T(4,128)} %param.18) | copy-start | bytes 388
  21.3 19.9 %all-to-all-start = ((bf16[16,192,128]{2,1,0:T(8,128)(2,1)}), bf16[16,192,128]{2,1,0:T(8,128)(2,1)S(1)}, u32[]{:S(2)}, u32[]{:S(2)}) async-start(bf16[16,192,128]{2,1,0:T(8,128)(2,1)} %pad_maximum_fusion.3), calls=%async_computation | async-start | bytes 1572864 | tf_op jit(solution)/shard_map/all_to_all | solution.py:39
  53.4 13.7 %all-to-all-start.1 = ((bf16[16,64,128]{2,1,0:T(8,128)(2,1)}), bf16[16,64,128]{2,1,0:T(8,128)(2,1)S(1)}, u32[]{:S(2)}, u32[]{:S(2)}) async-start(bf16[16,64,128]{2,1,0:T(8,128)(2,1)} %get-tuple-element.20), calls=%async_computation.1 | async-start | bytes 524288 | tf_op jit(solution)/shard_map/all_to_all | solution.py:39
  67.1 3.1 copy-start.4
  71.6 12.8 %all-to-all-start.2 = ((bf16[16,64,128]{2,1,0:T(8,128)(2,1)}), bf16[16,64,128]{2,1,0:T(8,128)(2,1)S(1)}, u32[]{:S(2)}, u32[]{:S(2)}) async-start(bf16[16,64,128]{2,1,0:T(8,128)(2,1)} %bitcast.15), calls=%async_computation.2 | async-start | bytes 524288 | tf_op jit(solution)/shard_map/all_to_all | solution.py:39
  102.0 11.1 %all-to-all-start.3 = ((bf16[16,64,128]{2,1,0:T(8,128)(2,1)}), bf16[16,64,128]{2,1,0:T(8,128)(2,1)S(1)}, u32[]{:S(2)}, u32[]{:S(2)}) async-start(bf16[16,64,128]{2,1,0:T(8,128)(2,1)} %get-tuple-element.21), calls=%async_computation.3 | async-start | bytes 524288 | tf_op jit(solution)/shard_map/all_to_all | solution.py:39
  107.7 8.7 %copy-start.28 = (f32[1,1024]{1,0:T(1,128)S(1)}, f32[1,1024]{1,0:T(1,128)}, u32[]{:S(2)}) copy-start(f32[1,1024]{1,0:T(1,128)} %get-tuple-element.145) | copy-start | bytes 12292
  107.8 136.1 %all-gather.15.cloned.1.call-start = ((), (), s32[]{:S(2)}) async-start(), calls=%async_computation.14 | async-start | bytes 4456448 | tf_op jit(solution)/shard_map/all_gather | solution.py:343
  108.5 209.1 %all-gather.13.cloned.1.call-start = ((), (), s32[]{:S(2)}) async-start(), calls=%async_computation.13 | async-start | bytes 4456448 | tf_op jit(solution)/shard_map/all_gather | solution.py:405
  113.8 9.1 %slice-start = ((s8[8388608]{0:T(1024)(128)(4,1)}), s8[4194304]{0:T(1024)(128)(4,1)S(1)}, s32[]{:S(2)}) async-start(s8[8388608]{0:T(1024)(128)(4,1)} %bitcast.312), calls=%async_computation.15 | async-start | bytes 8388608
  116.4 6.5 %slice-start.1 = ((s8[8388608]{0:T(1024)(128)(4,1)}), s8[4194304]{0:T(1024)(128)(4,1)S(1)}, s32[]{:S(2)}) async-start(s8[8388608]{0:T(1024)(128)(4,1)} %bitcast.312), calls=%async_computation.16 | async-start | bytes 8388608
  116.4 6.5 %copy-start.15 = (bf16[1,1,128,1024]{3,2,1,0:T(8,128)(2,1)S(1)}, bf16[1,1,128,1024]{3,2,1,0:T(8,128)(2,1)}, u32[]{:S(2)}) copy-start(bf16[1,1,128,1024]{3,2,1,0:T(8,128)(2,1)} %param.31) | copy-start | bytes 786436
  116.5 11.1 %slice-start.2 = ((s8[8388608]{0:T(1024)(128)(4,1)}), s8[4194304]{0:T(1024)(128)(4,1)S(1)}, s32[]{:S(2)}) async-start(s8[8388608]{0:T(1024)(128)(4,1)} %bitcast.314), calls=%async_computation.17 | async-start | bytes 8388608
  123.0 4.6 slice-start.3
  138.4 3.1 copy-start.3
  208.0 23.2 %copy-start.5 = (bf16[1024,1024]{1,0:T(8,128)(2,1)S(1)}, bf16[1024,1024]{1,0:T(8,128)(2,1)}, u32[]{:S(2)}) copy-start(bf16[1024,1024]{1,0:T(8,128)(2,1)} %param.25) | copy-start | bytes 6291460
  232.1 2.9 copy-start.27
  232.1 2.9 copy-start.33
  232.1 2.8 copy-start.40
  234.9 157.6 %all-gather.11.cloned.1.call-start = ((), (), s32[]{:S(2)}) async-start(), calls=%async_computation.12 | async-start | bytes 17825792 | tf_op jit(solution)/shard_map/all_gather | solution.py:392
  248.6 11.7 %copy-start.2 = (bf16[16,128,256]{2,1,0:T(8,128)(2,1)S(1)}, bf16[16,128,256]{2,1,0:T(8,128)(2,1)}, u32[]{:S(2)}) copy-start(bf16[16,128,256]{2,1,0:T(8,128)(2,1)} %get-tuple-element.24) | copy-start | bytes 3145732
  253.7 13.1 %all-to-all-start.6 = ((bf16[16,64,128]{2,1,0:T(8,128)(2,1)}), bf16[16,64,128]{2,1,0:T(8,128)(2,1)}, u32[]{:S(2)}, u32[]{:S(2)}) async-start(bf16[16,64,128]{2,1,0:T(8,128)(2,1)} %bitcast.335), calls=%async_computation.6 | async-start | bytes 524288 | tf_op jit(solution)/shard_map/all_to_all | solution.py:39
  280.4 17.4 %all-to-all-start.7 = ((bf16[16,192,128]{2,1,0:T(8,128)(2,1)}), bf16[16,192,128]{2,1,0:T(8,128)(2,1)}, u32[]{:S(2)}, u32[]{:S(2)}) async-start(bf16[16,192,128]{2,1,0:T(8,128)(2,1)} %self_backward.1), calls=%async_computation.7 | async-start | bytes 1572864 | tf_op jit(solution)/shard_map/all_to_all | solution.py:39
  287.7 5.2 %slice-start.4 = ((bf16[16,320,128]{2,1,0:T(8,128)(2,1)}), bf16[16,256,128]{2,1,0:T(8,128)(2,1)S(1)}, s32[]{:S(2)}) async-start(bf16[16,320,128]{2,1,0:T(8,128)(2,1)} %copy-done.6), calls=%async_computation.19 | async-start | bytes 2097152 | tf_op jit(solution)/shard_map/slice | solution.py:399
  292.9 2.6 copy-start.14
  297.8 3.8 copy-start.13
  305.6 12.0 %copy-start.16 = (bf16[16,64,128]{2,1,0:T(8,128)(2,1)S(1)}, bf16[16,64,128]{2,1,0:T(8,128)(2,1)}, u32[]{:S(2)}) copy-start(bf16[16,64,128]{2,1,0:T(8,128)(2,1)} %get-tuple-element.20) | copy-start | bytes 786436
  305.6 11.9 %all-to-all-start.8 = ((f32[16,8,192]{2,1,0:T(8,128)}), f32[16,8,192]{2,1,0:T(8,128)S(1)}, u32[]{:S(2)}, u32[]{:S(2)}) async-start(f32[16,8,192]{2,1,0:T(8,128)} %bitcast.67), calls=%async_computation.8 | async-start | bytes 262144 | tf_op jit(solution)/shard_map/all_to_all | solution.py:39
  317.6 74.9 %copy-start.19 = (bf16[16,192,128]{2,1,0:T(8,128)(2,1)S(1)}, bf16[16,192,128]{2,1,0:T(8,128)(2,1)}, u32[]{:S(2)}) copy-start(bf16[16,192,128]{2,1,0:T(8,128)(2,1)} %self_backward.1) | copy-start | bytes 2359300
  392.5 4.0 copy-start.23
  404.3 6.9 %copy-start.24 = (bf16[16,64,128]{2,1,0:T(8,128)(2,1)S(1)}, bf16[16,64,128]{2,1,0:T(8,128)(2,1)}, u32[]{:S(2)}) copy-start(bf16[16,64,128]{2,1,0:T(8,128)(2,1)} %get-tuple-element.21) | copy-start | bytes 786436
  420.1 4.9 copy-start.11
  427.2 18.1 %copy-start.21 = (bf16[2,32,4,192]{3,1,2,0:T(8,128)(2,1)S(1)}, bf16[2,32,4,192]{3,1,2,0:T(8,128)(2,1)}, u32[]{:S(2)}) copy-start(bf16[2,32,4,192]{3,1,2,0:T(8,128)(2,1)} %copy.199) | copy-start | bytes 294916
  427.2 18.8 %copy-start.20 = (bf16[2,32,4,192]{3,1,2,0:T(8,128)(2,1)S(1)}, bf16[2,32,4,192]{3,1,2,0:T(8,128)(2,1)}, u32[]{:S(2)}) copy-start(bf16[2,32,4,192]{3,1,2,0:T(8,128)(2,1)} %copy.200) | copy-start | bytes 294916
  427.2 21.3 %all-to-all-start.10 = ((bf16[32,32,384]{2,1,0:T(8,128)(2,1)}), bf16[32,32,384]{2,1,0:T(8,128)(2,1)S(1)}, u32[]{:S(2)}, u32[]{:S(2)}) async-start(bf16[32,32,384]{2,1,0:T(8,128)(2,1)} %pad_maximum_fusion.4), calls=%async_computation.10 | async-start | bytes 1572864 | tf_op jit(solution)/shard_map/all_to_all | solution.py:39
  439.8 6.9 %copy-start.12 = (bf16[2,128,4,256]{3,1,2,0:T(8,128)(2,1)S(1)}, bf16[2,128,4,256]{3,1,2,0:T(8,128)(2,1)}, u32[]{:S(2)}) copy-start(bf16[2,128,4,256]{3,1,2,0:T(8,128)(2,1)} %copy.202) | copy-start | bytes 1572868
  446.0 8.7 %copy-start.46 = (f32[128]{0:T(128)S(1)}, f32[128]{0:T(128)}, u32[]{:S(2)}) copy-start(f32[128]{0:T(128)} %get-tuple-element.115) | copy-start | bytes 1540
  446.0 8.7 %copy-start.45 = (f32[128]{0:T(128)S(1)}, f32[128]{0:T(128)}, u32[]{:S(2)}) copy-start(f32[128]{0:T(128)} %get-tuple-element.116) | copy-start | bytes 1540
  446.0 8.7 %copy-start.42 = (f32[128]{0:T(128)S(1)}, f32[128]{0:T(128)}, u32[]{:S(2)}) copy-start(f32[128]{0:T(128)} %copy-done.39) | copy-start | bytes 1540
  448.4 26.9 %all-to-all-start.9 = ((bf16[8,336,256]{2,1,0:T(8,128)(2,1)}), bf16[8,336,256]{2,1,0:T(8,128)(2,1)}, u32[]{:S(2)}, u32[]{:S(2)}) async-start(bf16[8,336,256]{2,1,0:T(8,128)(2,1)} %pad_dynamic-update-slice_fusion.2), calls=%async_computation.9 | async-start | bytes 2752512 | tf_op jit(solution)/shard_map/all_to_all | solution.py:39
  476.9 3.6 copy-start.44
  477.1 19.0 %collective-permute-start = (f32[320,256]{1,0:T(8,128)S(1)}, f32[320,256]{1,0:T(8,128)S(1)}, u32[]{:S(2)}, u32[]{:S(2)}) collective-permute-start(f32[320,256]{1,0:T(8,128)S(1)} %slice_reduce_fusion), channel_id=1, source_target_pairs={{0,0},{1,2},{2,4},{3,6},{4,32},{5,34},{6,36},{7,38},{8,64},{9,66},... | collective-permute-start | bytes 983048 | tf_op jit(solution)/shard_map/ppermute | solution.py:442
  (19 other events, 24.9 us)
Sparse Core Ops, SparseCore 0:
  9.7 64.5 all-gather.8
  110.3 73.8 all-gather.14
  235.0 54.5 all-gather.12
  291.1 101.3 all-gather.10

commit v2 on v1

--- a/solution.py
+++ b/solution.py
@@ -25,7 +25,7 @@
 ROW = ("x", "zh", "zl", "yl")
 ITEM = ("yh", "c", "zl", "yl")
 ITEMS = ("x", "zh")
-VMEM_BYTES = 56 * 1024 * 1024
+VMEM_BYTES = 32 * 1024 * 1024
 
 bf16 = jnp.bfloat16
 f32 = jnp.float32
@@ -296,19 +296,404 @@
 def norm_backward(da, xh, r, gain):
     d = da * (1.0 + gain)
     along = jnp.mean(d * xh, -1, keepdims=True)
-    back = r * (d - jnp.mean(d, -1, keepdims=True) - xh * along)
-    return back, jnp.sum(da * xh, 0), jnp.sum(da, 0)
-
-
-def over_item(turned, gathered):
-    return lax.dot_general(turned, gathered, (((0, 2), (0, 1)), ((), ())), preferred_element_type=f32)
-
-
-def column_pieces(grad_t):
-    columns, rows = grad_t.shape
-    pieces = grad_t.astype(bf16).reshape(2, columns // 2, 4, rows // 4).transpose(0, 2, 1, 3)
-    pieces = pieces.reshape(8, columns // 2, rows // 4)
-    return jnp.pad(pieces, ((0, 0), (0, 0), (0, 256 - rows // 4)))
+    return r * (d - jnp.mean(d, -1, keepdims=True) - xh * along)
+
+
+def token_rows(ref, lo, hi):
+    block = ref[:, lo:hi, :]
+    return block.reshape(HEADS * (hi - lo), block.shape[2]).T
+
+
+def store_heads(ref, lo, value):
+    turned = value.T.astype(bf16)
+    ref[:, lo : lo + HEAD, :] = turned.reshape(HEADS, HEAD, turned.shape[1])
+
+
+def load_all(pairs, sems):
+    copies = [pltpu.make_async_copy(src, dst, sems.at[n]) for n, (src, dst) in enumerate(pairs)]
+    for copy in copies:
+        copy.start()
+    return copies
+
+
+def enter_kernel(camera_ref, x_ref, cot_ref, mod_ref, wq_any, wk_any, wv_any, sent_ref, acts_ref, gains_ref, wq, wk, wv, sems):
+    copies = load_all(((wq_any, wq), (wk_any, wk), (wv_any, wv)), sems)
+    row = mod_ref[pl.ds(camera_ref[0], 1), :]
+    for n in range(6):
+        gains_ref[n : n + 1, :] = row[:, n * WIDTH : (n + 1) * WIDTH]
+    gains_ref[6:8, :] = jnp.zeros((2, WIDTH), f32)
+    xh, _ = normed(x_ref[...].astype(f32))
+    acts_ref[0] = cot_ref[...]
+    acts_ref[1] = xh.astype(bf16)
+    a1 = (xh * (1.0 + gains_ref[0:1, :]) + gains_ref[1:2, :]).astype(bf16)
+    for n, (copy, w) in enumerate(zip(copies, (wq, wk, wv))):
+        copy.wait()
+        store_heads(sent_ref, n * HEAD, mm(a1, w[...]))
+
+
+def middle_kernel(o_ref, x_ref, gains_ref, wo_any, wcq_any, first_ref, a2_ref, q_ref, wo, wcq, sems):
+    copies = load_all(((wo_any, wo), (wcq_any, wcq)), sems)
+    o1 = token_rows(o_ref, 0, HEAD)
+    copies[0].wait()
+    first = x_ref[...].astype(f32) + mm(o1, wo[...])
+    first_ref[...] = first
+    xh, _ = normed(first)
+    a2 = (xh * (1.0 + gains_ref[2:3, :]) + gains_ref[3:4, :]).astype(bf16)
+    a2_ref[...] = a2
+    copies[1].wait()
+    store_heads(q_ref, 0, mm(a2, wcq[...]))
+
+
+def gelu_both(a3, cot, we, wr):
+    u = mm(a3, we)
+    square = u * u
+    t = jnp.tanh(u * (GELU_A + GELU_A * GELU_B * square))
+    h = (0.5 * u * (1.0 + t)).astype(bf16)
+    dh = mm(cot, wr, 1, 1).astype(bf16).astype(f32)
+    slope = 0.5 * (1.0 + t) + 0.5 * u * (1.0 - t * t) * (GELU_A + 3.0 * GELU_A * GELU_B * square)
+    return h, (dh * slope).astype(bf16)
+
+
+def mlp_kernel(
+    oc_ref, first_ref, a2_ref, cot_ref, gains_ref, wco_ref, we_ref, wr_ref,
+    out_ref, back_ref, acts_ref, do_ref, dgb_ref, a3, second, y, da3,
+):
+    step = pl.program_id(0)
+
+    @pl.when(step == 0)
+    def _():
+        total = first_ref[...] + mm(token_rows(oc_ref, 0, HEAD), wco_ref[...])
+        second[...] = total
+        xh, _ = normed(total)
+        a3[...] = (xh * (1.0 + gains_ref[4:5, :]) + gains_ref[5:6, :]).astype(bf16)
+        y[...] = jnp.zeros_like(y)
+        da3[...] = jnp.zeros_like(da3)
+
+    h, du = gelu_both(a3[...], cot_ref[...], we_ref[...], wr_ref[...])
+    y[...] += mm(h, wr_ref[...])
+    da3[...] += mm(du, we_ref[...], 1, 1)
+
+    @pl.when(step == pl.num_programs(0) - 1)
+    def _():
+        total = second[...]
+        out_ref[...] = total + y[...]
+        xh, r = normed(total)
+        d = da3[...]
+        dgb_ref[...] = jnp.zeros_like(dgb_ref)
+        dgb_ref[0:1, :] = jnp.sum(d * xh, 0, keepdims=True)
+        dgb_ref[1:2, :] = jnp.sum(d, 0, keepdims=True)
+        back = cot_ref[...].astype(f32) + norm_backward(d, xh, r, gains_ref[4:5, :])
+        back_ref[...] = back
+        dy2 = back.astype(bf16)
+        acts_ref[0] = a2_ref[...]
+        acts_ref[1] = a3[...]
+        acts_ref[2] = dy2
+        store_heads(do_ref, 0, mm(dy2, wco_ref[...], 1, 1))
+
+
+def return_kernel(dq_ref, first_ref, second_back_ref, gains_ref, wcq_any, wo_any, back_ref, dy_ref, do_ref, dgb_ref, wcq, wo, sems):
+    copies = load_all(((wcq_any, wcq), (wo_any, wo)), sems)
+    xh, r = normed(first_ref[...])
+    dq = token_rows(dq_ref, 0, HEAD)
+    copies[0].wait()
+    da2 = mm(dq, wcq[...], 1, 1)
+    dgb_ref[...] = jnp.zeros_like(dgb_ref)
+    dgb_ref[0:1, :] = jnp.sum(da2 * xh, 0, keepdims=True)
+    dgb_ref[1:2, :] = jnp.sum(da2, 0, keepdims=True)
+    back = second_back_ref[...] + norm_backward(da2, xh, r, gains_ref[2:3, :])
+    back_ref[...] = back
+    dy1 = back.astype(bf16)
+    dy_ref[...] = dy1
+    copies[1].wait()
+    store_heads(do_ref, 0, mm(dy1, wo[...], 1, 1))
+
+
+def leave_kernel(got_ref, x_ref, back_ref, gains_ref, wq_any, wk_any, wv_any, out_ref, wq, wk, wv, sems):
+    copies = load_all(((wq_any, wq), (wk_any, wk), (wv_any, wv)), sems)
+    xh, r = normed(x_ref[...].astype(f32))
+    da1 = jnp.zeros(out_ref.shape, f32)
+    for n, (copy, w) in enumerate(zip(copies, (wq, wk, wv))):
+        copy.wait()
+        da1 += mm(token_rows(got_ref, n * HEAD, (n + 1) * HEAD), w[...], 1, 1)
+    out_ref[...] = back_ref[...] + norm_backward(da1, xh, r, gains_ref[0:1, :])
+
+
+def patches_kernel(got_ref, wk_ref, wv_ref, out_ref):
+    dk = token_rows(got_ref, 0, HEAD)
+    dv = token_rows(got_ref, HEAD, 2 * HEAD)
+    out_ref[...] = mm(dk, wk_ref[...], 1, 1) + mm(dv, wv_ref[...], 1, 1)
+
+
+def side_by_side(ref, lo, hi):
+    return jnp.concatenate([ref[n, lo:hi, :] for n in range(ref.shape[0])], 1)
+
+
+def one_above_other(ref):
+    block = ref[...]
+    return block.reshape(-1, block.shape[-1])
+
+
+def store_columns(ref, at, grad_t):
+    columns, rows = grad_t.shape[0] // 2, grad_t.shape[1] // 4
+    for e in range(2):
+        for v in range(4):
+            piece = grad_t[e * columns : (e + 1) * columns, v * rows : (v + 1) * rows]
+            if rows < 256:
+                piece = jnp.concatenate([piece, jnp.zeros((columns, 256 - rows), f32)], 1)
+            ref[e * 4 + v, at : at + columns, :] = piece.astype(bf16)
+
+
+def early_kernel(
+    head_ref, cot_ref, a2_ref, a3_ref, dqc_ref, dkv_ref, patches_ref, we_ref, wr_ref, col_ref, row_ref, e_acc, r_acc, q_acc, kv_acc
+):
+    step = pl.program_id(0)
+    a3, cot = one_above_other(a3_ref), one_above_other(cot_ref)
+    h, du = gelu_both(a3, cot, we_ref[...], wr_ref[...])
+    r = mm(h.T, cot)
+    e = mm(du.T, a3)
+    q = mm(side_by_side(dqc_ref, 0, HEAD), one_above_other(a2_ref))
+    kv = mm(side_by_side(dkv_ref, 0, 2 * HEAD), one_above_other(patches_ref))
+
+    @pl.when(step == 0)
+    def _():
+        r_acc[...], e_acc[...], q_acc[...], kv_acc[...] = r, e, q, kv
+
+    @pl.when(step > 0)
+    def _():
+        r_acc[...] += r
+        e_acc[...] += e
+        q_acc[...] += q
+        kv_acc[...] += kv
+
+    @pl.when(step == pl.num_programs(0) - 1)
+    def _():
+        store_columns(col_ref, 0, q_acc[...])
+        store_columns(col_ref, 32, kv_acc[:HEAD, :])
+        store_columns(col_ref, 64, kv_acc[HEAD:, :])
+        store_columns(col_ref, 96, e_acc[...])
+        row_ref[...] = r_acc[...].T.astype(bf16).reshape(row_ref.shape)
+
+
+def late_kernel(dqkv_ref, xh_ref, wt_ref, gains_ref, col_ref, dgb_ref, qkv_acc, sums):
+    step = pl.program_id(0)
+    turned = side_by_side(dqkv_ref, 0, 3 * HEAD)
+    qkv = mm(turned, one_above_other(xh_ref))
+    total = jnp.broadcast_to(jnp.sum(turned.astype(f32), 1, keepdims=True), sums.shape)
+
+    @pl.when(step == 0)
+    def _():
+        qkv_acc[...], sums[...] = qkv, total
+
+    @pl.when(step > 0)
+    def _():
+        qkv_acc[...] += qkv
+        sums[...] += total
+
+    @pl.when(step == pl.num_programs(0) - 1)
+    def _():
+        moment = qkv_acc[...]
+        count = sums[:, 0:1]
+        weights = wt_ref[...].astype(f32)
+        dgb_ref[...] = jnp.zeros_like(dgb_ref)
+        dgb_ref[0:1, :] = jnp.sum(weights * moment, 0, keepdims=True)
+        dgb_ref[1:2, :] = jnp.sum(weights * count, 0, keepdims=True)
+        grad = moment * (1.0 + gains_ref[0:1, :]) + count * gains_ref[1:2, :]
+        for n in range(3):
+            store_columns(col_ref, n * 32, grad[n * HEAD : (n + 1) * HEAD])
+
+
+def outputs_kernel(o_ref, dy1_ref, oc_ref, dy2_ref, row_ref, acc):
+    step = pl.program_id(0)
+    o = mm(side_by_side(o_ref, 0, HEAD), one_above_other(dy1_ref))
+    oc = mm(side_by_side(oc_ref, 0, HEAD), one_above_other(dy2_ref))
+    both = jnp.concatenate([o, oc], 0)
+
+    @pl.when(step == 0)
+    def _():
+        acc[...] = both
+
+    @pl.when(step > 0)
+    def _():
+        acc[...] += both
+
+    @pl.when(step == pl.num_programs(0) - 1)
+    def _():
+        row_ref[...] = acc[...].T.astype(bf16).reshape(row_ref.shape)
+
+
+WIDTH = 1024
+HIDDEN = 4096
+PATCH = 768
+UNITS = HIDDEN // BLOCKS
+GELU_A = 0.7978845608028654
+GELU_B = 0.044715
+
+
+def shaped(*shape, dtype=bf16):
+    return jax.ShapeDtypeStruct(shape, dtype)
+
+
+ANY = pl.BlockSpec(memory_space=pl.ANY)
+V = pl.BlockSpec(memory_space=pltpu.VMEM)
+S = pl.BlockSpec(memory_space=pltpu.SMEM)
+MB = 1 << 20
+
+
+def weight(rows=WIDTH, columns=WIDTH):
+    return pltpu.VMEM((rows, columns), bf16)
+
+
+def call(kernel, name, ins, outs, scratch, flops, traffic, limit=40):
+    return pl.pallas_call(
+        kernel,
+        out_shape=outs,
+        in_specs=ins,
+        out_specs=jax.tree.map(lambda _: V, outs),
+        scratch_shapes=scratch,
+        compiler_params=pltpu.CompilerParams(vmem_limit_bytes=limit * MB),
+        cost_estimate=pl.CostEstimate(flops=flops, bytes_accessed=traffic, transcendentals=0),
+        name=name,
+    )
+
+
+TOKENS_F32 = shaped(TOK, WIDTH, dtype=f32)
+TOKENS_BF16 = shaped(TOK, WIDTH)
+ROWS_F32 = shaped(8, WIDTH, dtype=f32)
+SQUARE = 2 * TOK * WIDTH * WIDTH
+
+
+def enter(*args):
+    return call(
+        enter_kernel, "enter", [S, V, V, V, ANY, ANY, ANY],
+        (shaped(BLOCKS, 3 * HEAD, TOK), shaped(2, TOK, WIDTH), ROWS_F32),
+        [weight(), weight(), weight(), pltpu.SemaphoreType.DMA((3,))], 3 * SQUARE, 8 * MB,
+    )(*args)
+
+
+def middle(*args):
+    return call(
+        middle_kernel, "middle", [V, V, V, ANY, ANY], (TOKENS_F32, TOKENS_BF16, OUT_T),
+        [weight(), weight(), pltpu.SemaphoreType.DMA((2,))], 2 * SQUARE, 6 * MB,
+    )(*args)
+
+
+def mlp(*args):
+    steps = 8
+    width = HIDDEN // steps
+    whole = lambda *shape: pl.BlockSpec(shape, lambda i: (0,) * len(shape))
+    outs = (TOKENS_F32, TOKENS_F32, shaped(3, TOK, WIDTH), OUT_T, ROWS_F32)
+    out_specs = tuple(whole(*o.shape) for o in outs)
+    tokens = whole(TOK, WIDTH)
+    return pl.pallas_call(
+        mlp_kernel,
+        grid=(steps,),
+        out_shape=outs,
+        in_specs=[
+            whole(BLOCKS, HEAD, TOK), tokens, tokens, tokens, whole(8, WIDTH), whole(WIDTH, WIDTH),
+            pl.BlockSpec((WIDTH, width), lambda i: (0, i)), pl.BlockSpec((width, WIDTH), lambda i: (i, 0)),
+        ],
+        out_specs=out_specs,
+        scratch_shapes=[
+            pltpu.VMEM((TOK, WIDTH), bf16), pltpu.VMEM((TOK, WIDTH), f32),
+            pltpu.VMEM((TOK, WIDTH), f32), pltpu.VMEM((TOK, WIDTH), f32),
+        ],
+        compiler_params=pltpu.CompilerParams(vmem_limit_bytes=40 * MB),
+        cost_estimate=pl.CostEstimate(flops=18 * SQUARE, bytes_accessed=22 * MB, transcendentals=TOK * HIDDEN),
+        name="mlp",
+    )(*args)
+
+
+def returned(*args):
+    return call(
+        return_kernel, "returned", [V, V, V, V, ANY, ANY], (TOKENS_F32, TOKENS_BF16, OUT_T, ROWS_F32),
+        [weight(), weight(), pltpu.SemaphoreType.DMA((2,))], 2 * SQUARE, 6 * MB,
+    )(*args)
+
+
+def leave(*args):
+    return call(
+        leave_kernel, "leave", [V, V, V, V, ANY, ANY, ANY], TOKENS_F32,
+        [weight(), weight(), weight(), pltpu.SemaphoreType.DMA((3,))], 3 * SQUARE, 8 * MB,
+    )(*args)
+
+
+def patches_back(*args):
+    return call(
+        patches_kernel, "patches_back", [V, V, V], shaped(SLOTS, PATCH, dtype=f32), [], 3 * SQUARE, 5 * MB
+    )(*args)
+
+
+STEPS = 4
+
+
+def blocks_of(*shape, at=None):
+    if at is None:
+        return pl.BlockSpec((BLOCKS // STEPS,) + shape, lambda i: (i,) + (0,) * len(shape))
+    return pl.BlockSpec((BLOCKS // STEPS, 1) + shape, lambda i: (i, at) + (0,) * len(shape))
+
+
+def whole_block(*shape):
+    return pl.BlockSpec(shape, lambda i: (0,) * len(shape))
+
+
+def early_grads(head, first_acts, acts, dqc, dkv, patches_all, expand_weight, reduce_weight):
+    outs = (shaped(8, 224, 256), shaped(32, 32, UNITS))
+    by_head = lambda spec: pl.BlockSpec(spec.block_shape, lambda i, head: spec.index_map(i))
+    ins = [
+        blocks_of(TOK, WIDTH, at=0), blocks_of(TOK, WIDTH, at=0), blocks_of(TOK, WIDTH, at=1),
+        blocks_of(HEAD, TOK), blocks_of(2 * HEAD, SLOTS), blocks_of(SLOTS, PATCH),
+    ]
+    own = [
+        pl.BlockSpec((WIDTH, UNITS), lambda i, head: (0, head[0])),
+        pl.BlockSpec((UNITS, WIDTH), lambda i, head: (head[0], 0)),
+    ]
+    return pl.pallas_call(
+        early_kernel,
+        grid_spec=pltpu.PrefetchScalarGridSpec(
+            num_scalar_prefetch=1,
+            grid=(STEPS,),
+            in_specs=[by_head(spec) for spec in ins] + own,
+            out_specs=tuple(by_head(whole_block(*o.shape)) for o in outs),
+            scratch_shapes=[
+                pltpu.VMEM((UNITS, WIDTH), f32), pltpu.VMEM((UNITS, WIDTH), f32),
+                pltpu.VMEM((HEAD, WIDTH), f32), pltpu.VMEM((2 * HEAD, PATCH), f32),
+            ],
+        ),
+        out_shape=outs,
+        compiler_params=pltpu.CompilerParams(vmem_limit_bytes=40 * MB),
+        cost_estimate=pl.CostEstimate(flops=20 * SQUARE, bytes_accessed=20 * MB, transcendentals=0),
+        name="early_grads",
+    )(head, first_acts, acts, acts, dqc, dkv, patches_all, expand_weight, reduce_weight)
+
+
+def late_grads(dqkv, first_acts, weights_t, gains):
+    outs = (shaped(8, 96, 256), ROWS_F32)
+    return pl.pallas_call(
+        late_kernel,
+        grid=(STEPS,),
+        out_shape=outs,
+        in_specs=[blocks_of(3 * HEAD, TOK), blocks_of(TOK, WIDTH, at=1), whole_block(3 * HEAD, WIDTH), whole_block(8, WIDTH)],
+        out_specs=tuple(whole_block(*o.shape) for o in outs),
+        scratch_shapes=[pltpu.VMEM((3 * HEAD, WIDTH), f32), pltpu.VMEM((3 * HEAD, TOK), f32)],
+        compiler_params=pltpu.CompilerParams(vmem_limit_bytes=40 * MB),
+        cost_estimate=pl.CostEstimate(flops=4 * SQUARE, bytes_accessed=6 * MB, transcendentals=0),
+        name="late_grads",
+    )(dqkv, first_acts, weights_t, gains)
+
+
+def output_grads(o_t, dy1_all, oc_t, acts):
+    out = shaped(32, 32, 2 * HEAD)
+    return pl.pallas_call(
+        outputs_kernel,
+        grid=(STEPS,),
+        out_shape=out,
+        in_specs=[blocks_of(HEAD, TOK), blocks_of(TOK, WIDTH), blocks_of(HEAD, TOK), blocks_of(TOK, WIDTH, at=2)],
+        out_specs=whole_block(*out.shape),
+        scratch_shapes=[pltpu.VMEM((2 * HEAD, WIDTH), f32)],
+        compiler_params=pltpu.CompilerParams(vmem_limit_bytes=40 * MB),
+        cost_estimate=pl.CostEstimate(flops=3 * SQUARE, bytes_accessed=9 * MB, transcendentals=0),
+        name="output_grads",
+    )(o_t, dy1_all, oc_t, acts)
 
 
 def home_route():
@@ -327,20 +712,17 @@
     tokens, patches, patch_counts, camera_ids, modulation, query_weight, key_weight, value_weight, output_weight,
     cross_query, cross_key, cross_value, cross_output, expand_weight, reduce_weight, cotangent,
 ):
-    width = tokens.shape[3]
     scale = HEAD**-0.5
     item = lax.axis_index(ITEMS)
     head = lax.axis_index(ITEM)
     view = lax.axis_index(VIEW)
-    camera = lax.dynamic_index_in_dim(camera_ids, item, 0, keepdims=False)
-    gains = lax.dynamic_index_in_dim(modulation, camera, 0, keepdims=False).reshape(6, width)
+    camera = lax.dynamic_slice_in_dim(camera_ids, item, 1, 0)
     counts = lax.dynamic_index_in_dim(patch_counts, item, 0, keepdims=False)
-
-    x = tokens[0, 0].astype(f32)
-    own_patches = patches[0, 0]
+    gather = lambda block: lax.all_gather(block, ITEM, axis=0, tiled=False)
+
+    x = tokens[0, 0]
     grad_out = cotangent[0, 0]
-    patches_all = lax.all_gather(own_patches, ITEM, axis=0, tiled=False)
-    grad_out_all = lax.all_gather(grad_out, ITEM, axis=0, tiled=False)
+    patches_all = gather(patches[0, 0])
 
     live = (jnp.arange(4)[None, :] * SLOTS < counts[:, None]).reshape(BLOCKS)
     n_live = jnp.sum(live.astype(jnp.int32))
@@ -348,101 +730,64 @@
     slot = jnp.arange(BLOCKS)
     order = jnp.sum(jnp.where(rank[None, :] == slot[:, None], slot[None, :], 0), 1).astype(jnp.int32)
     n_live = n_live.reshape(1)
-
-    xh1, r1 = normed(x)
-    a1 = (xh1 * (1.0 + gains[0]) + gains[1]).astype(bf16)
-
-    def heads_of(weight, rows, rc=1, lc=0):
-        return mm(weight, rows, lc, rc).astype(bf16).reshape(HEADS, HEAD, -1)
-
-    qkv = swap(
-        jnp.concatenate([heads_of(w, a1) for w in (query_weight, key_weight, value_weight)], 1), ITEM
-    )
-    o_t, keep_self = self_forward(qkv, scale)
-    o1_t = swap(o_t, ITEM).reshape(width, TOK)
-    first_sum = x + mm(o1_t, output_weight, 0, 0)
-    xh2, r2 = normed(first_sum)
-    a2 = (xh2 * (1.0 + gains[2]) + gains[3]).astype(bf16)
-    qc = swap(heads_of(cross_query, a2), ITEM)
-
     own_columns = lambda w: lax.dynamic_slice_in_dim(w, head * HEAD, HEAD, 1)
     kv_weight = jnp.concatenate([own_columns(cross_key), own_columns(cross_value)], 1)
+    weights_t = jnp.concatenate([own_columns(w).T for w in (query_weight, key_weight, value_weight)], 0)
+
+    after = lambda value, *others: lax.optimization_barrier((value,) + others)[0]
+    sent, first_acts, gains = enter(camera, x, grad_out, modulation, query_weight, key_weight, value_weight)
+    qkv, kv_weight, weights_t, order, n_live = lax.optimization_barrier(
+        (swap(sent, ITEM), kv_weight, weights_t, order, n_live)
+    )
+    first_acts = gather(first_acts)
+    o_t, keep_self = self_forward(qkv, scale)
+    first_sum, a2, sent = middle(swap(o_t, ITEM), x, gains, output_weight, cross_query)
+    qc = swap(sent, ITEM)
     kv = mm(kv_weight, patches_all.reshape(BLOCKS * SLOTS, -1), 0, 1).astype(bf16)
     oc_t, keep_cross = cross_forward(order, n_live, qc, kv, scale)
-    oc1_t = swap(oc_t, ITEM).reshape(width, TOK)
-    second_sum = first_sum + mm(oc1_t, cross_output, 0, 0)
-    xh3, r3 = normed(second_sum)
-    a3 = (xh3 * (1.0 + gains[4]) + gains[5]).astype(bf16)
-    u_t = mm(expand_weight, a3, 0, 1)
-    h32, gelu_pull = jax.vjp(partial(jax.nn.gelu, approximate=True), u_t)
-    h_t = h32.astype(bf16)
-    layer_out = second_sum + mm(h_t, reduce_weight, 0, 0)
-
-    dh_t = mm(reduce_weight, grad_out, 1, 1).astype(bf16)
-    du_t = gelu_pull(dh_t.astype(f32))[0].astype(bf16)
-    da3 = mm(du_t, expand_weight, 0, 1)
-    back3, dg3, db3 = norm_backward(da3, xh3, r3, gains[4])
-    d_second = grad_out.astype(f32) + back3
-    dy2 = d_second.astype(bf16)
-    do_t = heads_of(cross_output, dy2, 1, 1)
-    hidden = HEADS * HEAD // 4
-    sent = jnp.concatenate([do_t, h_t.reshape(HEADS, hidden, TOK), du_t.reshape(HEADS, hidden, TOK)], 1)
-    got = swap(sent, ITEM)
-    do_c, h_all, du_all = got[:, :HEAD], got[:, HEAD : HEAD + hidden], got[:, HEAD + hidden :]
-    acts = lax.all_gather(jnp.stack([a1, a2, a3, dy2]), ITEM, axis=0, tiled=False)
-    a1_all, a2_all, a3_all, dy2_all = (acts[:, n] for n in range(4))
+    layer_out, d_second, acts, sent, dgb3 = mlp(
+        swap(oc_t, ITEM), first_sum, a2, grad_out, gains, cross_output, expand_weight, reduce_weight
+    )
+    do_c = swap(sent, ITEM)
+    acts = gather(acts)
 
     dqc, dkv = cross_backward(order, n_live, qc, do_c, keep_cross, kv, scale)
-    halves = dkv.reshape(BLOCKS, 2 * HEAD, 2, TOK).transpose(0, 2, 1, 3).reshape(BLOCKS, 4 * HEAD, TOK)
-    got = swap(jnp.concatenate([dqc, halves], 1), ITEM)
-    dqc_t = got[:, :HEAD].reshape(width, TOK)
-    dkv_t = got[:, HEAD:].reshape(HEADS, 2, 2, HEAD, TOK).transpose(2, 0, 3, 1, 4).reshape(2, width, SLOTS)
-    patches_grad = mm(dkv_t[0], cross_key, 0, 1) + mm(dkv_t[1], cross_value, 0, 1)
-    da2 = mm(dqc_t, cross_query, 0, 1)
-    back2, dg2, db2 = norm_backward(da2, xh2, r2, gains[2])
-    d_first = d_second + back2
-    dy1 = d_first.astype(bf16)
-    dy1_all = lax.all_gather(dy1, ITEM, axis=0, tiled=False)
-    do1 = swap(heads_of(output_weight, dy1, 1, 1), ITEM)
+    d_first, dy1, sent, dgb2 = returned(swap(dqc, ITEM), first_sum, d_second, gains, cross_query, output_weight)
+    do1 = swap(sent, ITEM)
+    dy1_all = gather(dy1)
+    dkv_got = swap(after(dkv, do1), ITEM)
     dqkv = self_backward(qkv, do1, keep_self, scale)
-    dqkv_t = swap(dqkv, ITEM)
-    da1 = sum(
-        mm(dqkv_t[:, n * HEAD : (n + 1) * HEAD].reshape(width, TOK), w, 0, 1)
-        for n, w in enumerate((query_weight, key_weight, value_weight))
+    col_late, dgb1 = late_grads(dqkv, first_acts, weights_t, gains)
+    dqkv, dkv_got = lax.optimization_barrier((dqkv, dkv_got))
+    patches_grad = patches_back(dkv_got, cross_key, cross_value)
+    col_early, row_early = early_grads(
+        head.reshape(1), first_acts, acts, after(dqc, dqkv), dkv, patches_all, expand_weight, reduce_weight
     )
-    back1, dg1, db1 = norm_backward(da1, xh1, r1, gains[0])
-    tokens_grad = d_first + back1
-
-    qkv_grad = over_item(dqkv, a1_all)
-    cq_grad = over_item(dqc, a2_all)
-    ckv_grad = over_item(dkv, patches_all)
-    e_grad = over_item(du_all, a3_all)
-    turned = lambda gathered, block: lax.dot_general(
-        gathered, block, (((0, 1), (0, 2)), ((), ())), preferred_element_type=f32
-    )
-    o_grad = turned(dy1_all, o_t)
-    co_grad = turned(dy2_all, oc_t)
-    r_grad = turned(grad_out_all, h_all)
-
-    camera_grad = jnp.concatenate([dg1, db1, dg2, db2, dg3, db3]).reshape(8, 4, -1).transpose(1, 0, 2)
-    camera_grad = swap(jnp.broadcast_to(camera_grad[None], (4,) + camera_grad.shape).reshape(16, 8, -1), ITEM)
-    camera_grad = jnp.sum(camera_grad, 0)
+    row_late = output_grads(after(o_t, col_early), dy1_all, oc_t, acts)
+
+    camera_grad = jnp.concatenate([dgb1[:2], dgb2[:2], dgb3[:2]], 0).reshape(8, 4, -1).transpose(1, 0, 2)
+    camera_grad = camera_grad.reshape(4, -1, TOK)
+    lines = camera_grad.shape[1]
     high = camera_grad.astype(bf16)
     low = (camera_grad - high.astype(f32)).astype(bf16)
-    camera_rows = jnp.pad(jnp.stack([high, low], 1), ((0, 0), (0, 14), (0, 256 - camera_grad.shape[1])))
-
-    pieces = [qkv_grad[n * HEAD : (n + 1) * HEAD] for n in range(3)]
-    pieces += [cq_grad, ckv_grad[:HEAD], ckv_grad[HEAD:], e_grad]
-    pieces = [column_pieces(piece) for piece in pieces]
-    columns = sum(piece.shape[1] for piece in pieces)
-    got = swap(jnp.concatenate(pieces + [camera_rows], 1), ITEMS).astype(f32)
+    camera_grad = jnp.concatenate([high, low, jnp.zeros((4, 32 - 2 * lines, TOK), bf16)], 1)
+    camera_grad = jnp.broadcast_to(camera_grad[None], (4,) + camera_grad.shape).reshape(BLOCKS, 32, TOK)
+    got = swap(jnp.concatenate([dqkv, camera_grad], 1), ITEM)
+    tokens_grad = leave(got, x, d_first, gains, query_weight, key_weight, value_weight)
+    camera_sum = jnp.sum(got[:, 3 * HEAD :].astype(f32), 0)
+    camera_sum = (camera_sum[:lines] + camera_sum[lines : 2 * lines]).reshape(8, -1)
+    high = camera_sum.astype(bf16)
+    low = (camera_sum - high.astype(f32)).astype(bf16)
+    camera_rows = jnp.pad(jnp.stack([high, low], 1), ((0, 0), (0, 14), (0, 256 - camera_sum.shape[1])))
+
+    columns = col_late.shape[1] + col_early.shape[1]
+    got = swap(jnp.concatenate([col_late, col_early, camera_rows], 1), ITEMS).astype(f32)
     from_items = got[:, columns] + got[:, columns + 1]
     hits = camera_ids[None, :] == (view * 4 + jnp.arange(4))[:, None]
     modulation_grad = jnp.sum(jnp.where(hits[:, :, None], from_items[None], 0.0), 1)[:, :192]
     summed = lax.ppermute(jnp.sum(got[:, :columns], 0), AXES, home_route())
 
-    row_grads = jnp.concatenate([o_grad, co_grad, r_grad], 1).astype(bf16).reshape(32, 32, -1)
-    got = swap(row_grads, ROW).astype(f32)
+    got = swap(after(jnp.concatenate([row_early, row_late], 2), got), ROW).astype(f32)
     row_sums = jnp.sum(got.reshape((8, 4) + got.shape[1:]), 0)
     rows_of = lambda lo, hi: row_sums[:, :, lo:hi].transpose(0, 2, 1).reshape(4 * (hi - lo), 32)
 
@@ -456,13 +801,13 @@
         column_outs[0],
         column_outs[1],
         column_outs[2],
-        rows_of(0, HEAD),
+        rows_of(UNITS, UNITS + HEAD),
         column_outs[3],
         column_outs[4][:192],
         column_outs[5][:192],
-        rows_of(HEAD, 2 * HEAD),
+        rows_of(UNITS + HEAD, UNITS + 2 * HEAD),
         summed[6 * half :].T,
-        rows_of(2 * HEAD, 2 * HEAD + hidden),
+        rows_of(0, UNITS),
     )
 
 

time: 513 us -> 354 us (0.69)
  waiting for transfers between devices: 129 us -> 51.6 us
  matrix products: 77.7 us -> 6.05 us
  Pallas kernels: 62.5 us -> 103 us
  other arithmetic: 26.8 us -> 12.2 us
  starting transfers between devices: 64.9 us -> 52.2 us
  blocking collectives: 59.2 us -> 49.1 us
  local copies, waits for them, and re-layouts: 67.3 us -> 60.7 us
    all_gather x4, waiting for transfers between devices: 71 us -> 12.7 us  [on_device(): gather = lambda block: lax.all_gather(block, ITEM, axis=0, tiled=False)]
    pallas_call x0 -> x9, Pallas kernels: none -> 45.9 us  [the longest x1 14.7 us: mlp(): pl.pallas_call(mlp_kernel, grid=(steps,), out_shape=outs, in_specs=[whole...]
    dot_general x19 -> x1, matrix products: 50.6 us -> 6.05 us  [mm(): lax.dot_general(left, right, (((lc,), (rc,)), ((), ())), preferred_elemen...]
    unnamed x120 -> x126, local copies, waits for them, and re-layouts: 14.9 us -> 51.3 us
    dot_general x7 -> x0, matrix products: 27.2 us -> none  [the longest x4 16.1 us: over_item(): lax.dot_general(turned, gathered, (((0, 2), (0, 1)), ((), ())), preferred...]
    reshape x17 -> x4, local copies, waits for them, and re-layouts: 15.1 us -> 0.25 us  [the longest x2 0.1 us: on_device(): jnp.concatenate([dgb1[:2], dgb2[:2], dgb3[:2]], 0).reshape(8, 4, -1)]
    all_to_all x9 -> x7, starting transfers between devices: 61.2 us -> 46.7 us  [swap(): return lax.all_to_all(block, axes, 0, 0, tiled=True)]
    dot_general x3 -> x0, local copies, waits for them, and re-layouts: 12.7 us -> none  [on_device(): lax.dot_general(gathered, block, (((0, 1), (0, 2)), ((), ())), preferred_...]
  transfers between devices with their start and end apart: 14 -> 12, of which waited for: 10 -> 8; matrix products, arithmetic and copies ran while one was open for 25% -> 7% of each run, Pallas kernels for 9% -> 29%
where the time goes in v2:
time: 354 us; the launch traced here: 349 us
  Pallas kernels  103 us (29%)
  local copies, waits for them, and re-layouts  60.7 us (17%)
  starting transfers between devices  52.2 us (15%)
  waiting for transfers between devices  51.6 us (15%)
  blocking collectives  49.1 us (14%)
  between operations  14.2 us (4%)
  other arithmetic  12.2 us (3%)
  matrix products  6.05 us (2%)
    unnamed x126, local copies, waits for them, and re-layouts  51.3 us
    all_to_all x4, blocking collectives, swap(): return lax.all_to_all(block, axes, 0, 0, tiled=True)  49.1 us
    all_to_all x7, starting transfers between devices, swap(): return lax.all_to_all(block, axes, 0, 0, tiled=True)  46.7 us
    all_to_all x7, waiting for transfers between devices, swap(): return lax.all_to_all(block, axes, 0, 0, tiled=True)  30.1 us
    pallas_call x1, Pallas kernels, cross_backward(): pl.pallas_call(partial(cross_backward_kernel, scale=scale, step=2), out_s...  20.5 us
    pallas_call x1, Pallas kernels, cross_forward(): pl.pallas_call(partial(cross_forward_kernel, scale=scale, step=2), out_sh...  15.8 us
    pallas_call x1, Pallas kernels, mlp(): pl.pallas_call(mlp_kernel, grid=(steps,), out_shape=outs, in_specs=[whole...  14.7 us
    all_gather x4, waiting for transfers between devices, on_device(): gather = lambda block: lax.all_gather(block, ITEM, axis=0, tiled=False)  12.7 us
  transfers between devices with their start and end apart: 12, of which 8 were waited for; matrix products, arithmetic and copies ran while one was open for 7% of the time, Pallas kernels for 29%

profile of v2, /device:TPU:25, one launch (start us, length us, event | category | flops | bytes accessed | tf_op | source)
XLA Modules:
  0.0 348.9 jit_solution(7034847872531966107)
XLA Ops:
  9.2 1.6 copy-done.5
  10.8 1.6 copy-done.7
  12.4 1.6 copy-done.9
  16.9 3.2 enter.1
  21.0 6.5 %all-to-all-start = ((bf16[16,192,128]{2,1,0:T(8,128)(2,1)}), bf16[16,192,128]{2,1,0:T(8,128)(2,1)S(1)}, u32[]{:S(2)}, u32[]{:S(2)}) async-start(bf16[16,192,128]{2,1,0:T(8,128)(2,1)} %copy-done.39), calls=%async_computation | async-start | bytes 1572864 | tf_op jit(solution)/shard_map/all_to_all | solution.py:39
  27.5 1.2 constant_dynamic-slice_fusion
  35.4 1.8 pad_maximum_fusion.3.wt_ref
  37.3 3.8 %all-to-all-done.qkv_ref = bf16[16,192,128]{2,1,0:T(8,128)(2,1)S(1)} async-done(((bf16[16,192,128]{2,1,0:T(8,128)(2,1)}), bf16[16,192,128]{2,1,0:T(8,128)(2,1)S(1)}, u32[]{:S(2)}, u32[]{:S(2)}) %all-to-all-start) | async-done | bytes 786464 | tf_op jit(solution)/shard_map/all_to_all | solution.py:39
  41.0 9.3 %self_forward.1 = (bf16[16,64,128]{2,1,0:T(8,128)(2,1)S(1)}, f32[16,72,128]{2,1,0:T(8,128)S(1)}) custom-call(bf16[16,192,128]{2,1,0:T(8,128)(2,1)S(1)} %all-to-all-done.qkv_ref), custom_call_target="tpu_custom_call" | custom-call | flops 4294967296 | bytes 4194304 | tf_op jit(solution)/shard_map/self_forward/pallas_call | solution.py:223
  51.2 13.4 %all_to_all.55.o_ref = bf16[16,64,128]{2,1,0:T(8,128)(2,1)S(1)} all-to-all(bf16[16,64,128]{2,1,0:T(8,128)(2,1)S(1)} %get-tuple-element.83.o_ref), channel_id=1, replica_groups=mesh['yh'=2,'c'=2,'x'=4,'zh'=2,'zl'=2,'yl'=2] {'yh','c','zl','yl'}, dimensions={0} | all-to-all | bytes 524288 | tf_op jit(solution)/shard_map/all_to_all | solution.py:39
  64.7 1.6 middle.1
  67.0 6.7 %all-to-all-start.2 = ((bf16[16,64,128]{2,1,0:T(8,128)(2,1)}), bf16[16,64,128]{2,1,0:T(8,128)(2,1)}, u32[]{:S(2)}, u32[]{:S(2)}) async-start(bf16[16,64,128]{2,1,0:T(8,128)(2,1)} %copy-done.54), calls=%async_computation.2 | async-start | bytes 524288 | tf_op jit(solution)/shard_map/all_to_all | solution.py:39
  74.5 6.1 %convolution_convert_fusion.kv_ref = bf16[128,4096]{1,0:T(8,128)(2,1)} fusion(bf16[768,128]{1,0:T(8,128)(2,1)} %pad_maximum_fusion.4, bf16[4096,768]{1,0:T(8,128)(2,1)} %bitcast.57), kind=kOutput, calls=%fused_computation | convolution fusion | flops 805830656 | bytes 7536640 | tf_op jit(solution)/shard_map/dot_general | solution.py:35
  80.6 1.3 copy-done.34
  81.9 15.8 %cross_forward.1 = (bf16[16,64,128]{2,1,0:T(8,128)(2,1)S(1)}, f32[16,72,128]{2,1,0:T(8,128)S(1)}) custom-call(s32[16]{0:T(128)S(1)} %select_reduce_fusion.1.order_ref, s32[1]{0:T(128)} %bitcast.5.live_ref, bf16[16,64,128]{2,1,0:T(8,128)(2,1)} %all-to-all-done.2.q_ref, bf16[128,4096]{1,0:T(8,128)(2,1)S(1)} %copy-done.34), custom_call_target="tpu_custom_call" | custom-call | flops 6979321856 | bytes 4194304 | tf_op jit(solution)/shard_map/cross_forward/pallas_call | solution.py:257
  98.5 11.9 %all_to_all.56.oc_ref = bf16[16,64,128]{2,1,0:T(8,128)(2,1)S(1)} all-to-all(bf16[16,64,128]{2,1,0:T(8,128)(2,1)S(1)} %get-tuple-element.58.oc_ref), channel_id=1, replica_groups=mesh['yh'=2,'c'=2,'x'=4,'zh'=2,'zl'=2,'yl'=2] {'yh','c','zl','yl'}, dimensions={0} | all-to-all | bytes 524288 | tf_op jit(solution)/shard_map/all_to_all | solution.py:39
  110.4 3.5 %copy-done.2 = bf16[1024,4096]{1,0:T(8,128)(2,1)S(1)} copy-done((bf16[1024,4096]{1,0:T(8,128)(2,1)S(1)}, bf16[1024,4096]{1,0:T(8,128)(2,1)}, u32[]{:S(2)}) %copy-start.2) | copy-done | bytes 8388632
  113.9 14.7 %mlp.1 = (f32[128,1024]{1,0:T(8,128)}, f32[128,1024]{1,0:T(8,128)S(1)}, bf16[3,128,1024]{2,1,0:T(8,128)(2,1)S(1)}, bf16[16,64,128]{2,1,0:T(8,128)(2,1)S(1)}, f32[8,1024]{1,0:T(8,128)S(1)}) custom-call(bf16[16,64,128]{2,1,0:T(8,128)(2,1)S(1)} %all_to_all.56.oc_ref, f32[128,1024]{1,0:T(8,128)S(1)} %get-tuple-element.59.first_ref, ...), custom_call_target="tpu_custom_call" | custom-call | flops 4831838208 | bytes 23068672 | tf_op jit(solution)/shard_map/mlp/pallas_call | solution.py:587
  131.1 11.8 %all_to_all.57.do_ref = bf16[16,64,128]{2,1,0:T(8,128)(2,1)S(1)} all-to-all(bf16[16,64,128]{2,1,0:T(8,128)(2,1)} %copy-done.53), channel_id=1, replica_groups=mesh['yh'=2,'c'=2,'x'=4,'zh'=2,'zl'=2,'yl'=2] {'yh','c','zl','yl'}, dimensions={0} | all-to-all | bytes 524288 | tf_op jit(solution)/shard_map/all_to_all | solution.py:39
  145.2 20.5 %cross_backward.1 = (bf16[16,64,128]{2,1,0:T(8,128)(2,1)S(1)}, bf16[16,128,256]{2,1,0:T(8,128)(2,1)}) custom-call(s32[16]{0:T(128)S(1)} %select_reduce_fusion.1.order_ref, s32[1]{0:T(128)} %bitcast.5.live_ref, bf16[16,64,128]{2,1,0:T(8,128)(2,1)} %all-to-all-done.2.q_ref, bf16[16,64,128]{2,1,0:T(8,128)(2,1)S(1)} %all_to_all.57.do_ref, ...), custom_call_target="tpu_custom_call" | custom-call | flops 17448304640 | bytes 4194304 | tf_op jit(solution)/shard_map/cross_backward/pallas_call | solution.py:271
  165.7 11.9 %all_to_all.58.dq_ref = bf16[16,64,128]{2,1,0:T(8,128)(2,1)S(1)} all-to-all(bf16[16,64,128]{2,1,0:T(8,128)(2,1)S(1)} %get-tuple-element.80.dqc_ref), channel_id=1, replica_groups=mesh['yh'=2,'c'=2,'x'=4,'zh'=2,'zl'=2,'yl'=2] {'yh','c','zl','yl'}, dimensions={0} | all-to-all | bytes 524288 | tf_op jit(solution)/shard_map/all_to_all | solution.py:39
  178.3 2.5 returned.1
  183.1 6.4 %all-to-all-start.6 = ((bf16[16,64,128]{2,1,0:T(8,128)(2,1)}), bf16[16,64,128]{2,1,0:T(8,128)(2,1)S(1)}, u32[]{:S(2)}, u32[]{:S(2)}) async-start(bf16[16,64,128]{2,1,0:T(8,128)(2,1)} %copy-done.50), calls=%async_computation.6 | async-start | bytes 524288 | tf_op jit(solution)/shard_map/all_to_all | solution.py:39
  189.5 6.5 %all-to-all-done.6.do_ref = bf16[16,64,128]{2,1,0:T(8,128)(2,1)S(1)} async-done(((bf16[16,64,128]{2,1,0:T(8,128)(2,1)}), bf16[16,64,128]{2,1,0:T(8,128)(2,1)S(1)}, u32[]{:S(2)}, u32[]{:S(2)}) %all-to-all-start.6) | async-done | bytes 262176 | tf_op jit(solution)/shard_map/all_to_all | solution.py:39
  196.7 6.5 %all-to-all-start.7 = ((bf16[16,128,256]{2,1,0:T(8,128)(2,1)}), bf16[16,128,256]{2,1,0:T(8,128)(2,1)S(1)}, u32[]{:S(2)}, u32[]{:S(2)}) async-start(bf16[16,128,256]{2,1,0:T(8,128)(2,1)} %get-tuple-element.69.dkv_ref), calls=%async_computation.7 | async-start | bytes 2097152 | tf_op jit(solution)/shard_map/all_to_all | solution.py:39
  206.4 11.3 %self_backward.1.dqkv_ref = bf16[16,192,128]{2,1,0:T(8,128)(2,1)S(1)} custom-call(bf16[16,192,128]{2,1,0:T(8,128)(2,1)S(1)} %copy-done.37, bf16[16,64,128]{2,1,0:T(8,128)(2,1)S(1)} %copy-done.52, f32[16,72,128]{2,1,0:T(8,128)S(1)} %copy-done.56), custom_call_target="tpu_custom_call" | custom-call | flops 10737418240 | bytes 4194304 | tf_op jit(solution)/shard_map/self_backward/pallas_call | solution.py:237
  218.6 2.0 all-to-all-done.7.got_ref
  220.6 3.8 %copy-done.3 = bf16[32,128,1024]{2,1,0:T(8,128)(2,1)S(1)} copy-done((bf16[32,128,1024]{2,1,0:T(8,128)(2,1)S(1)}, bf16[32,128,1024]{2,1,0:T(8,128)(2,1)}, u32[]{:S(2)}) %copy-start.3) | copy-done | bytes 8388632
  226.6 2.4 late_grads.1
  230.1 2.2 pad_maximum_fusion.1
  232.3 8.4 %all-to-all-start.8 = ((bf16[16,224,128]{2,1,0:T(8,128)(2,1)}), bf16[16,224,128]{2,1,0:T(8,128)(2,1)S(1)}, u32[]{:S(2)}, u32[]{:S(2)}) async-start(bf16[16,224,128]{2,1,0:T(8,128)(2,1)} %pad_maximum_fusion.1), calls=%async_computation.8 | async-start | bytes 1835008 | tf_op jit(solution)/shard_map/all_to_all | solution.py:39
  240.6 15.1 %all-to-all-done.8.got_ref = bf16[16,224,128]{2,1,0:T(8,128)(2,1)S(1)} async-done(((bf16[16,224,128]{2,1,0:T(8,128)(2,1)}), bf16[16,224,128]{2,1,0:T(8,128)(2,1)S(1)}, u32[]{:S(2)}, u32[]{:S(2)}) %all-to-all-start.8) | async-done | bytes 917536 | tf_op jit(solution)/shard_map/all_to_all | solution.py:39
  255.9 2.8 copy-done.4
  259.7 11.1 %early_grads.1 = (bf16[8,224,256]{2,1,0:T(8,128)(2,1)S(1)}, bf16[32,32,256]{2,1,0:T(8,128)(2,1)S(1)}) custom-call(s32[1]{0:T(128)} %bitcast.13.head_ref, bf16[16,2,128,1024]{3,2,1,0:T(8,128)(2,1)} %bitcast.55, bf16[16,3,128,1024]{3,2,1,0:T(8,128)(2,1)} %bitcast.65, bf16[16,3,128,1024]{3,2,1,0:T(8,128)(2,1)} %bitcast.66, bf16[16,64,128]{2,1,0:T(8,128)(2,1)S(1)} %copy-done.33, ...), custom_call_target="tpu_custom_call" | custom-call | flops 5368709120 | bytes 20971520 | tf_op jit(solution)/shard_map/early_grads/pallas_call | solution.py:650
  272.8 7.0 %all-to-all-start.9 = ((bf16[8,336,256]{2,1,0:T(8,128)(2,1)}), bf16[8,336,256]{2,1,0:T(8,128)(2,1)}, u32[]{:S(2)}, u32[]{:S(2)}) async-start(bf16[8,336,256]{2,1,0:T(8,128)(2,1)} %pad_maximum_fusion), calls=%async_computation.9 | async-start | bytes 2752512 | tf_op jit(solution)/shard_map/all_to_all | solution.py:39
  281.1 1.4 copy-done.23
  282.6 1.4 copy-done.24
  284.0 1.9 patches_back.1
  286.6 4.1 %leave.1 = f32[128,1024]{1,0:T(8,128)} custom-call(bf16[16,224,128]{2,1,0:T(8,128)(2,1)S(1)} %all-to-all-done.8.got_ref, bf16[128,1024]{1,0:T(8,128)(2,1)S(1)} %bitcast.62, f32[128,1024]{1,0:T(8,128)S(1)} %copy-done.41, f32[8,1024]{1,0:T(8,128)S(1)} %get-tuple-element.55.gains_ref, bf16[1024,1024]{1,0:T(8,128)(2,1)S(1)} %copy-done.6, ...), custom_call_target="tpu_custom_call" | custom-call | flops 805306368 | bytes 8388608 | tf_op jit(solution)/shard_map/leave/pallas_call | solution.py:614
  290.7 11.9 %all-gather.15.cloned.1.call-done = bf16[2048,1024]{1,0:T(8,128)(2,1)} async-done(((bf16[128,1024]{1,0:T(8,128)(2,1)}), bf16[2048,1024]{1,0:T(8,128)(2,1)}) %all-gather.15.cloned.1.call-update) | async-done | bytes 4194320 | tf_op jit(solution)/shard_map/all_gather | solution.py:721
  302.6 2.2 copy-done.17
  306.7 4.3 %output_grads.1 = bf16[32,32,128]{2,1,0:T(8,128)(2,1)S(1)} custom-call(bf16[16,64,128]{2,1,0:T(8,128)(2,1)S(1)} %copy-done.29, bf16[16,128,1024]{2,1,0:T(8,128)(2,1)S(1)} %bitcast.59, bf16[16,64,128]{2,1,0:T(8,128)(2,1)S(1)} %copy-done.31, bf16[16,3,128,1024]{3,2,1,0:T(8,128)(2,1)} %bitcast.67), custom_call_target="tpu_custom_call" | custom-call | flops 805306368 | bytes 9437184 | tf_op jit(solution)/shard_map/output_grads/pallas_call | solution.py:686
  312.1 1.6 convert_element_type.103
  314.6 5.4 %collective-permute-start = (f32[320,256]{1,0:T(8,128)}, f32[320,256]{1,0:T(8,128)}, u32[]{:S(2)}, u32[]{:S(2)}) collective-permute-start(f32[320,256]{1,0:T(8,128)} %slice_reduce_fusion), channel_id=1, source_target_pairs={{0,0},{1,2},{2,4},{3,6},{4,32},{5,34},{6,36},{7,38},{8,64},{9,66},... | collective-permute-start | bytes 983048 | tf_op jit(solution)/shard_map/ppermute | solution.py:788
  320.0 5.2 %all-to-all-start.10 = ((bf16[32,32,384]{2,1,0:T(8,128)(2,1)}), bf16[32,32,384]{2,1,0:T(8,128)(2,1)S(1)}, u32[]{:S(2)}, u32[]{:S(2)}) async-start(bf16[32,32,384]{2,1,0:T(8,128)(2,1)} %pad_maximum_fusion.2), calls=%async_computation.10 | async-start | bytes 1572864 | tf_op jit(solution)/shard_map/all_to_all | solution.py:39
  325.9 8.1 %collective-permute-done = f32[320,256]{1,0:T(8,128)} collective-permute-done((f32[320,256]{1,0:T(8,128)}, f32[320,256]{1,0:T(8,128)}, u32[]{:S(2)}, u32[]{:S(2)}) %collective-permute-start) | collective-permute-done | bytes 327712 | tf_op jit(solution)/shard_map/ppermute | solution.py:788
  335.7 1.5 slice_bitcast_fusion.4
  337.2 2.8 all-to-all-done.10
  (177 shorter events, 45.0 us)
Async XLA Ops:
  7.2 24.1 %copy-start = (s32[8,4]{0,1:T(4,128)S(1)}, s32[8,4]{0,1:T(4,128)}, u32[]{:S(2)}) copy-start(s32[8,4]{0,1:T(4,128)} %param.18) | copy-start | bytes 388
  7.2 67.3 %all-gather.9.cloned.1.call-start = ((), (), s32[]{:S(2)}) async-start(), calls=%async_computation.11 | async-start | bytes 6684672 | tf_op jit(solution)/shard_map/all_gather | solution.py:721
  7.9 212.7 %all-gather.11.cloned.1.call-start = ((), (), s32[]{:S(2)}) async-start(), calls=%async_computation.12 | async-start | bytes 8912896 | tf_op jit(solution)/shard_map/all_gather | solution.py:721
  9.2 1.6 copy-start.5
  10.8 1.6 copy-start.7
  12.4 1.6 copy-start.9
  21.0 9.4 %copy-start.6 = (bf16[1024,1024]{1,0:T(8,128)(2,1)S(1)}, bf16[1024,1024]{1,0:T(8,128)(2,1)}, u32[]{:S(2)}) copy-start(bf16[1024,1024]{1,0:T(8,128)(2,1)} %wq_any.3) | copy-start | bytes 6291460
  21.0 20.0 %all-to-all-start = ((bf16[16,192,128]{2,1,0:T(8,128)(2,1)}), bf16[16,192,128]{2,1,0:T(8,128)(2,1)S(1)}, u32[]{:S(2)}, u32[]{:S(2)}) async-start(bf16[16,192,128]{2,1,0:T(8,128)(2,1)} %copy-done.39), calls=%async_computation | async-start | bytes 1572864 | tf_op jit(solution)/shard_map/all_to_all | solution.py:39
  41.0 9.3 %copy-start.36 = (bf16[16,192,128]{2,1,0:T(8,128)(2,1)}, bf16[16,192,128]{2,1,0:T(8,128)(2,1)S(1)}, u32[]{:S(2)}) copy-start(bf16[16,192,128]{2,1,0:T(8,128)(2,1)S(1)} %all-to-all-done.qkv_ref) | copy-start | bytes 2359300
  41.0 23.6 %copy-start.11 = (bf16[1024,1024]{1,0:T(8,128)(2,1)S(1)}, bf16[1024,1024]{1,0:T(8,128)(2,1)}, u32[]{:S(2)}) copy-start(bf16[1024,1024]{1,0:T(8,128)(2,1)} %wo_any.3) | copy-start | bytes 6291460
  41.0 23.6 %copy-start.13 = (bf16[1024,1024]{1,0:T(8,128)(2,1)S(1)}, bf16[1024,1024]{1,0:T(8,128)(2,1)}, u32[]{:S(2)}) copy-start(bf16[1024,1024]{1,0:T(8,128)(2,1)} %wcq_any.3) | copy-start | bytes 6291460
  41.0 23.6 %copy-start.21 = (bf16[1,1,128,1024]{3,2,1,0:T(8,128)(2,1)S(1)}, bf16[1,1,128,1024]{3,2,1,0:T(8,128)(2,1)}, u32[]{:S(2)}) copy-start(bf16[1,1,128,1024]{3,2,1,0:T(8,128)(2,1)} %param.16) | copy-start | bytes 786436
  51.2 13.5 %copy-start.28 = (bf16[16,64,128]{2,1,0:T(8,128)(2,1)}, bf16[16,64,128]{2,1,0:T(8,128)(2,1)S(1)}, u32[]{:S(2)}) copy-start(bf16[16,64,128]{2,1,0:T(8,128)(2,1)S(1)} %get-tuple-element.83.o_ref) | copy-start | bytes 786436
  67.0 13.6 %all-to-all-start.2 = ((bf16[16,64,128]{2,1,0:T(8,128)(2,1)}), bf16[16,64,128]{2,1,0:T(8,128)(2,1)}, u32[]{:S(2)}, u32[]{:S(2)}) async-start(bf16[16,64,128]{2,1,0:T(8,128)(2,1)} %copy-done.54), calls=%async_computation.2 | async-start | bytes 524288 | tf_op jit(solution)/shard_map/all_to_all | solution.py:39
  73.7 182.3 %all-gather.13.cloned.1.call-start = ((), (), s32[]{:S(2)}) async-start(), calls=%async_computation.13 | async-start | bytes 13369344 | tf_op jit(solution)/shard_map/all_gather | solution.py:721
  80.6 29.8 %copy-start.27 = (bf16[1,1,128,1024]{3,2,1,0:T(8,128)(2,1)S(1)}, bf16[1,1,128,1024]{3,2,1,0:T(8,128)(2,1)}, u32[]{:S(2)}) copy-start(bf16[1,1,128,1024]{3,2,1,0:T(8,128)(2,1)} %param.31) | copy-start | bytes 786436
  80.6 1.3 copy-start.34
  81.9 28.6 %copy-start.22 = (bf16[1024,1024]{1,0:T(8,128)(2,1)S(1)}, bf16[1024,1024]{1,0:T(8,128)(2,1)}, u32[]{:S(2)}) copy-start(bf16[1024,1024]{1,0:T(8,128)(2,1)} %wco_ref.1) | copy-start | bytes 6291460
  98.5 11.9 %copy-start.30 = (bf16[16,64,128]{2,1,0:T(8,128)(2,1)}, bf16[16,64,128]{2,1,0:T(8,128)(2,1)S(1)}, u32[]{:S(2)}) copy-start(bf16[16,64,128]{2,1,0:T(8,128)(2,1)S(1)} %get-tuple-element.58.oc_ref) | copy-start | bytes 786436
  110.4 3.5 %copy-start.2 = (bf16[1024,4096]{1,0:T(8,128)(2,1)S(1)}, bf16[1024,4096]{1,0:T(8,128)(2,1)}, u32[]{:S(2)}) copy-start(bf16[1024,4096]{1,0:T(8,128)(2,1)} %we_ref.3) | copy-start | bytes 25165828
  131.1 171.6 %all-gather.15.cloned.1.call-start = ((), (), s32[]{:S(2)}) async-start(), calls=%async_computation.14 | async-start | bytes 4456448 | tf_op jit(solution)/shard_map/all_gather | solution.py:721
  142.9 1.2 copy-start.35
  145.2 33.1 %copy-start.12 = (bf16[1024,1024]{1,0:T(8,128)(2,1)S(1)}, bf16[1024,1024]{1,0:T(8,128)(2,1)}, u32[]{:S(2)}) copy-start(bf16[1024,1024]{1,0:T(8,128)(2,1)} %wo_any.3) | copy-start | bytes 6291460
  145.2 33.1 %copy-start.14 = (bf16[1024,1024]{1,0:T(8,128)(2,1)S(1)}, bf16[1024,1024]{1,0:T(8,128)(2,1)}, u32[]{:S(2)}) copy-start(bf16[1024,1024]{1,0:T(8,128)(2,1)} %wcq_any.3) | copy-start | bytes 6291460
  145.2 33.1 %copy-start.45 = (f32[128,1024]{1,0:T(8,128)S(1)}, f32[128,1024]{1,0:T(8,128)}, u32[]{:S(2)}) copy-start(f32[128,1024]{1,0:T(8,128)} %copy-done.44) | copy-start | bytes 1572868
  183.1 13.0 %all-to-all-start.6 = ((bf16[16,64,128]{2,1,0:T(8,128)(2,1)}), bf16[16,64,128]{2,1,0:T(8,128)(2,1)S(1)}, u32[]{:S(2)}, u32[]{:S(2)}) async-start(bf16[16,64,128]{2,1,0:T(8,128)(2,1)} %copy-done.50), calls=%async_computation.6 | async-start | bytes 524288 | tf_op jit(solution)/shard_map/all_to_all | solution.py:39
  196.7 23.9 %all-to-all-start.7 = ((bf16[16,128,256]{2,1,0:T(8,128)(2,1)}), bf16[16,128,256]{2,1,0:T(8,128)(2,1)S(1)}, u32[]{:S(2)}, u32[]{:S(2)}) async-start(bf16[16,128,256]{2,1,0:T(8,128)(2,1)} %get-tuple-element.69.dkv_ref), calls=%async_computation.7 | async-start | bytes 2097152 | tf_op jit(solution)/shard_map/all_to_all | solution.py:39
  203.2 1.2 copy-start.37
  205.3 1.1 copy-start.56
  220.6 8.4 %copy-start.15 = (bf16[16,128,256]{2,1,0:T(8,128)(2,1)}, bf16[16,128,256]{2,1,0:T(8,128)(2,1)S(1)}, u32[]{:S(2)}) copy-start(bf16[16,128,256]{2,1,0:T(8,128)(2,1)S(1)} %all-to-all-done.7.got_ref) | copy-start | bytes 3145732
  220.6 3.8 %copy-start.3 = (bf16[32,128,1024]{2,1,0:T(8,128)(2,1)S(1)}, bf16[32,128,1024]{2,1,0:T(8,128)(2,1)}, u32[]{:S(2)}) copy-start(bf16[32,128,1024]{2,1,0:T(8,128)(2,1)} %all-gather.11.cloned.1.call-done) | copy-start | bytes 25165828
  224.4 1.1 copy-start.19
  232.3 23.5 %all-to-all-start.8 = ((bf16[16,224,128]{2,1,0:T(8,128)(2,1)}), bf16[16,224,128]{2,1,0:T(8,128)(2,1)S(1)}, u32[]{:S(2)}, u32[]{:S(2)}) async-start(bf16[16,224,128]{2,1,0:T(8,128)(2,1)} %pad_maximum_fusion.1), calls=%async_computation.8 | async-start | bytes 1835008 | tf_op jit(solution)/shard_map/all_to_all | solution.py:39
  255.9 2.8 copy-start.4
  259.7 11.9 %copy-start.48 = (bf16[8,96,256]{2,1,0:T(8,128)(2,1)S(1)}, bf16[8,96,256]{2,1,0:T(8,128)(2,1)}, u32[]{:S(2)}) copy-start(bf16[8,96,256]{2,1,0:T(8,128)(2,1)} %copy-done.47) | copy-start | bytes 1179652
  271.6 8.2 %copy-start.59 = (s32[8]{0:T(128)S(1)}, s32[8]{0:T(128)}, u32[]{:S(2)}) copy-start(s32[8]{0:T(128)} %param.19) | copy-start | bytes 100
  272.8 39.3 %all-to-all-start.9 = ((bf16[8,336,256]{2,1,0:T(8,128)(2,1)}), bf16[8,336,256]{2,1,0:T(8,128)(2,1)}, u32[]{:S(2)}, u32[]{:S(2)}) async-start(bf16[8,336,256]{2,1,0:T(8,128)(2,1)} %pad_maximum_fusion), calls=%async_computation.9 | async-start | bytes 2752512 | tf_op jit(solution)/shard_map/all_to_all | solution.py:39
  279.9 1.2 copy-start.16
  281.1 1.4 copy-start.23
  282.6 1.4 copy-start.24
  284.0 1.9 copy-start.8
  284.0 2.5 copy-start.10
  284.0 2.6 copy-start.41
  302.6 2.2 copy-start.17
  306.7 4.4 %copy-start.43 = (bf16[32,32,256]{2,1,0:T(8,128)(2,1)S(1)}, bf16[32,32,256]{2,1,0:T(8,128)(2,1)}, u32[]{:S(2)}) copy-start(bf16[32,32,256]{2,1,0:T(8,128)(2,1)} %copy-done.42) | copy-start | bytes 1572868
  313.6 28.7 %copy-start.1 = (s32[8,4]{0,1:T(4,128)S(1)}, s32[8,4]{0,1:T(4,128)}, u32[]{:S(2)}) copy-start(s32[8,4]{0,1:T(4,128)} %param.18) | copy-start | bytes 388
  314.6 19.4 %collective-permute-start = (f32[320,256]{1,0:T(8,128)}, f32[320,256]{1,0:T(8,128)}, u32[]{:S(2)}, u32[]{:S(2)}) collective-permute-start(f32[320,256]{1,0:T(8,128)} %slice_reduce_fusion), channel_id=1, source_target_pairs={{0,0},{1,2},{2,4},{3,6},{4,32},{5,34},{6,36},{7,38},{8,64},{9,66},... | collective-permute-start | bytes 983048 | tf_op jit(solution)/shard_map/ppermute | solution.py:788
  320.0 20.0 %all-to-all-start.10 = ((bf16[32,32,384]{2,1,0:T(8,128)(2,1)}), bf16[32,32,384]{2,1,0:T(8,128)(2,1)S(1)}, u32[]{:S(2)}, u32[]{:S(2)}) async-start(bf16[32,32,384]{2,1,0:T(8,128)(2,1)} %pad_maximum_fusion.2), calls=%async_computation.10 | async-start | bytes 1572864 | tf_op jit(solution)/shard_map/all_to_all | solution.py:39
  (24 other events, 20.5 us)
Sparse Core Ops, SparseCore 0:
  9.7 64.7 all-gather.8
  76.8 60.0 all-gather.10
  138.6 92.8 all-gather.12
  233.0 69.5 all-gather.14

commit v3 on v2

--- a/solution.py
+++ b/solution.py
@@ -25,7 +25,8 @@
 ROW = ("x", "zh", "zl", "yl")
 ITEM = ("yh", "c", "zl", "yl")
 ITEMS = ("x", "zh")
-VMEM_BYTES = 32 * 1024 * 1024
+GATHER = ("zl", "yl", "yh", "c")
+VMEM_BYTES = 60 * 1024 * 1024
 
 bf16 = jnp.bfloat16
 f32 = jnp.float32
@@ -119,7 +120,7 @@
     def one(i, carry):
         at = i * step
         qts = [qkv_ref[at + n, :HEAD, :] for n in range(step)]
-        dots = [do_ref[at + n] for n in range(step)]
+        dots = [do_ref[at + n, :HEAD, :] for n in range(step)]
         keeps = [keep_ref[at + n] for n in range(step)]
         dq = backward_block(qts, dots, keeps, kt[...], k[...], vt[...], dk_acc, dv_acc, scale)
         store_blocks(out_ref, at, slice(0, HEAD), dq)
@@ -134,6 +135,10 @@
 
 def slot_block(kv_ref, index):
     return kv_ref[:, pl.ds(pl.multiple_of(index * SLOTS, SLOTS), SLOTS)]
+
+
+def own_place(index):
+    return (index % 4) * 4 + index // 4
 
 
 def cross_forward_kernel(order_ref, live_ref, q_ref, kv_ref, o_ref, keep_ref, kt, v, *, scale, step):
@@ -191,10 +196,10 @@
     lax.fori_loop(0, BLOCKS // step, one, 0)
     for t in range(LIVE_MAX):
         cols = slice(t * SLOTS, (t + 1) * SLOTS)
-        dkv_ref[order_ref[t], :HEAD, :] = dk_acc[:, cols].astype(bf16)
-        dkv_ref[order_ref[t], HEAD:, :] = dv_acc[:, cols].astype(bf16)
+        dkv_ref[own_place(order_ref[t]), :HEAD, :] = dk_acc[:, cols].astype(bf16)
+        dkv_ref[own_place(order_ref[t]), HEAD:, :] = dv_acc[:, cols].astype(bf16)
     for t in range(LIVE_MAX, BLOCKS):
-        dkv_ref[order_ref[t]] = jnp.zeros((2 * HEAD, SLOTS), bf16)
+        dkv_ref[own_place(order_ref[t])] = jnp.zeros((2 * HEAD, SLOTS), bf16)
 
 
 def params():
@@ -331,15 +336,17 @@
         store_heads(sent_ref, n * HEAD, mm(a1, w[...]))
 
 
-def middle_kernel(o_ref, x_ref, gains_ref, wo_any, wcq_any, first_ref, a2_ref, q_ref, wo, wcq, sems):
+def middle_kernel(o_ref, x_ref, gains_ref, early_ref, wo_any, wcq_any, first_ref, acts_ref, q_ref, wo, wcq, sems):
     copies = load_all(((wo_any, wo), (wcq_any, wcq)), sems)
     o1 = token_rows(o_ref, 0, HEAD)
+    acts_ref[0:2] = early_ref[...]
+    acts_ref[2] = o1
     copies[0].wait()
     first = x_ref[...].astype(f32) + mm(o1, wo[...])
     first_ref[...] = first
     xh, _ = normed(first)
     a2 = (xh * (1.0 + gains_ref[2:3, :]) + gains_ref[3:4, :]).astype(bf16)
-    a2_ref[...] = a2
+    acts_ref[3] = a2
     copies[1].wait()
     store_heads(q_ref, 0, mm(a2, wcq[...]))
 
@@ -355,7 +362,7 @@
 
 
 def mlp_kernel(
-    oc_ref, first_ref, a2_ref, cot_ref, gains_ref, wco_ref, we_ref, wr_ref,
+    oc_ref, first_ref, cot_ref, gains_ref, wco_ref, we_ref, wr_ref,
     out_ref, back_ref, acts_ref, do_ref, dgb_ref, a3, second, y, da3,
 ):
     step = pl.program_id(0)
@@ -385,13 +392,12 @@
         back = cot_ref[...].astype(f32) + norm_backward(d, xh, r, gains_ref[4:5, :])
         back_ref[...] = back
         dy2 = back.astype(bf16)
-        acts_ref[0] = a2_ref[...]
-        acts_ref[1] = a3[...]
-        acts_ref[2] = dy2
+        acts_ref[0] = a3[...]
+        acts_ref[1] = dy2
         store_heads(do_ref, 0, mm(dy2, wco_ref[...], 1, 1))
 
 
-def return_kernel(dq_ref, first_ref, second_back_ref, gains_ref, wcq_any, wo_any, back_ref, dy_ref, do_ref, dgb_ref, wcq, wo, sems):
+def return_kernel(dq_ref, first_ref, second_back_ref, gains_ref, wcq_any, wo_any, back_ref, sent_ref, dgb_ref, wcq, wo, sems):
     copies = load_all(((wcq_any, wcq), (wo_any, wo)), sems)
     xh, r = normed(first_ref[...])
     dq = token_rows(dq_ref, 0, HEAD)
@@ -403,13 +409,17 @@
     back = second_back_ref[...] + norm_backward(da2, xh, r, gains_ref[2:3, :])
     back_ref[...] = back
     dy1 = back.astype(bf16)
-    dy_ref[...] = dy1
+    store_heads(sent_ref, HEAD, back)
     copies[1].wait()
-    store_heads(do_ref, 0, mm(dy1, wo[...], 1, 1))
-
-
-def leave_kernel(got_ref, x_ref, back_ref, gains_ref, wq_any, wk_any, wv_any, out_ref, wq, wk, wv, sems):
+    store_heads(sent_ref, 0, mm(dy1, wo[...], 1, 1))
+
+
+def leave_kernel(got_ref, x_ref, back_ref, gains_ref, wq_any, wk_any, wv_any, out_ref, camera_ref, wq, wk, wv, sems):
     copies = load_all(((wq_any, wq), (wk_any, wk), (wv_any, wv)), sems)
+    lines = got_ref[0, 3 * HEAD :, :].astype(f32)
+    for n in range(1, BLOCKS):
+        lines += got_ref[n, 3 * HEAD :, :].astype(f32)
+    camera_ref[...] = lines[:16] + lines[16:]
     xh, r = normed(x_ref[...].astype(f32))
     da1 = jnp.zeros(out_ref.shape, f32)
     for n, (copy, w) in enumerate(zip(copies, (wq, wk, wv))):
@@ -443,82 +453,119 @@
             ref[e * 4 + v, at : at + columns, :] = piece.astype(bf16)
 
 
-def early_kernel(
-    head_ref, cot_ref, a2_ref, a3_ref, dqc_ref, dkv_ref, patches_ref, we_ref, wr_ref, col_ref, row_ref, e_acc, r_acc, q_acc, kv_acc
-):
+def add_up(step, accs, terms):
+    @pl.when(step == 0)
+    def _():
+        for acc, term in zip(accs, terms):
+            acc[...] = term
+
+    @pl.when(step > 0)
+    def _():
+        for acc, term in zip(accs, terms):
+            acc[...] += term
+
+
+def cross_grads_kernel(dqc_ref, a2_ref, dkv_ref, patches_ref, col_ref, q_acc, kv_acc):
     step = pl.program_id(0)
-    a3, cot = one_above_other(a3_ref), one_above_other(cot_ref)
-    h, du = gelu_both(a3, cot, we_ref[...], wr_ref[...])
-    r = mm(h.T, cot)
-    e = mm(du.T, a3)
     q = mm(side_by_side(dqc_ref, 0, HEAD), one_above_other(a2_ref))
     kv = mm(side_by_side(dkv_ref, 0, 2 * HEAD), one_above_other(patches_ref))
-
-    @pl.when(step == 0)
-    def _():
-        r_acc[...], e_acc[...], q_acc[...], kv_acc[...] = r, e, q, kv
-
-    @pl.when(step > 0)
-    def _():
-        r_acc[...] += r
-        e_acc[...] += e
-        q_acc[...] += q
-        kv_acc[...] += kv
+    add_up(step, (q_acc, kv_acc), (q, kv))
 
     @pl.when(step == pl.num_programs(0) - 1)
     def _():
         store_columns(col_ref, 0, q_acc[...])
         store_columns(col_ref, 32, kv_acc[:HEAD, :])
         store_columns(col_ref, 64, kv_acc[HEAD:, :])
-        store_columns(col_ref, 96, e_acc[...])
-        row_ref[...] = r_acc[...].T.astype(bf16).reshape(row_ref.shape)
-
-
-def late_kernel(dqkv_ref, xh_ref, wt_ref, gains_ref, col_ref, dgb_ref, qkv_acc, sums):
+
+
+def hidden_grads_kernel(
+    head_ref, cot_ref, o1_ref, a3_ref, dy2_ref, do_ref, oc_ref, we_ref, wr_ref, col_ref, row_ref, e_acc, r_acc, o_acc, oc_acc
+):
+    step = pl.program_id(0)
+    a3, cot = one_above_other(a3_ref), one_above_other(cot_ref)
+    h, du = gelu_both(a3, cot, we_ref[...], wr_ref[...])
+    e = mm(du.T, a3)
+    r = mm(h.T, cot)
+    o = mm(side_by_side(do_ref, HEAD, 2 * HEAD), one_above_other(o1_ref))
+    oc = mm(side_by_side(oc_ref, 0, HEAD), one_above_other(dy2_ref))
+    add_up(step, (e_acc, r_acc, o_acc, oc_acc), (e, r, o, oc))
+
+    @pl.when(step == pl.num_programs(0) - 1)
+    def _():
+        store_columns(col_ref, 0, o_acc[...])
+        store_columns(col_ref, 32, e_acc[...])
+        rows = jnp.concatenate([r_acc[...], oc_acc[...], jnp.zeros((HEAD, WIDTH), f32)], 0)
+        row_ref[...] = rows.T.astype(bf16).reshape(row_ref.shape)
+
+
+def late_kernel(dqkv_ref, xh_ref, wt_ref, gains_ref, dgb2_ref, dgb3_ref, col_ref, sent_ref, qkv_acc, sums):
     step = pl.program_id(0)
     turned = side_by_side(dqkv_ref, 0, 3 * HEAD)
     qkv = mm(turned, one_above_other(xh_ref))
     total = jnp.broadcast_to(jnp.sum(turned.astype(f32), 1, keepdims=True), sums.shape)
-
-    @pl.when(step == 0)
-    def _():
-        qkv_acc[...], sums[...] = qkv, total
-
-    @pl.when(step > 0)
-    def _():
-        qkv_acc[...] += qkv
-        sums[...] += total
+    add_up(step, (qkv_acc, sums), (qkv, total))
+    blocks = dqkv_ref.shape[0]
+    for n in range(blocks):
+        sent_ref[step * blocks + n, : 3 * HEAD, :] = dqkv_ref[n]
 
     @pl.when(step == pl.num_programs(0) - 1)
     def _():
         moment = qkv_acc[...]
         count = sums[:, 0:1]
         weights = wt_ref[...].astype(f32)
-        dgb_ref[...] = jnp.zeros_like(dgb_ref)
-        dgb_ref[0:1, :] = jnp.sum(weights * moment, 0, keepdims=True)
-        dgb_ref[1:2, :] = jnp.sum(weights * count, 0, keepdims=True)
         grad = moment * (1.0 + gains_ref[0:1, :]) + count * gains_ref[1:2, :]
         for n in range(3):
             store_columns(col_ref, n * 32, grad[n * HEAD : (n + 1) * HEAD])
-
-
-def outputs_kernel(o_ref, dy1_ref, oc_ref, dy2_ref, row_ref, acc):
-    step = pl.program_id(0)
-    o = mm(side_by_side(o_ref, 0, HEAD), one_above_other(dy1_ref))
-    oc = mm(side_by_side(oc_ref, 0, HEAD), one_above_other(dy2_ref))
-    both = jnp.concatenate([o, oc], 0)
-
-    @pl.when(step == 0)
-    def _():
-        acc[...] = both
-
-    @pl.when(step > 0)
-    def _():
-        acc[...] += both
-
-    @pl.when(step == pl.num_programs(0) - 1)
-    def _():
-        row_ref[...] = acc[...].T.astype(bf16).reshape(row_ref.shape)
+        dg1 = jnp.sum(weights * moment, 0, keepdims=True)
+        db1 = jnp.sum(weights * count, 0, keepdims=True)
+        flat = jnp.concatenate([dg1, db1] + [ref[n : n + 1, :] for ref in (dgb2_ref, dgb3_ref) for n in range(2)], 1)
+        chunk = flat.shape[1] // 32
+        fill = jnp.zeros((1, 2 * TOK - chunk), f32)
+        for b in range(4):
+            lines = []
+            for i in range(8):
+                at = (i * 4 + b) * chunk
+                line = jnp.concatenate([flat[:, at : at + chunk], fill], 1)
+                lines += [line[:, :TOK], line[:, TOK:]]
+            lines = jnp.concatenate(lines, 0)
+            high = lines.astype(bf16)
+            both = jnp.concatenate([high, (lines - high.astype(f32)).astype(bf16)], 0)
+            for v in range(4):
+                sent_ref[v * 4 + b, 3 * HEAD :, :] = both
+
+
+def add_items_kernel(got_ref, out_ref):
+    total = got_ref[0].astype(f32)
+    for n in range(1, 8):
+        total += got_ref[n].astype(f32)
+    out_ref[...] = total
+
+
+def finish_columns_kernel(in_ref, *out_refs):
+    at = 0
+    for ref in out_refs[:-1]:
+        columns, rows = ref.shape
+        ref[...] = in_ref[at : at + columns, :rows]
+        at += columns
+    out_refs[-1][...] = in_ref[at:, :].T
+
+
+def finish_rows_kernel(camera_ref, view_ref, got_ref, r_ref, oc_ref, modulation_ref):
+    units = r_ref.shape[1] // 4
+    for s in range(4):
+        total = got_ref[s].astype(f32)
+        for n in range(1, 8):
+            total += got_ref[n * 4 + s].astype(f32)
+        r_ref[:, s * units : (s + 1) * units] = total[:, :units]
+        oc_ref[:, s * HEAD : (s + 1) * HEAD] = total[:, units : units + HEAD]
+    rows = [jnp.zeros((16, HEAD), f32) for _ in range(4)]
+    for n in range(8):
+        part = sum(got_ref[n * 4 + s, 0:16, units + HEAD : units + 2 * HEAD].astype(f32) for s in range(4))
+        for k in range(4):
+            rows[k] += jnp.where(camera_ref[n] == view_ref[0] * 4 + k, part, 0.0)
+    for k in range(4):
+        for n in range(3):
+            modulation_ref[k : k + 1, n * HEAD : (n + 1) * HEAD] = rows[k][n : n + 1] + rows[k][n + 3 : n + 4]
 
 
 WIDTH = 1024
@@ -543,14 +590,14 @@
     return pltpu.VMEM((rows, columns), bf16)
 
 
-def call(kernel, name, ins, outs, scratch, flops, traffic, limit=40):
+def call(kernel, name, ins, outs, scratch, flops, traffic):
     return pl.pallas_call(
         kernel,
         out_shape=outs,
         in_specs=ins,
         out_specs=jax.tree.map(lambda _: V, outs),
         scratch_shapes=scratch,
-        compiler_params=pltpu.CompilerParams(vmem_limit_bytes=limit * MB),
+        compiler_params=pltpu.CompilerParams(vmem_limit_bytes=VMEM_BYTES),
         cost_estimate=pl.CostEstimate(flops=flops, bytes_accessed=traffic, transcendentals=0),
         name=name,
     )
@@ -572,7 +619,7 @@
 
 def middle(*args):
     return call(
-        middle_kernel, "middle", [V, V, V, ANY, ANY], (TOKENS_F32, TOKENS_BF16, OUT_T),
+        middle_kernel, "middle", [V, V, V, V, ANY, ANY], (TOKENS_F32, shaped(4, TOK, WIDTH), OUT_T),
         [weight(), weight(), pltpu.SemaphoreType.DMA((2,))], 2 * SQUARE, 6 * MB,
     )(*args)
 
@@ -581,7 +628,7 @@
     steps = 8
     width = HIDDEN // steps
     whole = lambda *shape: pl.BlockSpec(shape, lambda i: (0,) * len(shape))
-    outs = (TOKENS_F32, TOKENS_F32, shaped(3, TOK, WIDTH), OUT_T, ROWS_F32)
+    outs = (TOKENS_F32, TOKENS_F32, shaped(2, TOK, WIDTH), OUT_T, ROWS_F32)
     out_specs = tuple(whole(*o.shape) for o in outs)
     tokens = whole(TOK, WIDTH)
     return pl.pallas_call(
@@ -589,7 +636,7 @@
         grid=(steps,),
         out_shape=outs,
         in_specs=[
-            whole(BLOCKS, HEAD, TOK), tokens, tokens, tokens, whole(8, WIDTH), whole(WIDTH, WIDTH),
+            whole(BLOCKS, HEAD, TOK), tokens, tokens, whole(8, WIDTH), whole(WIDTH, WIDTH),
             pl.BlockSpec((WIDTH, width), lambda i: (0, i)), pl.BlockSpec((width, WIDTH), lambda i: (i, 0)),
         ],
         out_specs=out_specs,
@@ -597,7 +644,7 @@
             pltpu.VMEM((TOK, WIDTH), bf16), pltpu.VMEM((TOK, WIDTH), f32),
             pltpu.VMEM((TOK, WIDTH), f32), pltpu.VMEM((TOK, WIDTH), f32),
         ],
-        compiler_params=pltpu.CompilerParams(vmem_limit_bytes=40 * MB),
+        compiler_params=pltpu.CompilerParams(vmem_limit_bytes=VMEM_BYTES),
         cost_estimate=pl.CostEstimate(flops=18 * SQUARE, bytes_accessed=22 * MB, transcendentals=TOK * HIDDEN),
         name="mlp",
     )(*args)
@@ -605,14 +652,14 @@
 
 def returned(*args):
     return call(
-        return_kernel, "returned", [V, V, V, V, ANY, ANY], (TOKENS_F32, TOKENS_BF16, OUT_T, ROWS_F32),
+        return_kernel, "returned", [V, V, V, V, ANY, ANY], (TOKENS_F32, shaped(BLOCKS, 2 * HEAD, TOK), ROWS_F32),
         [weight(), weight(), pltpu.SemaphoreType.DMA((2,))], 2 * SQUARE, 6 * MB,
     )(*args)
 
 
 def leave(*args):
     return call(
-        leave_kernel, "leave", [V, V, V, V, ANY, ANY, ANY], TOKENS_F32,
+        leave_kernel, "leave", [V, V, V, V, ANY, ANY, ANY], (TOKENS_F32, shaped(16, TOK, dtype=f32)),
         [weight(), weight(), weight(), pltpu.SemaphoreType.DMA((3,))], 3 * SQUARE, 8 * MB,
     )(*args)
 
@@ -626,29 +673,47 @@
 STEPS = 4
 
 
-def blocks_of(*shape, at=None):
-    if at is None:
-        return pl.BlockSpec((BLOCKS // STEPS,) + shape, lambda i: (i,) + (0,) * len(shape))
-    return pl.BlockSpec((BLOCKS // STEPS, 1) + shape, lambda i: (i, at) + (0,) * len(shape))
+def blocks_of(*shape):
+    return pl.BlockSpec((BLOCKS // STEPS,) + shape, lambda i: (i,) + (0,) * len(shape))
+
+
+def gathered(*shape, at=None):
+    plane = () if at is None else (at,)
+    return pl.BlockSpec((4, 1) + (1,) * len(plane) + shape, lambda i: (0, i) + plane + (0,) * len(shape))
 
 
 def whole_block(*shape):
     return pl.BlockSpec(shape, lambda i: (0,) * len(shape))
 
 
-def early_grads(head, first_acts, acts, dqc, dkv, patches_all, expand_weight, reduce_weight):
-    outs = (shaped(8, 224, 256), shaped(32, 32, UNITS))
+def cross_grads(dqc, acts, dkv, patches_all):
+    out = shaped(8, 96, 256)
+    return pl.pallas_call(
+        cross_grads_kernel,
+        grid=(STEPS,),
+        out_shape=out,
+        in_specs=[blocks_of(HEAD, TOK), gathered(TOK, WIDTH, at=3), blocks_of(2 * HEAD, SLOTS), gathered(SLOTS, PATCH)],
+        out_specs=whole_block(*out.shape),
+        scratch_shapes=[pltpu.VMEM((HEAD, WIDTH), f32), pltpu.VMEM((2 * HEAD, PATCH), f32)],
+        compiler_params=pltpu.CompilerParams(vmem_limit_bytes=VMEM_BYTES),
+        cost_estimate=pl.CostEstimate(flops=6 * SQUARE, bytes_accessed=12 * MB, transcendentals=0),
+        name="cross_grads",
+    )(dqc, acts, dkv, patches_all)
+
+
+def hidden_grads(head, acts, late_acts, do1, oc_t, expand_weight, reduce_weight):
+    outs = (shaped(8, 160, 256), shaped(32, 32, UNITS + 2 * HEAD))
     by_head = lambda spec: pl.BlockSpec(spec.block_shape, lambda i, head: spec.index_map(i))
     ins = [
-        blocks_of(TOK, WIDTH, at=0), blocks_of(TOK, WIDTH, at=0), blocks_of(TOK, WIDTH, at=1),
-        blocks_of(HEAD, TOK), blocks_of(2 * HEAD, SLOTS), blocks_of(SLOTS, PATCH),
+        gathered(TOK, WIDTH, at=0), gathered(TOK, WIDTH, at=2), gathered(TOK, WIDTH, at=0),
+        gathered(TOK, WIDTH, at=1), blocks_of(2 * HEAD, TOK), blocks_of(HEAD, TOK),
     ]
     own = [
         pl.BlockSpec((WIDTH, UNITS), lambda i, head: (0, head[0])),
         pl.BlockSpec((UNITS, WIDTH), lambda i, head: (head[0], 0)),
     ]
     return pl.pallas_call(
-        early_kernel,
+        hidden_grads_kernel,
         grid_spec=pltpu.PrefetchScalarGridSpec(
             num_scalar_prefetch=1,
             grid=(STEPS,),
@@ -656,44 +721,45 @@
             out_specs=tuple(by_head(whole_block(*o.shape)) for o in outs),
             scratch_shapes=[
                 pltpu.VMEM((UNITS, WIDTH), f32), pltpu.VMEM((UNITS, WIDTH), f32),
-                pltpu.VMEM((HEAD, WIDTH), f32), pltpu.VMEM((2 * HEAD, PATCH), f32),
+                pltpu.VMEM((HEAD, WIDTH), f32), pltpu.VMEM((HEAD, WIDTH), f32),
             ],
         ),
         out_shape=outs,
-        compiler_params=pltpu.CompilerParams(vmem_limit_bytes=40 * MB),
+        compiler_params=pltpu.CompilerParams(vmem_limit_bytes=VMEM_BYTES),
         cost_estimate=pl.CostEstimate(flops=20 * SQUARE, bytes_accessed=20 * MB, transcendentals=0),
-        name="early_grads",
-    )(head, first_acts, acts, acts, dqc, dkv, patches_all, expand_weight, reduce_weight)
-
-
-def late_grads(dqkv, first_acts, weights_t, gains):
-    outs = (shaped(8, 96, 256), ROWS_F32)
+        name="hidden_grads",
+    )(head, acts, acts, late_acts, late_acts, do1, oc_t, expand_weight, reduce_weight)
+
+
+def late_grads(dqkv, acts, weights_t, gains, dgb2, dgb3):
+    outs = (shaped(8, 96, 256), shaped(BLOCKS, 3 * HEAD + 32, TOK))
     return pl.pallas_call(
         late_kernel,
         grid=(STEPS,),
         out_shape=outs,
-        in_specs=[blocks_of(3 * HEAD, TOK), blocks_of(TOK, WIDTH, at=1), whole_block(3 * HEAD, WIDTH), whole_block(8, WIDTH)],
+        in_specs=[blocks_of(3 * HEAD, TOK), gathered(TOK, WIDTH, at=1), whole_block(3 * HEAD, WIDTH)]
+        + [whole_block(8, WIDTH)] * 3,
         out_specs=tuple(whole_block(*o.shape) for o in outs),
         scratch_shapes=[pltpu.VMEM((3 * HEAD, WIDTH), f32), pltpu.VMEM((3 * HEAD, TOK), f32)],
-        compiler_params=pltpu.CompilerParams(vmem_limit_bytes=40 * MB),
+        compiler_params=pltpu.CompilerParams(vmem_limit_bytes=VMEM_BYTES),
         cost_estimate=pl.CostEstimate(flops=4 * SQUARE, bytes_accessed=6 * MB, transcendentals=0),
         name="late_grads",
-    )(dqkv, first_acts, weights_t, gains)
-
-
-def output_grads(o_t, dy1_all, oc_t, acts):
-    out = shaped(32, 32, 2 * HEAD)
-    return pl.pallas_call(
-        outputs_kernel,
-        grid=(STEPS,),
-        out_shape=out,
-        in_specs=[blocks_of(HEAD, TOK), blocks_of(TOK, WIDTH), blocks_of(HEAD, TOK), blocks_of(TOK, WIDTH, at=2)],
-        out_specs=whole_block(*out.shape),
-        scratch_shapes=[pltpu.VMEM((2 * HEAD, WIDTH), f32)],
-        compiler_params=pltpu.CompilerParams(vmem_limit_bytes=40 * MB),
-        cost_estimate=pl.CostEstimate(flops=3 * SQUARE, bytes_accessed=9 * MB, transcendentals=0),
-        name="output_grads",
-    )(o_t, dy1_all, oc_t, acts)
+    )(dqkv, acts, weights_t, gains, dgb2, dgb3)
+
+
+def add_items(got):
+    return call(add_items_kernel, "add_items", [V], shaped(*got.shape[1:], dtype=f32), [], MB, 2 * MB)(got)
+
+
+def finish_columns(summed):
+    small = [(32, 256)] * 4 + [(32, 192)] * 2 + [(32, 256), (256, 128)]
+    outs = tuple(shaped(*shape, dtype=f32) for shape in small)
+    return call(finish_columns_kernel, "finish_columns", [V], outs, [], MB, MB)(summed)
+
+
+def finish_rows(camera_ids, view, got):
+    outs = (shaped(32, HIDDEN // 4, dtype=f32), shaped(32, 256, dtype=f32), shaped(4, 192, dtype=f32))
+    return call(finish_rows_kernel, "finish_rows", [S, S, V], outs, [], MB, 2 * MB)(camera_ids, view, got)
 
 
 def home_route():
@@ -718,13 +784,13 @@
     view = lax.axis_index(VIEW)
     camera = lax.dynamic_slice_in_dim(camera_ids, item, 1, 0)
     counts = lax.dynamic_index_in_dim(patch_counts, item, 0, keepdims=False)
-    gather = lambda block: lax.all_gather(block, ITEM, axis=0, tiled=False)
+    gather = lambda block: lax.all_gather(block, GATHER, axis=0, tiled=False).reshape((4, 4) + block.shape)
 
     x = tokens[0, 0]
     grad_out = cotangent[0, 0]
     patches_all = gather(patches[0, 0])
 
-    live = (jnp.arange(4)[None, :] * SLOTS < counts[:, None]).reshape(BLOCKS)
+    live = (jnp.arange(4)[:, None] * SLOTS < counts[None, :]).reshape(BLOCKS)
     n_live = jnp.sum(live.astype(jnp.int32))
     rank = jnp.where(live, jnp.cumsum(live) - 1, n_live + jnp.cumsum(~live) - 1)
     slot = jnp.arange(BLOCKS)
@@ -739,75 +805,61 @@
     qkv, kv_weight, weights_t, order, n_live = lax.optimization_barrier(
         (swap(sent, ITEM), kv_weight, weights_t, order, n_live)
     )
-    first_acts = gather(first_acts)
     o_t, keep_self = self_forward(qkv, scale)
-    first_sum, a2, sent = middle(swap(o_t, ITEM), x, gains, output_weight, cross_query)
+    first_sum, acts, sent = middle(swap(o_t, ITEM), x, gains, first_acts, output_weight, cross_query)
     qc = swap(sent, ITEM)
+    acts = gather(acts)
     kv = mm(kv_weight, patches_all.reshape(BLOCKS * SLOTS, -1), 0, 1).astype(bf16)
     oc_t, keep_cross = cross_forward(order, n_live, qc, kv, scale)
-    layer_out, d_second, acts, sent, dgb3 = mlp(
-        swap(oc_t, ITEM), first_sum, a2, grad_out, gains, cross_output, expand_weight, reduce_weight
+    layer_out, d_second, late_acts, sent, dgb3 = mlp(
+        swap(oc_t, ITEM), first_sum, grad_out, gains, cross_output, expand_weight, reduce_weight
     )
     do_c = swap(sent, ITEM)
-    acts = gather(acts)
-
+    late_acts = gather(late_acts)
     dqc, dkv = cross_backward(order, n_live, qc, do_c, keep_cross, kv, scale)
-    d_first, dy1, sent, dgb2 = returned(swap(dqc, ITEM), first_sum, d_second, gains, cross_query, output_weight)
-    do1 = swap(sent, ITEM)
-    dy1_all = gather(dy1)
+    d_first, sent, dgb2 = returned(swap(dqc, ITEM), first_sum, d_second, gains, cross_query, output_weight)
+    do1, col_cross = lax.optimization_barrier((swap(sent, ITEM), cross_grads(dqc, acts, dkv, patches_all)))
     dkv_got = swap(after(dkv, do1), ITEM)
     dqkv = self_backward(qkv, do1, keep_self, scale)
-    col_late, dgb1 = late_grads(dqkv, first_acts, weights_t, gains)
-    dqkv, dkv_got = lax.optimization_barrier((dqkv, dkv_got))
+    col_late, sent = late_grads(dqkv, acts, weights_t, gains, dgb2, dgb3)
+    sent, dkv_got = lax.optimization_barrier((sent, dkv_got))
+    col_hidden, row = hidden_grads(
+        head.reshape(1), acts, late_acts, after(do1, sent), oc_t, expand_weight, reduce_weight
+    )
+    got, col_hidden, row = lax.optimization_barrier((swap(sent, ITEM), col_hidden, row))
+    columns = swap(jnp.concatenate([col_late, col_cross, col_hidden], 1), ITEMS)
+    tokens_grad, camera_sum = leave(got, x, d_first, gains, query_weight, key_weight, value_weight)
     patches_grad = patches_back(dkv_got, cross_key, cross_value)
-    col_early, row_early = early_grads(
-        head.reshape(1), first_acts, acts, after(dqc, dqkv), dkv, patches_all, expand_weight, reduce_weight
-    )
-    row_late = output_grads(after(o_t, col_early), dy1_all, oc_t, acts)
-
-    camera_grad = jnp.concatenate([dgb1[:2], dgb2[:2], dgb3[:2]], 0).reshape(8, 4, -1).transpose(1, 0, 2)
-    camera_grad = camera_grad.reshape(4, -1, TOK)
-    lines = camera_grad.shape[1]
-    high = camera_grad.astype(bf16)
-    low = (camera_grad - high.astype(f32)).astype(bf16)
-    camera_grad = jnp.concatenate([high, low, jnp.zeros((4, 32 - 2 * lines, TOK), bf16)], 1)
-    camera_grad = jnp.broadcast_to(camera_grad[None], (4,) + camera_grad.shape).reshape(BLOCKS, 32, TOK)
-    got = swap(jnp.concatenate([dqkv, camera_grad], 1), ITEM)
-    tokens_grad = leave(got, x, d_first, gains, query_weight, key_weight, value_weight)
-    camera_sum = jnp.sum(got[:, 3 * HEAD :].astype(f32), 0)
-    camera_sum = (camera_sum[:lines] + camera_sum[lines : 2 * lines]).reshape(8, -1)
+
+    camera_sum = camera_sum.reshape(8, -1)[:, : 3 * HEAD]
     high = camera_sum.astype(bf16)
     low = (camera_sum - high.astype(f32)).astype(bf16)
-    camera_rows = jnp.pad(jnp.stack([high, low], 1), ((0, 0), (0, 14), (0, 256 - camera_sum.shape[1])))
-
-    columns = col_late.shape[1] + col_early.shape[1]
-    got = swap(jnp.concatenate([col_late, col_early, camera_rows], 1), ITEMS).astype(f32)
-    from_items = got[:, columns] + got[:, columns + 1]
-    hits = camera_ids[None, :] == (view * 4 + jnp.arange(4))[:, None]
-    modulation_grad = jnp.sum(jnp.where(hits[:, :, None], from_items[None], 0.0), 1)[:, :192]
-    summed = lax.ppermute(jnp.sum(got[:, :columns], 0), AXES, home_route())
-
-    got = swap(after(jnp.concatenate([row_early, row_late], 2), got), ROW).astype(f32)
-    row_sums = jnp.sum(got.reshape((8, 4) + got.shape[1:]), 0)
-    rows_of = lambda lo, hi: row_sums[:, :, lo:hi].transpose(0, 2, 1).reshape(4 * (hi - lo), 32)
-
-    half = HEAD // 2
-    column_outs = [summed[n * half : (n + 1) * half].T for n in range(6)]
+    lines = jnp.concatenate([high.reshape(8, 3, HEAD), low.reshape(8, 3, HEAD)], 1)
+    mine = jnp.arange(4) == lax.axis_index(("zl", "yl"))
+    lines = jnp.where(mine[None, :, None, None], lines[:, None], 0).astype(bf16).reshape(32, 6, HEAD)
+    row = row + jnp.pad(lines, ((0, 0), (0, 26), (UNITS + HEAD, 0)))
+
+    columns, row = lax.optimization_barrier((columns, row))
+    rows = swap(row, ROW)
+    summed = lax.ppermute(add_items(columns), AXES, home_route())
+    *turned, e_grad = finish_columns(summed)
+    q_grad, k_grad, v_grad, cq_grad, ck_grad, cv_grad, o_grad = (grad.T for grad in turned)
+    r_grad, co_grad, modulation_grad = finish_rows(camera_ids, view.reshape(1), rows)
     return (
         layer_out[None, None],
         tokens_grad[None, None],
         patches_grad[None, None],
         modulation_grad,
-        column_outs[0],
-        column_outs[1],
-        column_outs[2],
-        rows_of(UNITS, UNITS + HEAD),
-        column_outs[3],
-        column_outs[4][:192],
-        column_outs[5][:192],
-        rows_of(UNITS + HEAD, UNITS + 2 * HEAD),
-        summed[6 * half :].T,
-        rows_of(0, UNITS),
+        q_grad,
+        k_grad,
+        v_grad,
+        o_grad,
+        cq_grad,
+        ck_grad,
+        cv_grad,
+        co_grad.T,
+        e_grad,
+        r_grad.T,
     )
 
 

time: 354 us -> 331 us (0.935)
  local copies, waits for them, and re-layouts: 60.7 us -> 9.84 us
  Pallas kernels: 103 us -> 139 us
  waiting for transfers between devices: 51.6 us -> 42.3 us
  blocking collectives: 49.1 us -> 56.3 us
  other arithmetic: 12.2 us -> 6.84 us
    unnamed x126 -> x29, local copies, waits for them, and re-layouts: 51.3 us -> 3.67 us
    pallas_call x5 -> x8, Pallas kernels: 23.7 us -> 43.4 us  [the longest x1 12.9 us: hidden_grads(): pl.pallas_call(hidden_grads_kernel, grid_spec=pltpu.PrefetchScalarGridSpe...]
    all_gather x4 -> x3, waiting for transfers between devices: 12.7 us -> 0.04 us  [on_device(): lax.all_gather(block, GATHER, axis=0, tiled=False)]
    all_to_all x4, blocking collectives: 49.1 us -> 56.3 us  [swap(): return lax.all_to_all(block, axes, 0, 0, tiled=True)]
  transfers between devices with their start and end apart: 12 -> 11, of which waited for: 8 -> 5; matrix products, arithmetic and copies ran while one was open for 7% -> 5% of each run, Pallas kernels for 29% -> 42%
where the time goes in v3:
time: 331 us; the launch traced here: 329 us
  Pallas kernels  139 us (42%)
  blocking collectives  56.3 us (17%)
  starting transfers between devices  54 us (16%)
  waiting for transfers between devices  42.3 us (13%)
  between operations  14 us (4%)
  local copies, waits for them, and re-layouts  9.84 us (3%)
  other arithmetic  6.84 us (2%)
  matrix products  5.98 us (2%)
    all_to_all x4, blocking collectives, swap(): return lax.all_to_all(block, axes, 0, 0, tiled=True)  56.3 us
    all_to_all x7, starting transfers between devices, swap(): return lax.all_to_all(block, axes, 0, 0, tiled=True)  46.5 us
    all_to_all x7, waiting for transfers between devices, swap(): return lax.all_to_all(block, axes, 0, 0, tiled=True)  30.6 us
    pallas_call x1, Pallas kernels, cross_backward(): pl.pallas_call(partial(cross_backward_kernel, scale=scale, step=2), out_s...  20.7 us
    pallas_call x1, Pallas kernels, mlp(): pl.pallas_call(mlp_kernel, grid=(steps,), out_shape=outs, in_specs=[whole...  17.1 us
    pallas_call x1, Pallas kernels, cross_forward(): pl.pallas_call(partial(cross_forward_kernel, scale=scale, step=2), out_sh...  16.9 us
    pallas_call x1, Pallas kernels, self_backward(): pl.pallas_call(partial(self_backward_kernel, scale=scale, step=2), out_sh...  13.8 us
    pallas_call x1, Pallas kernels, hidden_grads(): pl.pallas_call(hidden_grads_kernel, grid_spec=pltpu.PrefetchScalarGridSpe...  12.9 us
  transfers between devices with their start and end apart: 11, of which 5 were waited for; matrix products, arithmetic and copies ran while one was open for 5% of the time, Pallas kernels for 42%

profile of v3, /device:TPU:25, one launch (start us, length us, event | category | flops | bytes accessed | tf_op | source)
XLA Modules:
  0.0 328.7 jit_solution(12555583102163248738)
XLA Ops:
  7.9 1.2 dynamic_slice.22.camera_ref
  9.2 6.1 %enter.1 = (bf16[16,192,128]{2,1,0:T(8,128)(2,1)}, bf16[2,128,1024]{2,1,0:T(8,128)(2,1)}, f32[8,1024]{1,0:T(8,128)}) custom-call(s32[1]{0:T(128)} %dynamic_slice.22.camera_ref, bf16[128,1024]{1,0:T(8,128)(2,1)} %bitcast.36, bf16[128,1024]{1,0:T(8,128)(2,1)} %bitcast.39, f32[16,6144]{1,0:T(8,128)} %mod_ref.1, bf16[1024,1024]{1,0:T(8,128)(2,1)} %wq_any.3, ...), custom_call_target="tpu_custom_call" | custom-call | flops 805306368 | bytes 8388608 | tf_op jit(solution)/shard_map/enter/pallas_call | solution.py:613
  15.3 6.4 %all-to-all-start = ((bf16[16,192,128]{2,1,0:T(8,128)(2,1)}), bf16[16,192,128]{2,1,0:T(8,128)(2,1)S(1)}, u32[]{:S(2)}, u32[]{:S(2)}) async-start(bf16[16,192,128]{2,1,0:T(8,128)(2,1)} %get-tuple-element.67), calls=%async_computation | async-start | bytes 1572864 | tf_op jit(solution)/shard_map/all_to_all | solution.py:40
  21.9 0.7 convert_reduce_fusion
  22.6 1.2 constant_dynamic-slice_fusion
  24.5 1.1 constant_dynamic-slice_fusion.2
  25.7 0.8 add_reduce_fusion
  27.1 1.2 constant_dynamic-slice_fusion.3
  28.5 0.8 pad_maximum_fusion.1.wt_ref
  29.2 9.5 %all-to-all-done.qkv_ref = bf16[16,192,128]{2,1,0:T(8,128)(2,1)S(1)} async-done(((bf16[16,192,128]{2,1,0:T(8,128)(2,1)}), bf16[16,192,128]{2,1,0:T(8,128)(2,1)S(1)}, u32[]{:S(2)}, u32[]{:S(2)}) %all-to-all-start) | async-done | bytes 786464 | tf_op jit(solution)/shard_map/all_to_all | solution.py:40
  38.7 0.9 copy-done.8
  39.6 11.4 %self_forward.1 = (bf16[16,64,128]{2,1,0:T(8,128)(2,1)}, f32[16,72,128]{2,1,0:T(8,128)}) custom-call(bf16[16,192,128]{2,1,0:T(8,128)(2,1)} %copy-done.8), custom_call_target="tpu_custom_call" | custom-call | flops 4294967296 | bytes 4194304 | tf_op jit(solution)/shard_map/self_forward/pallas_call | solution.py:228
  50.9 14.4 %all_to_all.55.o_ref = bf16[16,64,128]{2,1,0:T(8,128)(2,1)} all-to-all(bf16[16,64,128]{2,1,0:T(8,128)(2,1)} %get-tuple-element.71), channel_id=1, replica_groups=mesh['yh'=2,'c'=2,'x'=4,'zh'=2,'zl'=2,'yl'=2] {'yh','c','zl','yl'}, dimensions={0} | all-to-all | bytes 524288 | tf_op jit(solution)/shard_map/all_to_all | solution.py:40
  65.4 4.7 %middle.1 = (f32[128,1024]{1,0:T(8,128)}, bf16[4,128,1024]{2,1,0:T(8,128)(2,1)}, bf16[16,64,128]{2,1,0:T(8,128)(2,1)}) custom-call(bf16[16,64,128]{2,1,0:T(8,128)(2,1)} %all_to_all.55.o_ref, bf16[128,1024]{1,0:T(8,128)(2,1)} %bitcast.37, f32[8,1024]{1,0:T(8,128)} %get-tuple-element.72.gains_ref, bf16[2,128,1024]{2,1,0:T(8,128)(2,1)} %get-tuple-element.73.early_ref, ...), custom_call_target="tpu_custom_call" | custom-call | flops 536870912 | bytes 6291456 | tf_op jit(solution)/shard_map/middle/pallas_call | solution.py:621
  70.1 6.0 %all-to-all-start.2 = ((bf16[16,64,128]{2,1,0:T(8,128)(2,1)}), bf16[16,64,128]{2,1,0:T(8,128)(2,1)S(1)}, u32[]{:S(2)}, u32[]{:S(2)}) async-start(bf16[16,64,128]{2,1,0:T(8,128)(2,1)} %get-tuple-element.74), calls=%async_computation.2 | async-start | bytes 524288 | tf_op jit(solution)/shard_map/all_to_all | solution.py:40
  76.2 6.0 %convolution_convert_fusion.kv_ref = bf16[128,4096]{1,0:T(8,128)(2,1)} fusion(bf16[768,128]{1,0:T(8,128)(2,1)S(1)} %pad_maximum_fusion.2, bf16[4096,768]{1,0:T(8,128)(2,1)} %bitcast.34), kind=kOutput, calls=%fused_computation | convolution fusion | flops 805830656 | bytes 7536640 | tf_op jit(solution)/shard_map/dot_general | solution.py:36
  82.2 0.7 copy-done.12
  82.9 16.9 %cross_forward.1 = (bf16[16,64,128]{2,1,0:T(8,128)(2,1)}, f32[16,72,128]{2,1,0:T(8,128)}) custom-call(s32[16]{0:T(128)} %select_reduce_fusion.order_ref, s32[1]{0:T(128)} %bitcast.5.live_ref, bf16[16,64,128]{2,1,0:T(8,128)(2,1)} %copy-done.12, bf16[128,4096]{1,0:T(8,128)(2,1)} %convolution_convert_fusion.kv_ref), custom_call_target="tpu_custom_call" | custom-call | flops 6979321856 | bytes 4194304 | tf_op jit(solution)/shard_map/cross_forward/pallas_call | solution.py:262
  99.8 13.4 %all_to_all.56.oc_ref = bf16[16,64,128]{2,1,0:T(8,128)(2,1)} all-to-all(bf16[16,64,128]{2,1,0:T(8,128)(2,1)} %get-tuple-element.76.oc_ref), channel_id=1, replica_groups=mesh['yh'=2,'c'=2,'x'=4,'zh'=2,'zl'=2,'yl'=2] {'yh','c','zl','yl'}, dimensions={0} | all-to-all | bytes 524288 | tf_op jit(solution)/shard_map/all_to_all | solution.py:40
  113.2 17.1 %mlp.1 = (f32[128,1024]{1,0:T(8,128)}, f32[128,1024]{1,0:T(8,128)}, bf16[2,128,1024]{2,1,0:T(8,128)(2,1)}, bf16[16,64,128]{2,1,0:T(8,128)(2,1)}, f32[8,1024]{1,0:T(8,128)}) custom-call(bf16[16,64,128]{2,1,0:T(8,128)(2,1)} %all_to_all.56.oc_ref, f32[128,1024]{1,0:T(8,128)} %get-tuple-element.77.first_ref, bf16[128,1024]{1,0:T(8,128)(2,1)} %bitcast.40, ...), custom_call_target="tpu_custom_call" | custom-call | flops 4831838208 | bytes 23068672 | tf_op jit(solution)/shard_map/mlp/pallas_call | solution.py:634
  130.4 15.3 %all_to_all.57.do_ref = bf16[16,64,128]{2,1,0:T(8,128)(2,1)} all-to-all(bf16[16,64,128]{2,1,0:T(8,128)(2,1)} %get-tuple-element.79), channel_id=1, replica_groups=mesh['yh'=2,'c'=2,'x'=4,'zh'=2,'zl'=2,'yl'=2] {'yh','c','zl','yl'}, dimensions={0} | all-to-all | bytes 524288 | tf_op jit(solution)/shard_map/all_to_all | solution.py:40
  145.7 20.7 %cross_backward.1 = (bf16[16,64,128]{2,1,0:T(8,128)(2,1)}, bf16[16,128,256]{2,1,0:T(8,128)(2,1)}) custom-call(s32[16]{0:T(128)} %select_reduce_fusion.order_ref, s32[1]{0:T(128)} %bitcast.5.live_ref, bf16[16,64,128]{2,1,0:T(8,128)(2,1)} %copy-done.12, bf16[16,64,128]{2,1,0:T(8,128)(2,1)} %all_to_all.57.do_ref, f32[16,72,128]{2,1,0:T(8,128)} %get-tuple-element.80.keep_ref, ...), custom_call_target="tpu_custom_call" | custom-call | flops 17448304640 | bytes 4194304 | tf_op jit(solution)/shard_map/cross_backward/pallas_call | solution.py:276
  166.4 13.1 %all_to_all.58.dq_ref = bf16[16,64,128]{2,1,0:T(8,128)(2,1)} all-to-all(bf16[16,64,128]{2,1,0:T(8,128)(2,1)} %get-tuple-element.81.dqc_ref), channel_id=1, replica_groups=mesh['yh'=2,'c'=2,'x'=4,'zh'=2,'zl'=2,'yl'=2] {'yh','c','zl','yl'}, dimensions={0} | all-to-all | bytes 524288 | tf_op jit(solution)/shard_map/all_to_all | solution.py:40
  179.6 5.9 %returned.1 = (f32[128,1024]{1,0:T(8,128)}, bf16[16,128,128]{2,1,0:T(8,128)(2,1)}, f32[8,1024]{1,0:T(8,128)}) custom-call(bf16[16,64,128]{2,1,0:T(8,128)(2,1)} %all_to_all.58.dq_ref, f32[128,1024]{1,0:T(8,128)} %get-tuple-element.77.first_ref, f32[128,1024]{1,0:T(8,128)} %get-tuple-element.82.second_back_ref, f32[8,1024]{1,0:T(8,128)} %get-tuple-element.72.gains_ref, ...), custom_call_target="tpu_custom_call" | custom-call | flops 536870912 | bytes 6291456 | tf_op jit(solution)/shard_map/returned/pallas_call | solution.py:654
  185.5 5.8 %all-to-all-start.6 = ((bf16[16,128,128]{2,1,0:T(8,128)(2,1)}), bf16[16,128,128]{2,1,0:T(8,128)(2,1)S(1)}, u32[]{:S(2)}, u32[]{:S(2)}) async-start(bf16[16,128,128]{2,1,0:T(8,128)(2,1)} %get-tuple-element.83), calls=%async_computation.6 | async-start | bytes 1048576 | tf_op jit(solution)/shard_map/all_to_all | solution.py:40
  191.3 7.0 %cross_grads.1 = bf16[8,96,256]{2,1,0:T(8,128)(2,1)} custom-call(bf16[16,64,128]{2,1,0:T(8,128)(2,1)} %get-tuple-element.81.dqc_ref, bf16[4,4,4,128,1024]{4,3,2,1,0:T(8,128)(2,1)} %bitcast.28, bf16[16,128,256]{2,1,0:T(8,128)(2,1)} %get-tuple-element.92.dkv_ref, bf16[4,4,256,768]{3,2,1,0:T(8,128)(2,1)} %bitcast.35), custom_call_target="tpu_custom_call" | custom-call | flops 1610612736 | bytes 12582912 | tf_op jit(solution)/shard_map/cross_grads/pallas_call | solution.py:691
  198.3 5.4 %all-to-all-done.6.do_ref = bf16[16,128,128]{2,1,0:T(8,128)(2,1)S(1)} async-done(((bf16[16,128,128]{2,1,0:T(8,128)(2,1)}), bf16[16,128,128]{2,1,0:T(8,128)(2,1)S(1)}, u32[]{:S(2)}, u32[]{:S(2)}) %all-to-all-start.6) | async-done | bytes 524320 | tf_op jit(solution)/shard_map/all_to_all | solution.py:40
  203.7 7.7 %all-to-all-start.7 = ((bf16[16,128,256]{2,1,0:T(8,128)(2,1)}), bf16[16,128,256]{2,1,0:T(8,128)(2,1)S(1)}, u32[]{:S(2)}, u32[]{:S(2)}) async-start(bf16[16,128,256]{2,1,0:T(8,128)(2,1)} %get-tuple-element.92.dkv_ref), calls=%async_computation.7 | async-start | bytes 2097152 | tf_op jit(solution)/shard_map/all_to_all | solution.py:40
  211.5 13.8 %self_backward.1.dqkv_ref = bf16[16,192,128]{2,1,0:T(8,128)(2,1)} custom-call(bf16[16,192,128]{2,1,0:T(8,128)(2,1)} %copy-done.8, bf16[16,128,128]{2,1,0:T(8,128)(2,1)} %copy-done.6, f32[16,72,128]{2,1,0:T(8,128)} %get-tuple-element.87.keep_ref), custom_call_target="tpu_custom_call" | custom-call | flops 10737418240 | bytes 4194304 | tf_op jit(solution)/shard_map/self_backward/pallas_call | solution.py:242
  225.2 5.9 %late_grads.1 = (bf16[8,96,256]{2,1,0:T(8,128)(2,1)}, bf16[16,224,128]{2,1,0:T(8,128)(2,1)}) custom-call(bf16[16,192,128]{2,1,0:T(8,128)(2,1)} %self_backward.1.dqkv_ref, bf16[4,4,4,128,1024]{4,3,2,1,0:T(8,128)(2,1)} %bitcast.29, bf16[192,1024]{1,0:T(8,128)(2,1)} %pad_maximum_fusion.1.wt_ref, f32[8,1024]{1,0:T(8,128)} %get-tuple-element.72.gains_ref, ...), custom_call_target="tpu_custom_call" | custom-call | flops 1073741824 | bytes 6291456 | tf_op jit(solution)/shard_map/late_grads/pallas_call | solution.py:736
  231.2 3.4 %all-to-all-done.7.got_ref = bf16[16,128,256]{2,1,0:T(8,128)(2,1)S(1)} async-done(((bf16[16,128,256]{2,1,0:T(8,128)(2,1)}), bf16[16,128,256]{2,1,0:T(8,128)(2,1)S(1)}, u32[]{:S(2)}, u32[]{:S(2)}) %all-to-all-start.7) | async-done | bytes 1048608 | tf_op jit(solution)/shard_map/all_to_all | solution.py:40
  234.5 8.3 %all-to-all-start.8 = ((bf16[16,224,128]{2,1,0:T(8,128)(2,1)}), bf16[16,224,128]{2,1,0:T(8,128)(2,1)S(1)}, u32[]{:S(2)}, u32[]{:S(2)}) async-start(bf16[16,224,128]{2,1,0:T(8,128)(2,1)} %get-tuple-element.93), calls=%async_computation.8 | async-start | bytes 1835008 | tf_op jit(solution)/shard_map/all_to_all | solution.py:40
  242.9 12.9 %hidden_grads.1 = (bf16[8,160,256]{2,1,0:T(8,128)(2,1)}, bf16[32,32,384]{2,1,0:T(8,128)(2,1)}) custom-call(s32[1]{0:T(128)} %bitcast.10.head_ref, bf16[4,4,4,128,1024]{4,3,2,1,0:T(8,128)(2,1)} %bitcast.30, bf16[4,4,4,128,1024]{4,3,2,1,0:T(8,128)(2,1)} %bitcast.31, bf16[4,4,2,128,1024]{4,3,2,1,0:T(8,128)(2,1)} %bitcast.32, ...), custom_call_target="tpu_custom_call" | custom-call | flops 5368709120 | bytes 20971520 | tf_op jit(solution)/shard_map/hidden_grads/pallas_call | solution.py:715
  255.8 2.6 pad_maximum_fusion
  258.4 7.3 %all-to-all-start.9 = ((bf16[8,352,256]{2,1,0:T(8,128)(2,1)}), bf16[8,352,256]{2,1,0:T(8,128)(2,1)S(1)}, u32[]{:S(2)}, u32[]{:S(2)}) async-start(bf16[8,352,256]{2,1,0:T(8,128)(2,1)} %pad_maximum_fusion), calls=%async_computation.9 | async-start | bytes 2883584 | tf_op jit(solution)/shard_map/all_to_all | solution.py:40
  265.9 6.9 %leave.1 = (f32[128,1024]{1,0:T(8,128)}, f32[16,128]{1,0:T(8,128)}) custom-call(bf16[16,224,128]{2,1,0:T(8,128)(2,1)} %copy-done.4, bf16[128,1024]{1,0:T(8,128)(2,1)} %bitcast.38, f32[128,1024]{1,0:T(8,128)} %get-tuple-element.99.back_ref, f32[8,1024]{1,0:T(8,128)} %get-tuple-element.72.gains_ref, bf16[1024,1024]{1,0:T(8,128)(2,1)} %wq_any.3, ...), custom_call_target="tpu_custom_call" | custom-call | flops 805306368 | bytes 8388608 | tf_op jit(solution)/shard_map/leave/pallas_call | solution.py:661
  272.8 0.7 reshape.181
  273.8 1.0 pad_add_fusion
  274.8 12.3 %all-to-all-done.9.got_ref = bf16[8,352,256]{2,1,0:T(8,128)(2,1)S(1)} async-done(((bf16[8,352,256]{2,1,0:T(8,128)(2,1)}), bf16[8,352,256]{2,1,0:T(8,128)(2,1)S(1)}, u32[]{:S(2)}, u32[]{:S(2)}) %all-to-all-start.9) | async-done | bytes 1441824 | tf_op jit(solution)/shard_map/all_to_all | solution.py:40
  287.1 5.0 %all-to-all-start.10 = ((bf16[32,32,384]{2,1,0:T(8,128)(2,1)}), bf16[32,32,384]{2,1,0:T(8,128)(2,1)S(1)}, u32[]{:S(2)}, u32[]{:S(2)}) async-start(bf16[32,32,384]{2,1,0:T(8,128)(2,1)} %pad_add_fusion), calls=%async_computation.10 | async-start | bytes 1572864 | tf_op jit(solution)/shard_map/all_to_all | solution.py:40
  292.1 2.3 add_items.1
  294.4 7.4 %collective-permute-start = (f32[352,256]{1,0:T(8,128)}, f32[352,256]{1,0:T(8,128)S(1)}, u32[]{:S(2)}, u32[]{:S(2)}) collective-permute-start(f32[352,256]{1,0:T(8,128)} %add_items.1), channel_id=1, source_target_pairs={{0,0},{1,2},{2,4},{3,6},{4,32},{5,34},{6,36},{7,38},{8,64},{9,66},... | collective-permute-start | bytes 1081352 | tf_op jit(solution)/shard_map/ppermute | solution.py:844
  301.8 4.1 %patches_back.1 = f32[256,768]{1,0:T(8,128)} custom-call(bf16[16,128,256]{2,1,0:T(8,128)(2,1)} %copy-done.3, bf16[768,1024]{1,0:T(8,128)(2,1)} %wk_ref.1, bf16[768,1024]{1,0:T(8,128)(2,1)} %wv_ref.1), custom_call_target="tpu_custom_call" | custom-call | flops 805306368 | bytes 5242880 | tf_op jit(solution)/shard_map/patches_back/pallas_call | solution.py:668
  305.9 10.9 %collective-permute-done.in_ref = f32[352,256]{1,0:T(8,128)S(1)} collective-permute-done((f32[352,256]{1,0:T(8,128)}, f32[352,256]{1,0:T(8,128)S(1)}, u32[]{:S(2)}, u32[]{:S(2)}) %collective-permute-start) | collective-permute-done | bytes 360480 | tf_op jit(solution)/shard_map/ppermute | solution.py:844
  316.8 0.7 copy-done.11
  317.6 1.7 finish_columns.1
  319.3 0.9 copy-done.5
  320.2 1.9 finish_rows.1
  (56 shorter events, 3.0 us)
Async XLA Ops:
  7.2 14.5 %copy-start = (s32[8,4]{0,1:T(4,128)S(1)}, s32[8,4]{0,1:T(4,128)}, u32[]{:S(2)}) copy-start(s32[8,4]{0,1:T(4,128)} %param.18) | copy-start | bytes 388
  7.2 69.0 %all-gather.7.cloned.1.call-start = ((), (), s32[]{:S(2)}) async-start(), calls=%async_computation.11 | async-start | bytes 6684672 | tf_op jit(solution)/shard_map/all_gather | solution.py:787
  15.3 23.4 %all-to-all-start = ((bf16[16,192,128]{2,1,0:T(8,128)(2,1)}), bf16[16,192,128]{2,1,0:T(8,128)(2,1)S(1)}, u32[]{:S(2)}, u32[]{:S(2)}) async-start(bf16[16,192,128]{2,1,0:T(8,128)(2,1)} %get-tuple-element.67), calls=%async_computation | async-start | bytes 1572864 | tf_op jit(solution)/shard_map/all_to_all | solution.py:40
  21.7 169.6 %all-gather.9.cloned.1.call-start = ((), (), s32[]{:S(2)}) async-start(), calls=%async_computation.12 | async-start | bytes 17825792 | tf_op jit(solution)/shard_map/all_gather | solution.py:787
  38.7 0.9 copy-start.8
  70.1 12.0 %all-to-all-start.2 = ((bf16[16,64,128]{2,1,0:T(8,128)(2,1)}), bf16[16,64,128]{2,1,0:T(8,128)(2,1)S(1)}, u32[]{:S(2)}, u32[]{:S(2)}) async-start(bf16[16,64,128]{2,1,0:T(8,128)(2,1)} %get-tuple-element.74), calls=%async_computation.2 | async-start | bytes 524288 | tf_op jit(solution)/shard_map/all_to_all | solution.py:40
  76.1 166.7 %all-gather.11.cloned.1.call-start = ((), (), s32[]{:S(2)}) async-start(), calls=%async_computation.13 | async-start | bytes 8912896 | tf_op jit(solution)/shard_map/all_gather | solution.py:787
  82.2 0.7 copy-start.12
  185.5 18.2 %all-to-all-start.6 = ((bf16[16,128,128]{2,1,0:T(8,128)(2,1)}), bf16[16,128,128]{2,1,0:T(8,128)(2,1)S(1)}, u32[]{:S(2)}, u32[]{:S(2)}) async-start(bf16[16,128,128]{2,1,0:T(8,128)(2,1)} %get-tuple-element.83), calls=%async_computation.6 | async-start | bytes 1048576 | tf_op jit(solution)/shard_map/all_to_all | solution.py:40
  203.7 7.7 %copy-start.6 = (bf16[16,128,128]{2,1,0:T(8,128)(2,1)}, bf16[16,128,128]{2,1,0:T(8,128)(2,1)S(1)}, u32[]{:S(2)}) copy-start(bf16[16,128,128]{2,1,0:T(8,128)(2,1)S(1)} %all-to-all-done.6.do_ref) | copy-start | bytes 1572868
  203.7 30.8 %all-to-all-start.7 = ((bf16[16,128,256]{2,1,0:T(8,128)(2,1)}), bf16[16,128,256]{2,1,0:T(8,128)(2,1)S(1)}, u32[]{:S(2)}, u32[]{:S(2)}) async-start(bf16[16,128,256]{2,1,0:T(8,128)(2,1)} %get-tuple-element.92.dkv_ref), calls=%async_computation.7 | async-start | bytes 2097152 | tf_op jit(solution)/shard_map/all_to_all | solution.py:40
  234.5 21.2 %copy-start.3 = (bf16[16,128,256]{2,1,0:T(8,128)(2,1)}, bf16[16,128,256]{2,1,0:T(8,128)(2,1)S(1)}, u32[]{:S(2)}) copy-start(bf16[16,128,256]{2,1,0:T(8,128)(2,1)S(1)} %all-to-all-done.7.got_ref) | copy-start | bytes 3145732
  234.5 21.2 %all-to-all-start.8 = ((bf16[16,224,128]{2,1,0:T(8,128)(2,1)}), bf16[16,224,128]{2,1,0:T(8,128)(2,1)S(1)}, u32[]{:S(2)}, u32[]{:S(2)}) async-start(bf16[16,224,128]{2,1,0:T(8,128)(2,1)} %get-tuple-element.93), calls=%async_computation.8 | async-start | bytes 1835008 | tf_op jit(solution)/shard_map/all_to_all | solution.py:40
  242.9 12.9 %copy-start.7 = (bf16[8,96,256]{2,1,0:T(8,128)(2,1)S(1)}, bf16[8,96,256]{2,1,0:T(8,128)(2,1)}, u32[]{:S(2)}) copy-start(bf16[8,96,256]{2,1,0:T(8,128)(2,1)} %cross_grads.1) | copy-start | bytes 1179652
  242.9 12.9 %copy-start.10 = (bf16[8,96,256]{2,1,0:T(8,128)(2,1)S(1)}, bf16[8,96,256]{2,1,0:T(8,128)(2,1)}, u32[]{:S(2)}) copy-start(bf16[8,96,256]{2,1,0:T(8,128)(2,1)} %get-tuple-element.102) | copy-start | bytes 1179652
  255.8 2.7 copy-start.4
  258.4 28.6 %all-to-all-start.9 = ((bf16[8,352,256]{2,1,0:T(8,128)(2,1)}), bf16[8,352,256]{2,1,0:T(8,128)(2,1)S(1)}, u32[]{:S(2)}, u32[]{:S(2)}) async-start(bf16[8,352,256]{2,1,0:T(8,128)(2,1)} %pad_maximum_fusion), calls=%async_computation.9 | async-start | bytes 2883584 | tf_op jit(solution)/shard_map/all_to_all | solution.py:40
  265.9 7.9 %copy-start.9 = (bf16[32,32,384]{2,1,0:T(8,128)(2,1)S(1)}, bf16[32,32,384]{2,1,0:T(8,128)(2,1)}, u32[]{:S(2)}) copy-start(bf16[32,32,384]{2,1,0:T(8,128)(2,1)} %get-tuple-element.105) | copy-start | bytes 2359300
  287.1 5.0 %copy-start.2 = (bf16[8,352,256]{2,1,0:T(8,128)(2,1)}, bf16[8,352,256]{2,1,0:T(8,128)(2,1)S(1)}, u32[]{:S(2)}) copy-start(bf16[8,352,256]{2,1,0:T(8,128)(2,1)S(1)} %all-to-all-done.9.got_ref) | copy-start | bytes 4325380
  287.1 32.2 %all-to-all-start.10 = ((bf16[32,32,384]{2,1,0:T(8,128)(2,1)}), bf16[32,32,384]{2,1,0:T(8,128)(2,1)S(1)}, u32[]{:S(2)}, u32[]{:S(2)}) async-start(bf16[32,32,384]{2,1,0:T(8,128)(2,1)} %pad_add_fusion), calls=%async_computation.10 | async-start | bytes 1572864 | tf_op jit(solution)/shard_map/all_to_all | solution.py:40
  294.4 22.5 %collective-permute-start = (f32[352,256]{1,0:T(8,128)}, f32[352,256]{1,0:T(8,128)S(1)}, u32[]{:S(2)}, u32[]{:S(2)}) collective-permute-start(f32[352,256]{1,0:T(8,128)} %add_items.1), channel_id=1, source_target_pairs={{0,0},{1,2},{2,4},{3,6},{4,32},{5,34},{6,36},{7,38},{8,64},{9,66},... | collective-permute-start | bytes 1081352 | tf_op jit(solution)/shard_map/ppermute | solution.py:844
  301.8 20.4 %copy-start.1 = (s32[8,4]{0,1:T(4,128)S(1)}, s32[8,4]{0,1:T(4,128)}, u32[]{:S(2)}) copy-start(s32[8,4]{0,1:T(4,128)} %param.18) | copy-start | bytes 388
  316.8 0.7 copy-start.11
  319.3 0.9 copy-start.5
Sparse Core Ops, SparseCore 0:
  9.7 53.1 all-gather.6
  70.3 99.7 all-gather.8
  171.8 69.8 all-gather.10
